TPU v7x, 128 devices: a whole 4x4x4 slice. The times are simulated.
128 devices in a mesh: layer: 2 (over x_lo), row: 2 (over x_hi), col: 32 (over z, y, core).
Axes of the slice: x: 4 (x_hi: 2, x_lo: 2; x = x_hi * 2 + x_lo), y: 4, z: 4, core: 2. Of those that a mesh axis runs over, the one named last changes fastest.
Arguments:
- values: bfloat16 [8192, 8192], P('row', ('layer', 'col'))
- pattern: int32 [64, 64], replicated, may hold values from 0 to 1, as said below
- keep_square: int32 [64, 64], replicated, may hold values from 0 to 1, as said below
- keep_next: int32 [64, 64], replicated, may hold values from 0 to 1, as said below
Outputs:
- square: bfloat16 [8192, 8192], P('row', ('layer', 'col'))
- next_sign: bfloat16 [8192, 8192], P('row', ('layer', 'col'))
Inputs may be any that keep to these rules, and one draw needn't show every extreme that they name: `pattern`: 0 or 1; every diagonal block is 1; the number of 1 block differs from block row to block row. `keep_square`: 0 or 1; every diagonal block is 1. `keep_next`: 0 or 1; every diagonal block is 1.
All inputs are finite; a program needn't handle non-finite values.
Results may differ from a plain program's by a relative error of at most 0.0018.
Values may be sent and summed in bfloat16 or wider, within the bound.
No kernel may reach another device: no remote copies, remote signals or barrier semaphores. Data moves between devices by JAX's collectives and lax.ppermute only.
A program may use at most 128 MiB of HBM per device.

v0:
```python
import jax
import jax.numpy as jnp
from jax import lax
from jax.sharding import PartitionSpec as P

TILE = 128


def spread(value, axis, root):
    mine = lax.axis_index(axis) == root
    return lax.psum(jnp.where(mine, value, jnp.zeros_like(value)), axis)


def tile_mask(matrix, mask_tiles):
    row_tiles, col_tiles = mask_tiles.shape
    shaped = matrix.reshape(row_tiles, TILE, col_tiles, TILE)
    return (shaped * mask_tiles[:, None, :, None].astype(matrix.dtype)).reshape(matrix.shape)


def local(values, pattern, keep_square, keep_next):
    col_count = lax.axis_size("col")
    layer_index = lax.axis_index("layer")
    row_index = lax.axis_index("row")
    col_index = lax.axis_index("col")
    row_count, piece_width = values.shape
    row_tiles = row_count // TILE
    col_tiles = piece_width // TILE
    first_row = row_index * row_tiles
    first_col = (layer_index * col_count + col_index) * col_tiles

    def local_mask(mask_whole):
        return lax.dynamic_slice(mask_whole, (first_row, first_col), (row_tiles, col_tiles))

    start_matrix = tile_mask(values, local_mask(pattern))
    left_whole = lax.all_gather(start_matrix, "col", axis=1, tiled=True)

    def column_block(matrix):
        gathered = lax.all_gather(matrix, "layer", axis=1, tiled=True)
        return spread(gathered, "row", layer_index)

    def multiply(right_block):
        layer_part = jnp.dot(left_whole, right_block, preferred_element_type=jnp.float32)
        summed = lax.psum(layer_part, "layer")
        return lax.dynamic_slice_in_dim(summed, layer_index * piece_width, piece_width, 1)

    square_raw = multiply(column_block(start_matrix))
    square = tile_mask(square_raw, local_mask(keep_square)).astype(jnp.bfloat16)
    product = multiply(column_block(square))
    update = 1.5 * start_matrix.astype(jnp.float32) - 0.5 * product
    next_sign = tile_mask(update, local_mask(keep_next)).astype(jnp.bfloat16)
    return (square, next_sign)


def solution(mesh):
    return jax.shard_map(
        local,
        mesh=mesh,
        in_specs=(P("row", ("layer", "col")), P(), P(), P()),
        out_specs=(P("row", ("layer", "col")), P("row", ("layer", "col"))),
        check_vma=False,
    )
```

profile of v0, /device:TPU:0, one launch (start us, length us, event | category | flops | bytes accessed | tf_op | source)
XLA Modules:
  0.0 572.3 jit_solution(11293284728123939716)
XLA Ops:
  8.0 0.0 all-gather.6.cloned.1.call-start
  8.1 0.9 fusion
  9.0 0.1 broadcast_bitcast_fusion.2
  9.0 2.5 broadcast_multiply_fusion
  11.6 0.0 all-reduce.5.cloned.1.call-start
  11.6 38.2 %all-gather.6.cloned.1.call-done = bf16[4096,256]{1,0:T(8,128)(2,1)} async-done(((bf16[4096,128]{1,0:T(8,128)(2,1)}), bf16[4096,256]{1,0:T(8,128)(2,1)}) %all-gather.6.cloned.1.call-update) | async-done | bytes 2097168 | tf_op jit(solution)/shard_map/all_gather | solution.py:38
  49.8 3.0 broadcast_select_fusion.1
  52.9 0.0 all-reduce.5.cloned.1.call-update
  52.9 0.0 all-gather.4.cloned.1.call-start
  52.9 0.5 all-gather.4.cloned.1.call-update
  53.5 0.0 all-reduce.7.cloned.1.call-start
  53.5 70.9 %all-reduce.5.cloned.1.call-done = bf16[4096,256]{1,0:T(8,128)(2,1)} async-done(((bf16[4096,256]{1,0:T(8,128)(2,1)}), bf16[4096,256]{1,0:T(8,128)(2,1)}) %all-reduce.5.cloned.1.call-update) | async-done | bytes 2097168 | tf_op jit(solution)/shard_map/psum | solution.py:11
  124.4 57.5 %all-gather.4.cloned.1.call-done = bf16[4096,4096]{1,0:T(8,128)(2,1)} async-done(((bf16[4096,128]{1,0:T(8,128)(2,1)}), bf16[4096,4096]{1,0:T(8,128)(2,1)}) %all-gather.4.cloned.1.call-update) | async-done | bytes 33554448 | tf_op jit(solution)/shard_map/all_gather | solution.py:35
  181.9 17.2 %fusion.1 = f32[4096,256]{1,0:T(8,128)} fusion(bf16[4096,4096]{1,0:T(8,128)(2,1)} %all-gather.4.cloned.1.call-done, bf16[4096,256]{1,0:T(8,128)(2,1)} %all-reduce.5.cloned.1.call-done), kind=kOutput, calls=%fused_computation.12 | convolution fusion | flops 8589934592 | bytes 39845888 | tf_op jit(solution)/shard_map/dot_general | solution.py:42
  199.1 0.0 all-reduce.7.cloned.1.call-update
  199.2 0.0 all-gather.8.cloned.1.call-start
  199.2 0.7 copy-done.1
  199.9 0.2 convert_reduce_fusion.1
  200.1 0.1 broadcast_bitcast_fusion.1
  200.1 114.6 %all-reduce.7.cloned.1.call-done = f32[4096,256]{1,0:T(8,128)} async-done(((f32[4096,256]{1,0:T(8,128)}), f32[4096,256]{1,0:T(8,128)}) %all-reduce.7.cloned.1.call-update) | async-done | bytes 4194320 | tf_op jit(solution)/shard_map/psum | solution.py:43
  314.7 2.7 multiply_convert_fusion.1
  317.5 0.0 all-reduce.9.cloned.1.call-start
  317.5 36.7 %all-gather.8.cloned.1.call-done = bf16[4096,256]{1,0:T(8,128)(2,1)} async-done(((bf16[4096,128]{1,0:T(8,128)(2,1)}), bf16[4096,256]{1,0:T(8,128)(2,1)}) %all-gather.8.cloned.1.call-update) | async-done | bytes 2097168 | tf_op jit(solution)/shard_map/all_gather | solution.py:38
  354.2 3.0 broadcast_select_fusion
  357.3 0.0 all-reduce.11.cloned.1.call-start
  357.3 71.4 %all-reduce.9.cloned.1.call-done = bf16[4096,256]{1,0:T(8,128)(2,1)} async-done(((bf16[4096,256]{1,0:T(8,128)(2,1)}), bf16[4096,256]{1,0:T(8,128)(2,1)}) %all-reduce.9.cloned.1.call-update) | async-done | bytes 2097168 | tf_op jit(solution)/shard_map/psum | solution.py:11
  428.8 17.2 %fusion.2 = f32[4096,256]{1,0:T(8,128)} fusion(bf16[4096,4096]{1,0:T(8,128)(2,1)} %all-gather.4.cloned.1.call-done, bf16[4096,256]{1,0:T(8,128)(2,1)} %all-reduce.9.cloned.1.call-done), kind=kOutput, calls=%fused_computation.13 | convolution fusion | flops 8589934592 | bytes 39845888 | tf_op jit(solution)/shard_map/dot_general | solution.py:42
  446.0 0.7 copy-done.2
  446.7 0.2 convert_reduce_fusion
  446.9 0.1 broadcast_bitcast_fusion
  447.0 113.1 %all-reduce.11.cloned.1.call-done = f32[4096,256]{1,0:T(8,128)} async-done(((f32[4096,256]{1,0:T(8,128)}), f32[4096,256]{1,0:T(8,128)}) %all-reduce.11.cloned.1.call-update) | async-done | bytes 4194320 | tf_op jit(solution)/shard_map/psum | solution.py:43
  560.1 4.8 multiply_convert_fusion
  (8 shorter events, 0.1 us)
Async XLA Ops:
  8.0 41.8 %all-gather.6.cloned.1.call-start = ((), (), s32[]{:S(2)}) async-start(), calls=%async_computation.1 | async-start | bytes 3145728 | tf_op jit(solution)/shard_map/all_gather | solution.py:38
  11.6 112.8 %all-reduce.5.cloned.1.call-start = ((), (), s32[]{:S(2)}) async-start(), calls=%async_computation.2 | async-start | bytes 4194304 | tf_op jit(solution)/shard_map/psum | solution.py:11
  52.9 129.0 %all-gather.4.cloned.1.call-start = ((), (), s32[]{:S(2)}) async-start(), calls=%async_computation | async-start | bytes 34603008 | tf_op jit(solution)/shard_map/all_gather | solution.py:35
  53.5 261.3 %all-reduce.7.cloned.1.call-start = ((), (), s32[]{:S(2)}) async-start(), calls=%async_computation.3 | async-start | bytes 8388608 | tf_op jit(solution)/shard_map/psum | solution.py:43
  199.1 0.8 copy-start.1
  199.2 155.0 %all-gather.8.cloned.1.call-start = ((), (), s32[]{:S(2)}) async-start(), calls=%async_computation.4 | async-start | bytes 3145728 | tf_op jit(solution)/shard_map/all_gather | solution.py:38
  317.5 111.3 %all-reduce.9.cloned.1.call-start = ((), (), s32[]{:S(2)}) async-start(), calls=%async_computation.5 | async-start | bytes 4194304 | tf_op jit(solution)/shard_map/psum | solution.py:11
  357.3 202.8 %all-reduce.11.cloned.1.call-start = ((), (), s32[]{:S(2)}) async-start(), calls=%async_computation.6 | async-start | bytes 8388608 | tf_op jit(solution)/shard_map/psum | solution.py:43
  446.0 0.8 copy-start.2
  446.0 114.1 %copy-start = (bf16[4096,128]{1,0:T(8,128)(2,1)S(1)}, bf16[4096,128]{1,0:T(8,128)(2,1)}, u32[]{:S(2)}) copy-start(bf16[4096,128]{1,0:T(8,128)(2,1)} %param.4) | copy-start | bytes 3145732
Sparse Core Ops, SparseCore 0:
  11.7 38.0 all-gather.5
  53.0 71.3 all-reduce.4
  199.3 115.4 all-reduce.6
  317.6 36.5 all-gather.7
  357.4 71.3 all-reduce.8
  446.1 113.9 all-reduce.10
Sparse Core Ops, SparseCore 1:
  56.3 125.5 all-gather.3
where the time goes:
time: 574 us; the launch traced here: 572 us
  waiting for transfers between devices  503 us (88%)
  matrix products  34.4 us (6%)
  other arithmetic  17.4 us (3%)
  between operations  15.6 us (3%)
    psum x2, waiting for transfers between devices, multiply(): summed = lax.psum(layer_part, 'layer')  228 us
    psum x2, waiting for transfers between devices, spread(): return lax.psum(jnp.where(mine, value, jnp.zeros_like(value)), axis)  142 us
    all_gather x2, waiting for transfers between devices, column_block(): gathered = lax.all_gather(matrix, 'layer', axis=1, tiled=True)  74.8 us
    all_gather x1, waiting for transfers between devices, local(): left_whole = lax.all_gather(start_matrix, 'col', axis=1, tiled=True)  57.5 us
    dot_general x2, matrix products, multiply(): jnp.dot(left_whole, right_block, preferred_element_type=jnp.float32)  34.4 us
  transfers between devices with their start and end apart: 7, of which 7 were waited for; matrix products, arithmetic and copies ran while one was open for 0% of the time, Pallas kernels for 0%

commit v1 on v0

--- a/solution.py
+++ b/solution.py
@@ -1,9 +1,20 @@
+import functools
+
 import jax
 import jax.numpy as jnp
 from jax import lax
+from jax.experimental import pallas as pl
+from jax.experimental.pallas import tpu as pltpu
 from jax.sharding import PartitionSpec as P
 
 TILE = 128
+SHIFT = 10
+MASK = (1 << SHIFT) - 1
+BF16 = jnp.bfloat16
+F32 = jnp.float32
+HALF, SENT = 18, 11
+TIERS = ((12, 34, 16), (16, 46, 20))
+VMEM_LIMIT = 60 * 1024 * 1024
 
 
 def spread(value, axis, root):
@@ -17,7 +28,7 @@
     return (shaped * mask_tiles[:, None, :, None].astype(matrix.dtype)).reshape(matrix.shape)
 
 
-def local(values, pattern, keep_square, keep_next):
+def dense(values, pattern, keep_square, keep_next):
     col_count = lax.axis_size("col")
     layer_index = lax.axis_index("layer")
     row_index = lax.axis_index("row")
@@ -51,6 +62,407 @@
     return (square, next_sign)
 
 
+def shift_x(value, by):
+    def flat(x):
+        return x % 2 * 2 + x // 2
+
+    return lax.ppermute(value, ("layer", "row"), [(flat(x), flat((x + by) % 4)) for x in range(4)])
+
+
+def shift_ring(value, by, stage):
+    def target(c):
+        z, y, core = c // 8, c // 2 % 4, c % 2
+        if core == stage:
+            y = (y + by) % 4
+        else:
+            z = (z + by) % 4
+        return z * 8 + y * 2 + core
+
+    return lax.ppermute(value, "col", [(c, target(c)) for c in range(32)])
+
+
+def swap_core(value):
+    return lax.ppermute(value, "col", [(c, c ^ 1) for c in range(32)])
+
+
+def swap_layer(value):
+    return lax.ppermute(value, "layer", [(0, 1), (1, 0)])
+
+
+def after(value, *others):
+    return lax.optimization_barrier((value, *others))[0]
+
+
+def blocks_of(count):
+    return jax.ShapeDtypeStruct((count * TILE, TILE), BF16)
+
+
+def at_block(index):
+    return pl.ds(pl.multiple_of(index * TILE, TILE), TILE)
+
+
+ANY = pl.BlockSpec(memory_space=pl.ANY)
+VMEM = pl.BlockSpec(memory_space=pltpu.VMEM)
+
+
+def fetch(sources, offsets, scratch, sems):
+    copies = [
+        pltpu.make_async_copy(src, scratch.at[pl.ds(off * TILE, src.shape[0])], sems.at[n])
+        for n, (src, off) in enumerate(zip(sources, offsets, strict=True))
+    ]
+    for copy in copies:
+        copy.start()
+    return copies
+
+
+def offsets_of(arrays):
+    offsets, total = [], 0
+    for a in arrays:
+        offsets.append(total)
+        total += a.shape[0] // TILE
+    return offsets, total
+
+
+def pack_column(pattern, values):
+    def kernel(pattern_ref, values_ref, own_ref, sent_ref):
+        layer = lax.axis_index("layer")
+        first = lax.axis_index("row") * 32
+        column = layer * 32 + lax.axis_index("col")
+
+        def step(a, counts):
+            n, m = counts
+            for s in range(2):
+                t = 2 * a + s
+                keep = pattern_ref[first + t, column]
+
+                @pl.when((keep != 0) & (n < HALF))
+                def _(n=n, t=t):
+                    own_ref[at_block(n), :] = values_ref[at_block(t), :]
+
+                @pl.when((keep != 0) & (m < SENT) & (layer != s))
+                def _(m=m, t=t):
+                    sent_ref[at_block(m), :] = values_ref[at_block(t), :]
+
+                n = n + keep
+                m = m + jnp.where(layer != s, keep, 0)
+            return n, m
+
+        lax.fori_loop(0, 16, step, (0, 0))
+
+    return pl.pallas_call(
+        kernel,
+        grid_spec=pltpu.PrefetchScalarGridSpec(
+            num_scalar_prefetch=1, grid=(), in_specs=[VMEM], out_specs=[VMEM, VMEM]),
+        out_shape=[blocks_of(HALF), blocks_of(SENT)],
+        compiler_params=pltpu.CompilerParams(vmem_limit_bytes=VMEM_LIMIT),
+        name="pack_column",
+    )(pattern, values)
+
+
+def repack(index, sources, caps, name):
+    offsets, total = offsets_of(sources)
+    count = len(sources)
+
+    def kernel(index_ref, *refs):
+        srcs, outs = refs[:count], refs[count : count + len(caps)]
+        scratch, sems = refs[count + len(caps) :]
+        for copy in fetch(srcs, offsets, scratch, sems):
+            copy.wait()
+        base = 0
+        for out, cap in zip(outs, caps, strict=True):
+            for p in range(cap):
+                out[pl.ds(p * TILE, TILE), :] = scratch[at_block(index_ref[base + p]), :]
+            base += cap
+
+    return pl.pallas_call(
+        kernel,
+        grid_spec=pltpu.PrefetchScalarGridSpec(
+            num_scalar_prefetch=1, grid=(), in_specs=[ANY] * count, out_specs=[VMEM] * len(caps),
+            scratch_shapes=[pltpu.VMEM((total * TILE, TILE), BF16), pltpu.SemaphoreType.DMA((count,))]),
+        out_shape=[blocks_of(cap) for cap in caps],
+        compiler_params=pltpu.CompilerParams(vmem_limit_bytes=VMEM_LIMIT),
+        name=name,
+    )(index, *sources)
+
+
+def sum_of_products(row, list_ref, count, left, right):
+    def step(i, total):
+        for u in range(4):
+            code = list_ref[row, i * 4 + u]
+            a = left[at_block(code >> SHIFT), :]
+            b = right[at_block(code & MASK), :]
+            total += jnp.dot(a, b, preferred_element_type=F32)
+        return total
+
+    return lax.fori_loop(0, (count + 3) >> 2, step, jnp.zeros((TILE, TILE), F32))
+
+
+def load_operands(left_srcs, right_srcs, left_offs, right_offs, left, right, sems):
+    n = len(left_srcs)
+    copies = fetch(left_srcs, left_offs, left, sems)
+    copies += fetch(right_srcs, right_offs, right, sems.at[pl.ds(n, len(right_srcs))])
+    zero = jnp.zeros((TILE, TILE), BF16)
+    left[pl.ds(left.shape[0] - TILE, TILE), :] = zero
+    right[pl.ds(right.shape[0] - TILE, TILE), :] = zero
+    for copy in copies:
+        copy.wait()
+
+
+def square_blocks(lists, meta, lefts, rights, cap):
+    left_offs, left_total = offsets_of(lefts)
+    right_offs, right_total = offsets_of(rights)
+    nl, nr = len(lefts), len(rights)
+
+    def kernel(list_ref, meta_ref, *refs):
+        out, left, right, sems = refs[nl + nr :]
+        load_operands(refs[:nl], refs[nl : nl + nr], left_offs, right_offs, left, right, sems)
+
+        def step(o, carry):
+            @pl.when(meta_ref[1, o] != 0)
+            def _():
+                total = sum_of_products(o, list_ref, meta_ref[0, o], left, right)
+                out[at_block(jnp.minimum(meta_ref[2, o], cap - 1)), :] = total.astype(BF16)
+
+            return carry
+
+        lax.fori_loop(0, 32, step, 0)
+
+    return pl.pallas_call(
+        kernel,
+        grid_spec=pltpu.PrefetchScalarGridSpec(
+            num_scalar_prefetch=2, grid=(), in_specs=[ANY] * (nl + nr), out_specs=VMEM,
+            scratch_shapes=[
+                pltpu.VMEM(((left_total + 1) * TILE, TILE), BF16),
+                pltpu.VMEM(((right_total + 1) * TILE, TILE), BF16),
+                pltpu.SemaphoreType.DMA((nl + nr,)),
+            ]),
+        out_shape=blocks_of(cap),
+        compiler_params=pltpu.CompilerParams(vmem_limit_bytes=VMEM_LIMIT),
+        name="square_blocks",
+    )(lists, meta, *lefts, *rights)
+
+
+def next_blocks(lists, meta, lefts, rights, own):
+    left_offs, left_total = offsets_of(lefts)
+    right_offs, right_total = offsets_of(rights)
+    nl, nr = len(lefts), len(rights)
+    n_out = 2 if own else 1
+
+    def kernel(list_ref, meta_ref, *refs):
+        outs = refs[nl + nr : nl + nr + n_out]
+        left, right, sems = refs[nl + nr + n_out :]
+        load_operands(refs[:nl], refs[nl : nl + nr], left_offs, right_offs, left, right, sems)
+        layer = lax.axis_index("layer")
+        column = layer if own else 1 - layer
+
+        def step(a, carry):
+            o = column * 16 + a
+            outs[0][at_block(a), :] = jnp.zeros((TILE, TILE), BF16)
+
+            @pl.when(meta_ref[1, o] != 0)
+            def _():
+                total = sum_of_products(o, list_ref, meta_ref[0, o], left, right)
+                start = left[at_block(meta_ref[2, o]), :].astype(F32)
+                outs[0][at_block(a), :] = (1.5 * start - 0.5 * total).astype(BF16)
+
+            return carry
+
+        lax.fori_loop(0, 16, step, 0)
+
+        if own:
+            def place(t, carry):
+                slot = meta_ref[3, t]
+
+                @pl.when(slot >= 0)
+                def _():
+                    outs[1][at_block(t), :] = right[at_block(slot), :]
+
+                @pl.when(slot < 0)
+                def _():
+                    outs[1][at_block(t), :] = jnp.zeros((TILE, TILE), BF16)
+
+                return carry
+
+            lax.fori_loop(0, 32, place, 0)
+
+    return pl.pallas_call(
+        kernel,
+        grid_spec=pltpu.PrefetchScalarGridSpec(
+            num_scalar_prefetch=2, grid=(), in_specs=[ANY] * (nl + nr), out_specs=[VMEM] * n_out,
+            scratch_shapes=[
+                pltpu.VMEM(((left_total + 1) * TILE, TILE), BF16),
+                pltpu.VMEM(((right_total + 1) * TILE, TILE), BF16),
+                pltpu.SemaphoreType.DMA((nl + nr,)),
+            ]),
+        out_shape=[blocks_of(16)] + ([blocks_of(32)] if own else []),
+        compiler_params=pltpu.CompilerParams(vmem_limit_bytes=VMEM_LIMIT),
+        name="next_own" if own else "next_sent",
+    )(lists, meta, *lefts, *rights)
+
+
+def interleave(mine, other):
+    def kernel(mine_ref, other_ref, out_ref):
+        layer = lax.axis_index("layer")
+        for a in range(16):
+            out_ref[at_block(2 * a + layer), :] = mine_ref[pl.ds(a * TILE, TILE), :]
+            out_ref[at_block(2 * a + 1 - layer), :] = other_ref[pl.ds(a * TILE, TILE), :]
+
+    return pl.pallas_call(
+        kernel,
+        in_specs=[VMEM, VMEM],
+        out_specs=VMEM,
+        out_shape=blocks_of(32),
+        compiler_params=pltpu.CompilerParams(vmem_limit_bytes=VMEM_LIMIT),
+        name="interleave",
+    )(mine, other)
+
+
+def dot01(a, b):
+    return jnp.dot(a.astype(BF16), b.astype(BF16), preferred_element_type=F32)
+
+
+def dot01t(a, b):
+    return lax.dot_general(a.astype(BF16), b.astype(BF16), (((1,), (1,)), ((), ())), preferred_element_type=F32)
+
+
+def whole(value):
+    return value.astype(jnp.int32)
+
+
+def choose(hit, value, length, dest):
+    slots = lax.broadcasted_iota(jnp.int32, (length, *value.shape), 0)
+    return jnp.sum(jnp.where(hit[None] & (dest[None] == slots), value[None], 0), axis=tuple(range(1, value.ndim + 1)))
+
+
+def iota(shape, dim):
+    return lax.broadcasted_iota(jnp.int32, shape, dim)
+
+
+def zz(k):
+    return k % 32 // 8
+
+
+def yy(k):
+    return k % 8 // 2
+
+
+def tier_of(pattern, keep_square):
+    owner = (iota((4, 64), 1) // 32 == iota((4, 64), 0) // 2) & (iota((4, 64), 1) % 2 == iota((4, 64), 0) % 2)
+    group = iota((64, 32), 0) % 32 == iota((64, 32), 1)
+    c, ring = iota((32, 8), 0), iota((32, 8), 1)
+    ring = (c % 2 == ring // 4) & (jnp.where(c % 2 == 0, zz(c), yy(c)) == ring % 4)
+    counts = dot01(owner, pattern)
+    sent = jnp.max(counts)
+    half = jnp.maximum(jnp.max(counts[0] + counts[1]), jnp.max(counts[2] + counts[3]))
+    chunks = dot01(counts, group)
+    first, second = jnp.max(chunks), jnp.max(dot01(chunks, ring))
+    third = jnp.max(dot01(dot01(owner, keep_square), group))
+    which = jnp.int32(len(TIERS))
+    for n in reversed(range(len(TIERS))):
+        c1, c2, c3 = TIERS[n]
+        which = jnp.where((first <= c1) & (second <= c2) & (third <= c3), n, which)
+    return jnp.where((half <= HALF) & (sent <= SENT), which, len(TIERS)).astype(jnp.int32)
+
+
+def tables(pattern, keep_square, keep_next, tier):
+    c1, c2, c3 = [jnp.where(tier == 0, a, b) for a, b in zip(*TIERS, strict=True)]
+    most1, most2 = [max(t[n] for t in TIERS) for n in range(2)]
+    layer, row, col = lax.axis_index("layer"), lax.axis_index("row"), lax.axis_index("col")
+    z, y, core, x = col // 8, col // 2 % 4, col % 2, row * 2 + layer
+    i, k = iota((64, 64), 0), iota((64, 64), 1)
+    a16, k16 = iota((16, 64), 0), iota((16, 64), 1)
+    j2, k2 = iota((2, 64), 0), iota((2, 64), 1)
+    rowsel = k16 == row * 32 + a16 * 2 + layer
+    colsel = j2 * 32 + col == k2
+    rank0 = dot01((i // 32 == k // 32) & (k < i), pattern)
+    rows = dot01(rowsel, pattern)
+    cols = dot01t(colsel, pattern)
+    col_rank0 = whole(dot01t(colsel, rank0))
+    has = rows > 0
+
+    below = iota((16, 16), 1) < iota((16, 16), 0)
+    sent_rank = whole(dot01(below, rows))
+    group_count = dot01(rows, i % 32 == k % 32)
+    rank1 = whole(dot01(below, group_count) + dot01(rows, (i % 32 == k % 32) & (i < k)))
+    n1 = jnp.sum(group_count, axis=0, keepdims=True)
+    before = jnp.where(k % 2 == 0, (zz(i) == zz(k)) & (yy(i) < yy(k)), (yy(i) == yy(k)) & (zz(i) < zz(k)))
+    rank2 = rank1 + whole(dot01(n1, before & (i < 32) & (i % 2 == k % 2)))
+    ez, ey = (zz(k16) - z) % 4, (yy(k16) - y) % 4
+    even = k16 % 2 == 0
+    slot_left = jnp.where(even, ez, ey) * c2 + jnp.where(k16 % 2 == core, 0, 4 * c2) + rank2
+    list1 = choose(has & (k16 % 32 == col), jnp.where(k16 // 32 == layer, a16 * 2 + layer, 32 + sent_rank), most1, rank1)
+    list2 = choose(
+        has & (k16 % 2 == core) & (jnp.where(even, ez, ey) == 0),
+        jnp.where(even, ey, ez) * c1 + rank1,
+        most2,
+        rank2,
+    )
+
+    slot_right = (k2 // 32 * 2 + j2 - x) % 4 * HALF + col_rank0
+    kept = dot01t(colsel, keep_square)
+    g3 = dot01(kept, (i // 32 == k // 32) & (i % 2 == k % 2) & (i < k))
+    rank3 = jnp.sum(g3, axis=0, keepdims=True) + jnp.where(j2 == 1, kept[:1], 0)
+    slot_square = (k2 // 32 * 2 + k2 % 2 - x) % 4 * c3 + whole(rank3)
+    keep_mine = dot01t(kept, rowsel)
+    next_mine = dot01t(dot01t(colsel, keep_next), rowsel)
+    place3 = whole(dot01t(rank3, rowsel))
+    nothing_left = 8 * c2
+
+    def pairs(right_has, keep, right_slots, nothing_right):
+        hit = (rows[None] * right_has[:, None] * keep[:, :, None]).reshape(32, 64)
+        rank = whole(dot01(hit, i < k))
+        nothing = (nothing_left << SHIFT) + nothing_right
+        code = ((slot_left[None] << SHIFT) + right_slots[:, None]).reshape(32, 64) - nothing
+        where = (hit[:, None] > 0) & (rank[:, None] == iota((32, 64, 64), 1))
+        return jnp.sum(jnp.where(where, code[:, None], 0), axis=2) + nothing, whole(jnp.sum(hit, axis=1))
+
+    square_list, square_count = pairs(cols, keep_mine, slot_right, 4 * HALF)
+    next_list, next_count = pairs(kept, next_mine, slot_square, 4 * c3)
+    square_meta = jnp.stack([square_count, whole(keep_mine).reshape(32), place3.reshape(32)])
+    start = jnp.sum(jnp.where(colsel[:, None] & has[None], slot_left[None] - nothing_left, 0), axis=2) + nothing_left
+    own = jnp.where(kept > 0, slot_square, -1)
+    own = jnp.where(layer == 0, own[0], own[1])
+    own = lax.dynamic_slice(own, (row * 32,), (32,))
+    next_meta = jnp.stack([next_count, whole(next_mine).reshape(32), start.reshape(32), own])
+    return list1, list2, square_list, square_meta, next_list, next_meta
+
+
+def packed(caps, values, pattern, keep_square, keep_next, own, received, *lists):
+    c1, c2, c3 = caps
+    list1, list2, square_list, square_meta, next_list, next_meta = lists
+
+    with jax.named_scope("left_rows"):
+        (chunk,) = repack(list1, [values, received], [c1], "pack_rows")
+        chunks = [chunk] + [shift_ring(chunk, -e, 0) for e in (1, 2, 3)]
+        (ring,) = repack(list2, chunks, [c2], "pack_ring")
+        rings = [ring] + [shift_ring(ring, -e, 1) for e in (1, 2, 3)]
+        lefts = rings + [swap_core(v) for v in rings]
+    with jax.named_scope("right_columns"):
+        rights = [own] + [shift_x(after(own, chunk), -e) for e in (1, 2, 3)]
+    with jax.named_scope("square"):
+        sq = square_blocks(square_list, square_meta, lefts, rights, c3)
+        squares = [sq] + [shift_x(sq, -e) for e in (1, 2, 3)]
+    with jax.named_scope("next"):
+        (sent,) = next_blocks(next_list, next_meta, lefts, squares, False)
+        other = swap_layer(sent)
+        mine, square = next_blocks(next_list, next_meta, lefts, squares, True)
+        next_sign = interleave(mine, other)
+    return (square, next_sign)
+
+
+def local(values, pattern, keep_square, keep_next):
+    own, sent = pack_column(pattern, values)
+    received = swap_layer(sent)
+    tier = tier_of(pattern, keep_square)
+    lists = tables(pattern, keep_square, keep_next, tier)
+
+    def without_lists(*args):
+        return dense(*args[:4])
+
+    branches = [functools.partial(packed, caps) for caps in TIERS] + [without_lists]
+    return lax.switch(tier, branches, values, pattern, keep_square, keep_next, own, received, *lists)
+
+
 def solution(mesh):
     return jax.shard_map(
         local,

time: 574 us -> 178 us (0.31)
  waiting for transfers between devices: 503 us -> 73.8 us
  Pallas kernels: 0 us -> 36.3 us
  matrix products: 34.4 us -> 8.39 us
  starting transfers between devices: 0.29 us -> 19.4 us
  other arithmetic: 17.4 us -> 11 us
  local copies, waits for them, and re-layouts: 1.64 us -> 7.86 us
    psum x4 -> x0, waiting for transfers between devices: 370 us -> none  [the longest x2 228 us: multiply(): summed = lax.psum(layer_part, 'layer')]
    all_gather x3 -> x0, waiting for transfers between devices: 132 us -> none  [the longest x2 74.8 us: column_block(): gathered = lax.all_gather(matrix, 'layer', axis=1, tiled=True)]
    ppermute x0 -> x18, waiting for transfers between devices: none -> 73.8 us  [the longest x6 59.6 us: shift_x(): lax.ppermute(value, ('layer', 'row'), [(flat(x), flat((x + by) % 4)) for...]
    pallas_call x0 -> x7, Pallas kernels: none -> 36.3 us  [the longest x2 17.1 us: next_blocks(): pl.pallas_call(kernel, grid_spec=pltpu.PrefetchScalarGridSpec(num_scalar_...]
    dot_general x2 -> x19, matrix products: 34.4 us -> 8.39 us  [the longest x13 5.75 us: dot01(): return jnp.dot(a.astype(BF16), b.astype(BF16), preferred_element_type=F32)]
    ppermute x0 -> x18, starting transfers between devices: none -> 19.4 us  [the longest x6 10.4 us: shift_ring(): return lax.ppermute(value, 'col', [(c, target(c)) for c in range(32)])]
    convert_element_type x5, other arithmetic: 8.79 us -> 1.51 us  [the longest x2 0.84 us: dot01(): return jnp.dot(a.astype(BF16), b.astype(BF16), preferred_element_type=F32)]
  transfers between devices with their start and end apart: 7 -> 18, of which waited for: 7 -> 9; matrix products, arithmetic and copies ran while one was open for 0% -> 10% of each run, Pallas kernels for 0% -> 5%
where the time goes in v1:
time: 178 us; the launch traced here: 177 us
  waiting for transfers between devices  73.8 us (41%)
  Pallas kernels  36.3 us (20%)
  between operations  20 us (11%)
  starting transfers between devices  19.4 us (11%)
  other arithmetic  11 us (6%)
  matrix products  8.39 us (5%)
  local copies, waits for them, and re-layouts  7.86 us (4%)
    ppermute x6, waiting for transfers between devices, shift_x(): lax.ppermute(value, ('layer', 'row'), [(flat(x), flat((x + by) % 4)) for...  59.6 us
    pallas_call x2, Pallas kernels, next_blocks(): pl.pallas_call(kernel, grid_spec=pltpu.PrefetchScalarGridSpec(num_scalar_...  17.1 us
    ppermute x6, starting transfers between devices, shift_ring(): return lax.ppermute(value, 'col', [(c, target(c)) for c in range(32)])  10.4 us
    ppermute x6, waiting for transfers between devices, shift_ring(): return lax.ppermute(value, 'col', [(c, target(c)) for c in range(32)])  10.1 us
    pallas_call x1, Pallas kernels, square_blocks(): pl.pallas_call(kernel, grid_spec=pltpu.PrefetchScalarGridSpec(num_scalar_...  8.17 us
    ppermute x6, starting transfers between devices, shift_x(): lax.ppermute(value, ('layer', 'row'), [(flat(x), flat((x + by) % 4)) for...  7.44 us
    dot_general x13, matrix products, dot01(): return jnp.dot(a.astype(BF16), b.astype(BF16), preferred_element_type=F32)  5.75 us
    pallas_call x2, Pallas kernels, repack(): pl.pallas_call(kernel, grid_spec=pltpu.PrefetchScalarGridSpec(num_scalar_...  4.79 us
  transfers between devices with their start and end apart: 18, of which 9 were waited for; matrix products, arithmetic and copies ran while one was open for 10% of the time, Pallas kernels for 5%

profile of v1, /device:TPU:0, one launch (start us, length us, event | category | flops | bytes accessed | tf_op | source)
XLA Modules:
  0.0 177.0 jit_solution(16076533322903232641)
XLA Ops:
  7.2 4.0 %pack_column.1 = (bf16[2304,128]{1,0:T(8,128)(2,1)}, bf16[1408,128]{1,0:T(8,128)(2,1)}) custom-call(s32[64,64]{1,0:T(8,128)} %pattern_ref.1, bf16[4096,128]{1,0:T(8,128)(2,1)} %values_ref.1), custom_call_target="tpu_custom_call" | custom-call | tf_op jit(solution)/shard_map/pack_column/pallas_call | solution.py:152
  11.2 0.9 collective-permute-start.34
  14.5 0.9 fusion.218
  15.4 1.6 fusion.20
  17.1 0.9 fusion.154
  19.7 0.9 fusion.16
  22.8 0.8 convolution_reduce_fusion.1
  34.1 136.0 %conditional.1 = (bf16[4096,128]{1,0:T(8,128)(2,1)}, bf16[4096,128]{1,0:T(8,128)(2,1)}) conditional(s32[]{:T(128)} %clamp.3, (f32[2,16,64]{2,1,0:T(8,128)S(1)}, f32[2,16,64]{2,1,0:T(8,128)S(1)}, f32[32]{0:T(128)}, s32[32,64]{1,0:T(8,128)S(1)}, s32[32,64,64]{2,1,0:T(8,128)S(1)}, /*index=5*/s32[16,64]{1,0:T(8,128)S(1)}, ...), branch_computations={%region_11.16_spmd, %region_16.21_spmd, %region_21.26_spmd} | conditional | flops 17191403520 | bytes 295953984 | solution.py:463
  34.8 1.0 select_reduce_fusion.3.index_ref
  35.9 1.7 pack_rows.2.refs_0_
  37.6 3.1 %collective-permute-start = (bf16[1536,128]{1,0:T(8,128)(2,1)}, bf16[1536,128]{1,0:T(8,128)(2,1)S(1)}, u32[]{:S(2)}, u32[]{:S(2)}) collective-permute-start(bf16[1536,128]{1,0:T(8,128)(2,1)} %pack_rows.2.refs_0_), channel_id=1, source_target_pairs={{0,6},{1,25},{2,0},{3,27},{4,2},{5,29},{6,4},{7,31},{8,14},{9,1},{... | collective-permute-start | bytes 1179656 | tf_op jit(solution)/shard_map/cond/branch_0_fun/left_rows/ppermute | solution.py:81
  41.3 1.3 collective-permute-start.2
  43.3 2.1 %select_reduce_fusion.2.index_ref = s32[46]{0:T(128)} fusion(s32[46,16,64]{2,1,0:T(8,128)S(1)} %get-tuple-element.546, s32[16,64]{1,0:T(8,128)S(1)} %multiply_add_fusion, s32[16,64]{1,0:T(8,128)S(1)} %get-tuple-element.545, pred[16,64]{1,0:T(8,128)(4,1)} %get-tuple-element.704), kind=kLoop, calls=%fused_computation.2 | loop fusion | flops 188370 | bytes 197816 | tf_op jit(solution)/shard_map/reduce_sum | solution.py:334
  45.4 5.0 %collective-permute-done.refs_1_ = bf16[1536,128]{1,0:T(8,128)(2,1)S(1)} collective-permute-done((bf16[1536,128]{1,0:T(8,128)(2,1)}, bf16[1536,128]{1,0:T(8,128)(2,1)S(1)}, u32[]{:S(2)}, u32[]{:S(2)}) %collective-permute-start) | collective-permute-done | bytes 393248 | tf_op jit(solution)/shard_map/cond/branch_0_fun/left_rows/ppermute | solution.py:81
  50.5 4.0 %collective-permute-done.2.refs_3_ = bf16[1536,128]{1,0:T(8,128)(2,1)S(1)} collective-permute-done((bf16[1536,128]{1,0:T(8,128)(2,1)}, bf16[1536,128]{1,0:T(8,128)(2,1)S(1)}, u32[]{:S(2)}, u32[]{:S(2)}) %collective-permute-start.2) | collective-permute-done | bytes 393248 | tf_op jit(solution)/shard_map/cond/branch_0_fun/left_rows/ppermute | solution.py:81
  55.2 3.1 %pack_ring.2.refs_0_ = bf16[4352,128]{1,0:T(8,128)(2,1)} custom-call(s32[46]{0:T(128)} %select_reduce_fusion.2.index_ref, bf16[1536,128]{1,0:T(8,128)(2,1)} %pack_rows.2.refs_0_, bf16[1536,128]{1,0:T(8,128)(2,1)} %copy-done.19, bf16[1536,128]{1,0:T(8,128)(2,1)} %copy-done.20, bf16[1536,128]{1,0:T(8,128)(2,1)} %copy-done.21), custom_call_target="tpu_custom_call" | custom-call | tf_op jit(solution)/shard_map/cond/branch_0_fun/left_rows/pack_ring/pallas_call | solution.py:177
  58.3 4.4 %collective-permute-start.3 = (bf16[4352,128]{1,0:T(8,128)(2,1)}, bf16[4352,128]{1,0:T(8,128)(2,1)S(1)}, u32[]{:S(2)}, u32[]{:S(2)}) collective-permute-start(bf16[4352,128]{1,0:T(8,128)(2,1)} %pack_ring.2.refs_0_), channel_id=1, source_target_pairs={{0,24},{1,7},{2,26},{3,1},{4,28},{5,3},{6,30},{7,5},{8,0},{9,15},{... | collective-permute-start | bytes 3342344 | tf_op jit(solution)/shard_map/cond/branch_0_fun/left_rows/ppermute | solution.py:81
  62.7 1.0 collective-permute-start.5
  63.7 2.4 %collective-permute-start.10 = (bf16[2304,128]{1,0:T(8,128)(2,1)S(1)}, bf16[2304,128]{1,0:T(8,128)(2,1)S(1)}, u32[]{:S(2)}, u32[]{:S(2)}) collective-permute-start(bf16[2304,128]{1,0:T(8,128)(2,1)S(1)} %copy-done.5), channel_id=1, source_target_pairs={{0,96},{64,0},{32,64},{96,32},{1,97},{65,1},{33,65},{97,33},{2,98}... | collective-permute-start | bytes 1769480 | tf_op jit(solution)/shard_map/cond/branch_0_fun/right_columns/ppermute | solution.py:69
  66.7 22.6 %collective-permute-done.10.refs_9_ = bf16[2304,128]{1,0:T(8,128)(2,1)S(1)} collective-permute-done((bf16[2304,128]{1,0:T(8,128)(2,1)S(1)}, bf16[2304,128]{1,0:T(8,128)(2,1)S(1)}, u32[]{:S(2)}, u32[]{:S(2)}) %collective-permute-start.10) | collective-permute-done | bytes 589856 | tf_op jit(solution)/shard_map/cond/branch_0_fun/right_columns/ppermute | solution.py:69
  90.6 1.1 collective-permute-done.5.refs_3_
  93.8 15.1 %collective-permute-done.12.refs_11_ = bf16[2304,128]{1,0:T(8,128)(2,1)S(1)} collective-permute-done((bf16[2304,128]{1,0:T(8,128)(2,1)S(1)}, bf16[2304,128]{1,0:T(8,128)(2,1)S(1)}, u32[]{:S(2)}, u32[]{:S(2)}) %collective-permute-start.12) | collective-permute-done | bytes 589856 | tf_op jit(solution)/shard_map/cond/branch_0_fun/right_columns/ppermute | solution.py:69
  109.7 8.2 %square_blocks.2.refs_8_ = bf16[2048,128]{1,0:T(8,128)(2,1)} custom-call(s32[32,64]{1,0:T(8,128)} %broadcast_add_fusion.list_ref, s32[3,32]{1,0:T(4,128)S(1)} %get-tuple-element.573.meta_ref, bf16[4352,128]{1,0:T(8,128)(2,1)} %pack_ring.2.refs_0_, bf16[4352,128]{1,0:T(8,128)(2,1)} %copy-done.1, bf16[4352,128]{1,0:T(8,128)(2,1)} %collective-permute-done.4.refs_2_, ...), custom_call_target="tpu_custom_call" | custom-call | tf_op jit(solution)/shard_map/cond/branch_0_fun/square/square_blocks/pallas_call | solution.py:230
  117.8 2.5 %collective-permute-start.13 = (bf16[2048,128]{1,0:T(8,128)(2,1)}, bf16[2048,128]{1,0:T(8,128)(2,1)S(1)}, u32[]{:S(2)}, u32[]{:S(2)}) collective-permute-start(bf16[2048,128]{1,0:T(8,128)(2,1)} %square_blocks.2.refs_8_), channel_id=1, source_target_pairs={{0,96},{64,0},{32,64},{96,32},{1,97},{65,1},{33,65},{97,33},{2,98}... | collective-permute-start | bytes 1572872 | tf_op jit(solution)/shard_map/cond/branch_0_fun/square/ppermute | solution.py:69
  120.4 1.3 collective-permute-start.15
  123.0 10.0 %collective-permute-done.13.refs_9_ = bf16[2048,128]{1,0:T(8,128)(2,1)S(1)} collective-permute-done((bf16[2048,128]{1,0:T(8,128)(2,1)}, bf16[2048,128]{1,0:T(8,128)(2,1)S(1)}, u32[]{:S(2)}, u32[]{:S(2)}) %collective-permute-start.13) | collective-permute-done | bytes 524320 | tf_op jit(solution)/shard_map/cond/branch_0_fun/square/ppermute | solution.py:69
  133.0 3.9 %collective-permute-done.14.refs_10_ = bf16[2048,128]{1,0:T(8,128)(2,1)S(1)} collective-permute-done((bf16[2048,128]{1,0:T(8,128)(2,1)}, bf16[2048,128]{1,0:T(8,128)(2,1)S(1)}, u32[]{:S(2)}, u32[]{:S(2)}) %collective-permute-start.14) | collective-permute-done | bytes 524320 | tf_op jit(solution)/shard_map/cond/branch_0_fun/square/ppermute | solution.py:69
  136.9 8.1 %collective-permute-done.15.refs_11_ = bf16[2048,128]{1,0:T(8,128)(2,1)S(1)} collective-permute-done((bf16[2048,128]{1,0:T(8,128)(2,1)}, bf16[2048,128]{1,0:T(8,128)(2,1)S(1)}, u32[]{:S(2)}, u32[]{:S(2)}) %collective-permute-start.15) | collective-permute-done | bytes 524320 | tf_op jit(solution)/shard_map/cond/branch_0_fun/square/ppermute | solution.py:69
  145.9 7.5 %next_sent.2 = bf16[2048,128]{1,0:T(8,128)(2,1)} custom-call(s32[32,64]{1,0:T(8,128)} %broadcast_add_fusion.1.list_ref, s32[4,32]{1,0:T(4,128)S(1)} %get-tuple-element.540.meta_ref, bf16[4352,128]{1,0:T(8,128)(2,1)} %pack_ring.2.refs_0_, bf16[4352,128]{1,0:T(8,128)(2,1)} %copy-done.1, bf16[4352,128]{1,0:T(8,128)(2,1)} %collective-permute-done.4.refs_2_, ...), custom_call_target="tpu_custom_call" | custom-call | tf_op jit(solution)/shard_map/cond/branch_0_fun/next/next_sent/pallas_call | solution.py:288
  153.4 9.6 %next_own.2 = (bf16[2048,128]{1,0:T(8,128)(2,1)}, bf16[4096,128]{1,0:T(8,128)(2,1)}) custom-call(s32[32,64]{1,0:T(8,128)} %broadcast_add_fusion.1.list_ref, s32[4,32]{1,0:T(4,128)S(1)} %get-tuple-element.540.meta_ref, bf16[4352,128]{1,0:T(8,128)(2,1)} %pack_ring.2.refs_0_, bf16[4352,128]{1,0:T(8,128)(2,1)} %copy-done.1, ...), custom_call_target="tpu_custom_call" | custom-call | tf_op jit(solution)/shard_map/cond/branch_0_fun/next/next_own/pallas_call | solution.py:288
  163.1 4.0 %collective-permute-done.16.other_ref = bf16[2048,128]{1,0:T(8,128)(2,1)S(1)} collective-permute-done((bf16[2048,128]{1,0:T(8,128)(2,1)}, bf16[2048,128]{1,0:T(8,128)(2,1)S(1)}, u32[]{:S(2)}, u32[]{:S(2)}) %collective-permute-start.16) | collective-permute-done | bytes 524320 | tf_op jit(solution)/shard_map/cond/branch_0_fun/next/ppermute | solution.py:89
  167.9 2.2 %interleave.2 = bf16[4096,128]{1,0:T(8,128)(2,1)} custom-call(bf16[2048,128]{1,0:T(8,128)(2,1)} %get-tuple-element.577.mine_ref, bf16[2048,128]{1,0:T(8,128)(2,1)} %copy-done.15), custom_call_target="tpu_custom_call" | custom-call | tf_op jit(solution)/shard_map/cond/branch_0_fun/next/interleave/pallas_call | solution.py:310
  (184 shorter events, 21.6 us)
Async XLA Ops:
  11.2 19.9 %collective-permute-start.34 = (bf16[1408,128]{1,0:T(8,128)(2,1)}, bf16[1408,128]{1,0:T(8,128)(2,1)S(1)}, u32[]{:S(2)}, u32[]{:S(2)}) collective-permute-start(bf16[1408,128]{1,0:T(8,128)(2,1)} %get-tuple-element.634), channel_id=1, source_target_pairs={{0,64},{64,0},{1,65},{65,1},{2,66},{66,2},{3,67},{67,3},{4,68},{68... | collective-permute-start | bytes 1081352 | tf_op jit(solution)/shard_map/ppermute | solution.py:89
  35.8 30.8 %copy-start.73 = (s32[2,64]{1,0:T(2,128)S(1)}, s32[2,64]{1,0:T(2,128)}, u32[]{:S(2)}) copy-start(s32[2,64]{1,0:T(2,128)} %get-tuple-element.572) | copy-start | bytes 1540 | tf_op jit(solution)/shard_map/cond
  35.8 30.8 %copy-start.75 = (s32[2,64]{1,0:T(2,128)S(1)}, s32[2,64]{1,0:T(2,128)}, u32[]{:S(2)}) copy-start(s32[2,64]{1,0:T(2,128)} %get-tuple-element.642) | copy-start | bytes 1540 | tf_op jit(solution)/shard_map/cond
  35.8 30.9 %copy-start.77 = (s32[2,64]{1,0:T(2,128)S(1)}, s32[2,64]{1,0:T(2,128)}, u32[]{:S(2)}) copy-start(s32[2,64]{1,0:T(2,128)} %get-tuple-element.652) | copy-start | bytes 1540 | tf_op jit(solution)/shard_map/cond
  35.8 30.9 %copy-start.79 = (s32[2,64]{1,0:T(2,128)S(1)}, s32[2,64]{1,0:T(2,128)}, u32[]{:S(2)}) copy-start(s32[2,64]{1,0:T(2,128)} %get-tuple-element.569) | copy-start | bytes 1540 | tf_op jit(solution)/shard_map/cond
  35.8 30.9 %copy-start.81 = (s32[2,64]{1,0:T(2,128)S(1)}, s32[2,64]{1,0:T(2,128)}, u32[]{:S(2)}) copy-start(s32[2,64]{1,0:T(2,128)} %get-tuple-element.570) | copy-start | bytes 1540 | tf_op jit(solution)/shard_map/cond
  35.8 30.9 %copy-start.83 = (s32[2,64]{1,0:T(2,128)S(1)}, s32[2,64]{1,0:T(2,128)}, u32[]{:S(2)}) copy-start(s32[2,64]{1,0:T(2,128)} %get-tuple-element.571) | copy-start | bytes 1540 | tf_op jit(solution)/shard_map/cond
  35.8 55.9 %copy-start.43 = (pred[64]{0:T(512)(128)(4,1)S(1)}, pred[64]{0:T(512)(128)(4,1)}, u32[]{:S(2)}) copy-start(pred[64]{0:T(512)(128)(4,1)} %get-tuple-element.673) | copy-start | bytes 196 | tf_op jit(solution)/shard_map/cond
  35.8 55.9 %copy-start.46 = (s32[64]{0:T(128)S(1)}, s32[64]{0:T(128)}, u32[]{:S(2)}) copy-start(s32[64]{0:T(128)} %get-tuple-element.677) | copy-start | bytes 772 | tf_op jit(solution)/shard_map/cond
  35.8 55.9 %copy-start.49 = (s32[64]{0:T(128)S(1)}, s32[64]{0:T(128)}, u32[]{:S(2)}) copy-start(s32[64]{0:T(128)} %get-tuple-element.675) | copy-start | bytes 772 | tf_op jit(solution)/shard_map/cond
  35.9 55.9 %copy-start.63 = (s32[2,1,64]{2,0,1:T(2,128)S(1)}, s32[2,1,64]{2,0,1:T(2,128)}, u32[]{:S(2)}) copy-start(s32[2,1,64]{2,0,1:T(2,128)} %get-tuple-element.538) | copy-start | bytes 1540 | tf_op jit(solution)/shard_map/cond
  37.6 54.9 %copy-start.68 = (f32[32]{0:T(128)S(1)}, f32[32]{0:T(128)}, u32[]{:S(2)}) copy-start(f32[32]{0:T(128)} %get-tuple-element.565) | copy-start | bytes 388 | tf_op jit(solution)/shard_map/cond
  37.6 12.9 %collective-permute-start = (bf16[1536,128]{1,0:T(8,128)(2,1)}, bf16[1536,128]{1,0:T(8,128)(2,1)S(1)}, u32[]{:S(2)}, u32[]{:S(2)}) collective-permute-start(bf16[1536,128]{1,0:T(8,128)(2,1)} %pack_rows.2.refs_0_), channel_id=1, source_target_pairs={{0,6},{1,25},{2,0},{3,27},{4,2},{5,29},{6,4},{7,31},{8,14},{9,1},{... | collective-permute-start | bytes 1179656 | tf_op jit(solution)/shard_map/cond/branch_0_fun/left_rows/ppermute | solution.py:81
  40.6 9.8 %collective-permute-start.1 = (bf16[1536,128]{1,0:T(8,128)(2,1)}, bf16[1536,128]{1,0:T(8,128)(2,1)S(1)}, u32[]{:S(2)}, u32[]{:S(2)}) collective-permute-start(bf16[1536,128]{1,0:T(8,128)(2,1)} %pack_rows.2.refs_0_), channel_id=1, source_target_pairs={{0,4},{1,17},{2,6},{3,19},{4,0},{5,21},{6,2},{7,23},{8,12},{9,25},... | collective-permute-start | bytes 1179656 | tf_op jit(solution)/shard_map/cond/branch_0_fun/left_rows/ppermute | solution.py:81
  41.3 50.4 %copy-start.52 = (pred[64]{0:T(512)(128)(4,1)S(1)}, pred[64]{0:T(512)(128)(4,1)}, u32[]{:S(2)}) copy-start(pred[64]{0:T(512)(128)(4,1)} %copy-done.51) | copy-start | bytes 196 | tf_op jit(solution)/shard_map/cond
  41.3 50.4 %copy-start.56 = (s32[64]{0:T(128)S(1)}, s32[64]{0:T(128)}, u32[]{:S(2)}) copy-start(s32[64]{0:T(128)} %copy-done.55) | copy-start | bytes 772 | tf_op jit(solution)/shard_map/cond
  41.3 50.4 %copy-start.60 = (s32[64]{0:T(128)S(1)}, s32[64]{0:T(128)}, u32[]{:S(2)}) copy-start(s32[64]{0:T(128)} %copy-done.59) | copy-start | bytes 772 | tf_op jit(solution)/shard_map/cond
  41.3 13.1 %collective-permute-start.2 = (bf16[1536,128]{1,0:T(8,128)(2,1)}, bf16[1536,128]{1,0:T(8,128)(2,1)S(1)}, u32[]{:S(2)}, u32[]{:S(2)}) collective-permute-start(bf16[1536,128]{1,0:T(8,128)(2,1)} %pack_rows.2.refs_0_), channel_id=1, source_target_pairs={{0,2},{1,9},{2,4},{3,11},{4,6},{5,13},{6,0},{7,15},{8,10},{9,17},{... | collective-permute-start | bytes 1179656 | tf_op jit(solution)/shard_map/cond/branch_0_fun/left_rows/ppermute | solution.py:81
  58.3 31.0 %collective-permute-start.3 = (bf16[4352,128]{1,0:T(8,128)(2,1)}, bf16[4352,128]{1,0:T(8,128)(2,1)S(1)}, u32[]{:S(2)}, u32[]{:S(2)}) collective-permute-start(bf16[4352,128]{1,0:T(8,128)(2,1)} %pack_ring.2.refs_0_), channel_id=1, source_target_pairs={{0,24},{1,7},{2,26},{3,1},{4,28},{5,3},{6,30},{7,5},{8,0},{9,15},{... | collective-permute-start | bytes 3342344 | tf_op jit(solution)/shard_map/cond/branch_0_fun/left_rows/ppermute | solution.py:81
  62.7 27.4 %collective-permute-start.4 = (bf16[4352,128]{1,0:T(8,128)(2,1)}, bf16[4352,128]{1,0:T(8,128)(2,1)}, u32[]{:S(2)}, u32[]{:S(2)}) collective-permute-start(bf16[4352,128]{1,0:T(8,128)(2,1)} %pack_ring.2.refs_0_), channel_id=1, source_target_pairs={{0,16},{1,5},{2,18},{3,7},{4,20},{5,1},{6,22},{7,3},{8,24},{9,13},... | collective-permute-start | bytes 3342344 | tf_op jit(solution)/shard_map/cond/branch_0_fun/left_rows/ppermute | solution.py:81
  62.7 29.0 %collective-permute-start.5 = (bf16[4352,128]{1,0:T(8,128)(2,1)}, bf16[4352,128]{1,0:T(8,128)(2,1)}, u32[]{:S(2)}, u32[]{:S(2)}) collective-permute-start(bf16[4352,128]{1,0:T(8,128)(2,1)} %pack_ring.2.refs_0_), channel_id=1, source_target_pairs={{0,8},{1,3},{2,10},{3,5},{4,12},{5,7},{6,14},{7,1},{8,16},{9,11},{... | collective-permute-start | bytes 3342344 | tf_op jit(solution)/shard_map/cond/branch_0_fun/left_rows/ppermute | solution.py:81
  63.7 25.6 %collective-permute-start.10 = (bf16[2304,128]{1,0:T(8,128)(2,1)S(1)}, bf16[2304,128]{1,0:T(8,128)(2,1)S(1)}, u32[]{:S(2)}, u32[]{:S(2)}) collective-permute-start(bf16[2304,128]{1,0:T(8,128)(2,1)S(1)} %copy-done.5), channel_id=1, source_target_pairs={{0,96},{64,0},{32,64},{96,32},{1,97},{65,1},{33,65},{97,33},{2,98}... | collective-permute-start | bytes 1769480 | tf_op jit(solution)/shard_map/cond/branch_0_fun/right_columns/ppermute | solution.py:69
  66.1 25.7 %collective-permute-start.11 = (bf16[2304,128]{1,0:T(8,128)(2,1)S(1)}, bf16[2304,128]{1,0:T(8,128)(2,1)}, u32[]{:S(2)}, u32[]{:S(2)}) collective-permute-start(bf16[2304,128]{1,0:T(8,128)(2,1)S(1)} %copy-done.5), channel_id=1, source_target_pairs={{0,32},{64,96},{32,0},{96,64},{1,33},{65,97},{33,1},{97,65},{2,34}... | collective-permute-start | bytes 1769480 | tf_op jit(solution)/shard_map/cond/branch_0_fun/right_columns/ppermute | solution.py:69
  89.3 19.6 %collective-permute-start.6 = (bf16[4352,128]{1,0:T(8,128)(2,1)}, bf16[4352,128]{1,0:T(8,128)(2,1)}, u32[]{:S(2)}, u32[]{:S(2)}) collective-permute-start(bf16[4352,128]{1,0:T(8,128)(2,1)} %pack_ring.2.refs_0_), channel_id=1, source_target_pairs={{0,1},{1,0},{2,3},{3,2},{4,5},{5,4},{6,7},{7,6},{8,9},{9,8},{10,11... | collective-permute-start | bytes 3342344 | tf_op jit(solution)/shard_map/cond/branch_0_fun/left_rows/ppermute | solution.py:85
  90.1 18.7 %collective-permute-start.7 = (bf16[4352,128]{1,0:T(8,128)(2,1)S(1)}, bf16[4352,128]{1,0:T(8,128)(2,1)}, u32[]{:S(2)}, u32[]{:S(2)}) collective-permute-start(bf16[4352,128]{1,0:T(8,128)(2,1)S(1)} %collective-permute-done.3.refs_1_), channel_id=1, source_target_pairs={{0,1},{1,0},{2,3},{3,2},{4,5},{5,4},{6,7},{7,6},{8,9},{9,8},{10,11... | collective-permute-start | bytes 3342344 | tf_op jit(solution)/shard_map/cond/branch_0_fun/left_rows/ppermute | solution.py:85
  90.1 19.5 %collective-permute-start.8 = (bf16[4352,128]{1,0:T(8,128)(2,1)}, bf16[4352,128]{1,0:T(8,128)(2,1)}, u32[]{:S(2)}, u32[]{:S(2)}) collective-permute-start(bf16[4352,128]{1,0:T(8,128)(2,1)} %collective-permute-done.4.refs_2_), channel_id=1, source_target_pairs={{0,1},{1,0},{2,3},{3,2},{4,5},{5,4},{6,7},{7,6},{8,9},{9,8},{10,11... | collective-permute-start | bytes 3342344 | tf_op jit(solution)/shard_map/cond/branch_0_fun/left_rows/ppermute | solution.py:85
  91.7 18.0 %collective-permute-start.9 = (bf16[4352,128]{1,0:T(8,128)(2,1)}, bf16[4352,128]{1,0:T(8,128)(2,1)}, u32[]{:S(2)}, u32[]{:S(2)}) collective-permute-start(bf16[4352,128]{1,0:T(8,128)(2,1)} %collective-permute-done.5.refs_3_), channel_id=1, source_target_pairs={{0,1},{1,0},{2,3},{3,2},{4,5},{5,4},{6,7},{7,6},{8,9},{9,8},{10,11... | collective-permute-start | bytes 3342344 | tf_op jit(solution)/shard_map/cond/branch_0_fun/left_rows/ppermute | solution.py:85
  91.8 17.0 %collective-permute-start.12 = (bf16[2304,128]{1,0:T(8,128)(2,1)S(1)}, bf16[2304,128]{1,0:T(8,128)(2,1)S(1)}, u32[]{:S(2)}, u32[]{:S(2)}) collective-permute-start(bf16[2304,128]{1,0:T(8,128)(2,1)S(1)} %copy-done.5), channel_id=1, source_target_pairs={{0,64},{64,32},{32,96},{96,0},{1,65},{65,33},{33,97},{97,1},{2,66}... | collective-permute-start | bytes 1769480 | tf_op jit(solution)/shard_map/cond/branch_0_fun/right_columns/ppermute | solution.py:69
  117.8 15.1 %collective-permute-start.13 = (bf16[2048,128]{1,0:T(8,128)(2,1)}, bf16[2048,128]{1,0:T(8,128)(2,1)S(1)}, u32[]{:S(2)}, u32[]{:S(2)}) collective-permute-start(bf16[2048,128]{1,0:T(8,128)(2,1)} %square_blocks.2.refs_8_), channel_id=1, source_target_pairs={{0,96},{64,0},{32,64},{96,32},{1,97},{65,1},{33,65},{97,33},{2,98}... | collective-permute-start | bytes 1572872 | tf_op jit(solution)/shard_map/cond/branch_0_fun/square/ppermute | solution.py:69
  120.3 16.6 %collective-permute-start.14 = (bf16[2048,128]{1,0:T(8,128)(2,1)}, bf16[2048,128]{1,0:T(8,128)(2,1)S(1)}, u32[]{:S(2)}, u32[]{:S(2)}) collective-permute-start(bf16[2048,128]{1,0:T(8,128)(2,1)} %square_blocks.2.refs_8_), channel_id=1, source_target_pairs={{0,32},{64,96},{32,0},{96,64},{1,33},{65,97},{33,1},{97,65},{2,34}... | collective-permute-start | bytes 1572872 | tf_op jit(solution)/shard_map/cond/branch_0_fun/square/ppermute | solution.py:69
  120.4 24.7 %collective-permute-start.15 = (bf16[2048,128]{1,0:T(8,128)(2,1)}, bf16[2048,128]{1,0:T(8,128)(2,1)S(1)}, u32[]{:S(2)}, u32[]{:S(2)}) collective-permute-start(bf16[2048,128]{1,0:T(8,128)(2,1)} %square_blocks.2.refs_8_), channel_id=1, source_target_pairs={{0,64},{64,32},{32,96},{96,0},{1,65},{65,33},{33,97},{97,1},{2,66}... | collective-permute-start | bytes 1572872 | tf_op jit(solution)/shard_map/cond/branch_0_fun/square/ppermute | solution.py:69
  153.3 13.8 %collective-permute-start.16 = (bf16[2048,128]{1,0:T(8,128)(2,1)}, bf16[2048,128]{1,0:T(8,128)(2,1)S(1)}, u32[]{:S(2)}, u32[]{:S(2)}) collective-permute-start(bf16[2048,128]{1,0:T(8,128)(2,1)} %next_sent.2), channel_id=1, source_target_pairs={{0,64},{64,0},{1,65},{65,1},{2,66},{66,2},{3,67},{67,3},{4,68},{68... | collective-permute-start | bytes 1572872 | tf_op jit(solution)/shard_map/cond/branch_0_fun/next/ppermute | solution.py:89
  (23 other events, 232.8 us)

commit v2 on v1

v2 whole, which is shorter than its diff:
```python
import functools

import jax
import jax.numpy as jnp
from jax import lax
from jax.experimental import pallas as pl
from jax.experimental.pallas import tpu as pltpu
from jax.sharding import PartitionSpec as P

TILE = 128
SHIFT = 10
MASK = (1 << SHIFT) - 1
BF16 = jnp.bfloat16
F32 = jnp.float32
TIERS = ((18, 11, 14, 38, 18), (32, 16, 32, 128, 32))
VMEM_LIMIT = 20 * 1024 * 1024


def shift_ring(value, by, stage):
    def target(c):
        z, y, core = c // 8, c // 2 % 4, c % 2
        if core == stage:
            y = (y + by) % 4
        else:
            z = (z + by) % 4
        return z * 8 + y * 2 + core

    return lax.ppermute(value, "col", [(c, target(c)) for c in range(32)])


def carry_x(value):
    def target(i):
        layer, row, col = i // 64, i // 32 % 2, i % 32
        x = (row * 2 + layer + (1 if col % 2 == 0 else -1)) % 4
        return x % 2 * 64 + x // 2 * 32 + col

    return lax.ppermute(value, ("layer", "row", "col"), [(i, target(i)) for i in range(128)])


def gather_x(value):
    carried = carry_x(value)
    crossed = carry_x(swap_core(value))
    return [value, carried, carry_x(carried), swap_core(crossed)]


def place_x(x, e, core):
    return jnp.where(core == 0, (4 - e) % 4, e)


def swap_core(value):
    return lax.ppermute(value, "col", [(c, c ^ 1) for c in range(32)])


def swap_layer(value):
    return lax.ppermute(value, "layer", [(0, 1), (1, 0)])


def after(value, *others):
    return lax.optimization_barrier((value, *others))[0]


def blocks_of(count):
    return jax.ShapeDtypeStruct((count * TILE, TILE), BF16)


def at_block(index):
    return pl.ds(pl.multiple_of(index * TILE, TILE), TILE)


ANY = pl.BlockSpec(memory_space=pl.ANY)
VMEM = pl.BlockSpec(memory_space=pltpu.VMEM)


def fetch(sources, offsets, scratch, sems):
    copies = [
        pltpu.make_async_copy(src, scratch.at[pl.ds(off * TILE, src.shape[0])], sems.at[n])
        for n, (src, off) in enumerate(zip(sources, offsets, strict=True))
    ]
    for copy in copies:
        copy.start()
    return copies


def offsets_of(arrays):
    offsets, total = [], 0
    for a in arrays:
        offsets.append(total)
        total += a.shape[0] // TILE
    return offsets, total


def pack_column(pattern, values, half, part):
    def kernel(pattern_ref, values_ref, own_ref, sent_ref):
        layer = lax.axis_index("layer")
        first = lax.axis_index("row") * 32
        column = layer * 32 + lax.axis_index("col")

        def step(a, counts):
            n, m = counts
            for s in range(2):
                t = 2 * a + s
                keep = pattern_ref[first + t, column]

                @pl.when((keep != 0) & (n < half))
                def _(n=n, t=t):
                    own_ref[at_block(n), :] = values_ref[at_block(t), :]

                @pl.when((keep != 0) & (m < part) & (layer != s))
                def _(m=m, t=t):
                    sent_ref[at_block(m), :] = values_ref[at_block(t), :]

                n = n + keep
                m = m + jnp.where(layer != s, keep, 0)
            return n, m

        lax.fori_loop(0, 16, step, (0, 0))

    return pl.pallas_call(
        kernel,
        grid_spec=pltpu.PrefetchScalarGridSpec(
            num_scalar_prefetch=1, grid=(), in_specs=[VMEM], out_specs=[VMEM, VMEM]),
        out_shape=[blocks_of(half), blocks_of(part)],
        compiler_params=pltpu.CompilerParams(vmem_limit_bytes=VMEM_LIMIT),
        name="pack_column",
    )(pattern, values)


def pack_rows(pattern, values, received, cap):
    def kernel(pattern_ref, values_ref, received_ref, out_ref):
        layer = lax.axis_index("layer")
        first = lax.axis_index("row") * 32 + layer
        col = lax.axis_index("col")
        count = lax.fori_loop(0, 16, lambda a, n: n + pattern_ref[first + 2 * a, (1 - layer) * 32 + col], 0, unroll=4)

        def step(a, n):
            keep = pattern_ref[first + 2 * a, layer * 32 + col]

            @pl.when((keep != 0) & (n < cap))
            def _():
                out_ref[at_block(n), :] = values_ref[at_block(2 * a + layer), :]

            return n + keep

        end = lax.fori_loop(0, 16, step, jnp.where(layer == 0, 0, count))
        base = jnp.where(layer == 0, end, 0)

        def copy(n, carry):
            out_ref[at_block(base + n), :] = received_ref[at_block(n), :]
            return carry

        lax.fori_loop(0, jnp.minimum(count, cap - base), copy, 0)

    return pl.pallas_call(
        kernel,
        grid_spec=pltpu.PrefetchScalarGridSpec(
            num_scalar_prefetch=1, grid=(), in_specs=[VMEM, VMEM], out_specs=VMEM),
        out_shape=blocks_of(cap),
        compiler_params=pltpu.CompilerParams(vmem_limit_bytes=VMEM_LIMIT),
        name="pack_rows",
    )(pattern, values, received)


def pack_ring(info, chunks, cap):
    def kernel(info_ref, *refs):
        out = refs[4]
        for e in range(4):
            def copy(n, carry, e=e):
                place = jnp.minimum(info_ref[e, 2] + n, cap - 1)
                out[at_block(place), :] = refs[e][at_block(n), :]
                return carry

            lax.fori_loop(0, info_ref[e, 1], copy, 0)

    return pl.pallas_call(
        kernel,
        grid_spec=pltpu.PrefetchScalarGridSpec(
            num_scalar_prefetch=1, grid=(), in_specs=[VMEM] * 4, out_specs=VMEM),
        out_shape=blocks_of(cap),
        compiler_params=pltpu.CompilerParams(vmem_limit_bytes=VMEM_LIMIT),
        name="pack_ring",
    )(info, *chunks)


def sum_of_products(row, list_ref, count, left, right):
    def step(i, total):
        codes = [list_ref[row, i * 4 + u] for u in range(4)]
        a = jnp.concatenate([left[at_block(c >> SHIFT), :] for c in codes], axis=1)
        b = jnp.concatenate([right[at_block(c & MASK), :] for c in codes], axis=0)
        return total + jnp.dot(a, b, preferred_element_type=F32)

    return lax.fori_loop(0, (count + 3) >> 2, step, jnp.zeros((TILE, TILE), F32))


def vmem_for(blocks):
    return blocks * TILE * TILE * 2 + 6 * 1024 * 1024


def load_operands(left_srcs, right_srcs, left_offs, right_offs, left, right, sems):
    n = len(left_srcs)
    copies = fetch(left_srcs, left_offs, left, sems)
    copies += fetch(right_srcs, right_offs, right, sems.at[pl.ds(n, len(right_srcs))])
    zero = jnp.zeros((TILE, TILE), BF16)
    left[pl.ds(left.shape[0] - TILE, TILE), :] = zero
    right[pl.ds(right.shape[0] - TILE, TILE), :] = zero
    for copy in copies:
        copy.wait()


def square_blocks(lists, lefts, rights, cap):
    left_offs, left_total = offsets_of(lefts)
    right_offs, right_total = offsets_of(rights)
    nl, nr = len(lefts), len(rights)

    def kernel(list_ref, *refs):
        out, left, right, sems = refs[nl + nr :]
        load_operands(refs[:nl], refs[nl : nl + nr], left_offs, right_offs, left, right, sems)

        def step(o, carry):
            @pl.when(list_ref[o, 65] != 0)
            def _():
                total = sum_of_products(o, list_ref, list_ref[o, 64], left, right)
                out[at_block(jnp.minimum(list_ref[o, 66], cap - 1)), :] = total.astype(BF16)

            return carry

        lax.fori_loop(0, 32, step, 0)

    return pl.pallas_call(
        kernel,
        grid_spec=pltpu.PrefetchScalarGridSpec(
            num_scalar_prefetch=1, grid=(), in_specs=[ANY] * (nl + nr), out_specs=VMEM,
            scratch_shapes=[
                pltpu.VMEM(((left_total + 1) * TILE, TILE), BF16),
                pltpu.VMEM(((right_total + 1) * TILE, TILE), BF16),
                pltpu.SemaphoreType.DMA((nl + nr,)),
            ]),
        out_shape=blocks_of(cap),
        compiler_params=pltpu.CompilerParams(vmem_limit_bytes=vmem_for(left_total + right_total)),
        name="square_blocks",
    )(lists, *lefts, *rights)


def next_blocks(lists, lefts, rights, own):
    left_offs, left_total = offsets_of(lefts)
    right_offs, right_total = offsets_of(rights)
    nl, nr = len(lefts), len(rights)
    n_out = 2 if own else 1

    def kernel(list_ref, *refs):
        outs = refs[nl + nr : nl + nr + n_out]
        left, right, sems = refs[nl + nr + n_out :]
        load_operands(refs[:nl], refs[nl : nl + nr], left_offs, right_offs, left, right, sems)
        layer = lax.axis_index("layer")
        column = layer if own else 1 - layer

        def step(a, carry):
            o = column * 16 + a
            outs[0][at_block(a), :] = jnp.zeros((TILE, TILE), BF16)

            @pl.when(list_ref[o, 65] != 0)
            def _():
                total = sum_of_products(o, list_ref, list_ref[o, 64], left, right)
                start = left[at_block(list_ref[o, 66]), :].astype(F32)
                outs[0][at_block(a), :] = (1.5 * start - 0.5 * total).astype(BF16)

            return carry

        lax.fori_loop(0, 16, step, 0)

        if own:
            def place(t, carry):
                slot = list_ref[t, 67]

                @pl.when(slot >= 0)
                def _():
                    outs[1][at_block(t), :] = right[at_block(slot), :]

                @pl.when(slot < 0)
                def _():
                    outs[1][at_block(t), :] = jnp.zeros((TILE, TILE), BF16)

                return carry

            lax.fori_loop(0, 32, place, 0)

    return pl.pallas_call(
        kernel,
        grid_spec=pltpu.PrefetchScalarGridSpec(
            num_scalar_prefetch=1, grid=(), in_specs=[ANY] * (nl + nr), out_specs=[VMEM] * n_out,
            scratch_shapes=[
                pltpu.VMEM(((left_total + 1) * TILE, TILE), BF16),
                pltpu.VMEM(((right_total + 1) * TILE, TILE), BF16),
                pltpu.SemaphoreType.DMA((nl + nr,)),
            ]),
        out_shape=[blocks_of(16)] + ([blocks_of(32)] if own else []),
        compiler_params=pltpu.CompilerParams(vmem_limit_bytes=vmem_for(left_total + right_total)),
        name="next_own" if own else "next_sent",
    )(lists, *lefts, *rights)


def interleave(mine, other):
    def kernel(mine_ref, other_ref, out_ref):
        layer = lax.axis_index("layer")
        for a in range(16):
            out_ref[at_block(2 * a + layer), :] = mine_ref[pl.ds(a * TILE, TILE), :]
            out_ref[at_block(2 * a + 1 - layer), :] = other_ref[pl.ds(a * TILE, TILE), :]

    return pl.pallas_call(
        kernel,
        in_specs=[VMEM, VMEM],
        out_specs=VMEM,
        out_shape=blocks_of(32),
        compiler_params=pltpu.CompilerParams(vmem_limit_bytes=VMEM_LIMIT),
        name="interleave",
    )(mine, other)


def dot01(a, b):
    return jnp.dot(a.astype(F32).astype(BF16), b.astype(F32).astype(BF16), preferred_element_type=F32)


def dot01t(a, b):
    a, b = a.astype(F32).astype(BF16), b.astype(F32).astype(BF16)
    return lax.dot_general(a, b, (((1,), (1,)), ((), ())), preferred_element_type=F32)


def iota(shape, dim):
    return lax.broadcasted_iota(jnp.int32, shape, dim)


def along(value):
    return jnp.sum(value, axis=1, keepdims=True)


def zz(k):
    return (k & 31) >> 3


def yy(k):
    return (k & 7) >> 1


def tables(pattern, keep_square, keep_next):
    def kernel(pattern_ref, square_ref, next_ref, square_out, next_out, info_out):
        layer, row, col = lax.axis_index("layer"), lax.axis_index("row"), lax.axis_index("col")
        core, x = col & 1, row * 2 + layer
        z, y = zz(col), yy(col)
        pat = pattern_ref[...].astype(F32)
        keep = square_ref[...].astype(F32)
        keep2 = next_ref[...].astype(F32)
        i, k = iota((64, 64), 0), iota((64, 64), 1)
        parity = (i & 1) == (k & 1)
        even = (k & 1) == 0
        same_z, same_y = zz(i) == zz(k), yy(i) == yy(k)
        group = ((i & 31) == (k & 31)).astype(F32)

        g, g_k = iota((8, 64), 0), iota((8, 64), 1)
        owner = ((g_k >> 5) == (g >> 1)) & ((g_k & 1) == (g & 1))
        counts = dot01(owner, pat)
        ring = parity & ((even & same_z) | (~even & same_y))
        need = (
            jnp.max(dot01((g_k >> 5) == g, pat)),
            jnp.max(counts),
            jnp.max(dot01(counts, group)),
            jnp.max(dot01(counts, ring)),
            jnp.max(dot01(dot01(owner, keep), group)),
        )
        fits = need[0] <= TIERS[0][0]
        for a, b in zip(need[1:], TIERS[0][1:], strict=True):
            fits = fits & (a <= b)
        half, _, _, c2, c3 = [jnp.where(fits, a, b).astype(jnp.int32) for a, b in zip(*TIERS, strict=True)]

        o, kk = iota((32, 64), 0), iota((32, 64), 1)
        j = o >> 4
        p, q = iota((32, 32), 0), iota((32, 32), 1)
        same_j = (p >> 4) == (q >> 4)
        rowsel = (kk == row * 32 + 2 * (o & 15) + layer).astype(F32)
        colsel = (kk == j * 32 + col).astype(F32)
        rows = dot01(rowsel, pat)
        cols = dot01t(colsel, pat)
        kept = dot01t(colsel, keep)
        keep_mine = along(kept * rowsel)
        next_mine = along(dot01(rowsel, keep2) * colsel)

        column_count = dot01(same_j, rows)
        rank1 = dot01(same_j & (q < p), rows) + dot01(column_count, i == k - 32)
        before = parity & ((even & same_z & (yy(i) < yy(k))) | (~even & same_y & (zz(i) < zz(k))))
        offset = dot01(column_count, before)
        number = dot01(column_count, group)
        distance = jnp.where((kk & 1) == 0, zz(kk) - z, yy(kk) - y) & 3
        slot_left = distance * c2 + jnp.where((kk & 1) == core, 0, 4 * c2) + (offset + rank1).astype(jnp.int32)
        nothing_left = 8 * c2

        def place(x_other):
            e = (x_other - x) & 3
            return jnp.where(core == 0, (4 - e) & 3, e)

        rank0 = dot01(cols, ((i >> 5) == (k >> 5)) & (i < k))
        slot_right = place((kk >> 5) * 2 + j) * half + rank0.astype(jnp.int32)
        both = dot01((p & 15) == (q & 15), kept)
        first = dot01(q == (p & 15), kept)
        rank3 = dot01(both, parity & ((i >> 5) == (k >> 5)) & (i < k)) + jnp.where(j == 1, first, 0.0)
        slot_square = place((kk >> 5) * 2 + (kk & 1)) * c3 + rank3.astype(jnp.int32)

        lane = iota((32, 128), 1)

        def listed(hit, right, nothing_right):
            rank = dot01(hit, i < k)
            rank = jnp.where(hit > 0, rank, -1.0).astype(jnp.int32)
            code = ((slot_left << SHIFT) + right).astype(F32)
            number = along(hit)
            nothing = ((nothing_left << SHIFT) + nothing_right).astype(F32)

            def step(n, out):
                value = along(jnp.where(rank == n, code, 0.0))
                value = jnp.where(number > n.astype(F32), value, nothing)
                return jnp.where(lane == n, value, out)

            most = jnp.max(number).astype(jnp.int32)
            out = lax.fori_loop(0, most, step, jnp.full((32, 128), 1.0, F32) * nothing)
            return jnp.where(lane == 64, number, out)

        square = listed(rows * cols * keep_mine, slot_right, 4 * half)
        square = jnp.where(lane == 65, keep_mine, square)
        square = jnp.where(lane == 66, along(rank3 * rowsel), square)
        square_out[...] = square.astype(jnp.int32)

        following = listed(rows * kept * next_mine, slot_square, 4 * c3)
        following = jnp.where(lane == 65, next_mine, following)
        start = along(jnp.where(colsel * rows > 0, slot_left - nothing_left, 0).astype(F32))
        following = jnp.where(lane == 66, start + nothing_left.astype(F32), following)
        mine = (q == layer * 16).astype(F32)
        own_slot = dot01(mine, slot_square)
        own_kept = dot01(mine, kept)
        here = (kk == row * 32 + o).astype(F32)
        own = along(here * own_kept * (own_slot + 1.0)) - 1.0
        following = jnp.where(lane == 67, own, following)
        next_out[...] = following.astype(jnp.int32)

        target = jnp.where(core == 0, z * 8 + ((y + g) & 3) * 2, ((z + g) & 3) * 8 + y * 2 + 1)
        ring_sel = (g_k == target).astype(F32)
        ring_number = along(ring_sel * number[:8])
        ring_offset = along(ring_sel * offset[:8])
        lane8 = iota((8, 128), 1)
        info = jnp.where(lane8 == 1, ring_number, jnp.where(lane8 == 2, ring_offset, jnp.where(fits, 0.0, 1.0)))
        info_out[...] = info.astype(jnp.int32)

    return pl.pallas_call(
        kernel,
        in_specs=[VMEM] * 3,
        out_specs=[VMEM] * 3,
        out_shape=[jax.ShapeDtypeStruct((n, 128), jnp.int32) for n in (32, 32, 8)],
        name="tables",
    )(pattern, keep_square, keep_next)


def first_half(caps, values, pattern):
    own, sent = pack_column(pattern, values, caps[0], caps[1])
    return own, swap_layer(sent)


def packed(caps, values, pattern, own, received, square_list, next_list, info):
    half, part, c1, c2, c3 = caps
    if own.shape[0] != half * TILE or received.shape[0] != part * TILE:
        own, received = first_half(caps, values, pattern)

    with jax.named_scope("left_chunk"):
        chunk = pack_rows(pattern, values, received, c1)
        chunks = [chunk] + [shift_ring(chunk, -e, 0) for e in (1, 2, 3)]
    with jax.named_scope("right_columns"):
        carried = carry_x(after(own, chunk))
        *chunks, carried = lax.optimization_barrier((*chunks, carried))
        crossed, carried2 = carry_x(after(swap_core(own), chunks[1])), carry_x(carried)
    with jax.named_scope("left_rows"):
        ring = pack_ring(info, chunks, c2)
        ring3, ring1 = shift_ring(ring, 1, 1), shift_ring(ring, -1, 1)
        middle = c2 // 2 * TILE
        lo2, hi2 = shift_ring(ring3[:middle], 1, 1), shift_ring(ring1[middle:], -1, 1)
        rings = [ring, ring1, lo2, hi2, ring3]
        lefts = rings + [swap_core(v) for v in rings]
    with jax.named_scope("right_columns"):
        rights = [own, carried, carried2, swap_core(crossed)]
    with jax.named_scope("square"):
        squares = gather_x(square_blocks(square_list, lefts, rights, c3))
    with jax.named_scope("next"):
        (sent,) = next_blocks(next_list, lefts, squares, False)
        other = swap_layer(sent)
        mine, square = next_blocks(next_list, lefts, squares, True)
        next_sign = interleave(mine, other)
    return (square, next_sign)


def local(values, pattern, keep_square, keep_next):
    own, received = first_half(TIERS[0], values, pattern)
    square_list, next_list, info = tables(pattern, keep_square, keep_next)
    branches = [functools.partial(packed, caps) for caps in TIERS]
    return lax.switch(info[0, 0], branches, values, pattern, own, received, square_list, next_list, info)


def solution(mesh):
    return jax.shard_map(
        local,
        mesh=mesh,
        in_specs=(P("row", ("layer", "col")), P(), P(), P()),
        out_specs=(P("row", ("layer", "col")), P("row", ("layer", "col"))),
        check_vma=False,
    )
```

time: 178 us -> 121 us (0.68)
  between operations: 20 us -> 1.29 us
  other arithmetic: 11 us -> 0 us
  waiting for transfers between devices: 73.8 us -> 64.5 us
  matrix products: 8.39 us -> 0 us
  local copies, waits for them, and re-layouts: 7.86 us -> 0.6 us
  Pallas kernels: 36.3 us -> 30.5 us
  starting transfers between devices: 19.4 us -> 23.8 us
    ppermute x6, waiting for transfers between devices: 59.6 us -> 29.7 us  [carry_x(): lax.ppermute(value, ('layer', 'row', 'col'), [(i, target(i)) for i in ran...]
    ppermute x6 -> x7, waiting for transfers between devices: 10.1 us -> 24.2 us  [shift_ring(): return lax.ppermute(value, 'col', [(c, target(c)) for c in range(32)])]
    dot_general x19 -> x0, matrix products: 8.39 us -> none  [the longest x13 5.75 us: dot01(): return jnp.dot(a.astype(BF16), b.astype(BF16), preferred_element_type=F32)]
    reduce_sum x6 -> x0, other arithmetic: 4.61 us -> none  [the longest x2 3.06 us: choose(): jnp.sum(jnp.where(hit[None] & (dest[None] == slots), value[None], 0), axi...]
    cond x60 -> x0, local copies, waits for them, and re-layouts: 4.09 us -> none
    ppermute x2, waiting for transfers between devices: 4.04 us -> 7.56 us  [swap_layer(): return lax.ppermute(value, 'layer', [(0, 1), (1, 0)])]
    pallas_call x2, Pallas kernels: 17.1 us -> 13.7 us  [next_blocks(): pl.pallas_call(kernel, grid_spec=pltpu.PrefetchScalarGridSpec(num_scalar_...]
    ppermute x4 -> x9, waiting for transfers between devices: 0.01 us -> 3.01 us  [swap_core(): return lax.ppermute(value, 'col', [(c, c ^ 1) for c in range(32)])]
  transfers between devices with their start and end apart: 18 -> 24, of which waited for: 9 -> 13; matrix products, arithmetic and copies ran while one was open for 10% -> 0% of each run, Pallas kernels for 5% -> 10%
where the time goes in v2:
time: 121 us
  waiting for transfers between devices  64.5 us (53%)
  Pallas kernels  30.5 us (25%)
  starting transfers between devices  23.8 us (20%)
  between operations  1.29 us (1%)
    ppermute x6, waiting for transfers between devices, carry_x(): lax.ppermute(value, ('layer', 'row', 'col'), [(i, target(i)) for i in ran...  29.7 us
    ppermute x7, waiting for transfers between devices, shift_ring(): return lax.ppermute(value, 'col', [(c, target(c)) for c in range(32)])  24.2 us
    pallas_call x2, Pallas kernels, next_blocks(): pl.pallas_call(kernel, grid_spec=pltpu.PrefetchScalarGridSpec(num_scalar_...  13.7 us
    ppermute x7, starting transfers between devices, shift_ring(): return lax.ppermute(value, 'col', [(c, target(c)) for c in range(32)])  11.8 us
    ppermute x2, waiting for transfers between devices, swap_layer(): return lax.ppermute(value, 'layer', [(0, 1), (1, 0)])  7.56 us
    ppermute x6, starting transfers between devices, carry_x(): lax.ppermute(value, ('layer', 'row', 'col'), [(i, target(i)) for i in ran...  6.38 us
    pallas_call x1, Pallas kernels, square_blocks(): pl.pallas_call(kernel, grid_spec=pltpu.PrefetchScalarGridSpec(num_scalar_...  6.27 us
    pallas_call x1, Pallas kernels, tables(): pl.pallas_call(kernel, in_specs=[VMEM] * 3, out_specs=[VMEM] * 3, out_sha...  3.22 us
  transfers between devices with their start and end apart: 24, of which 13 were waited for; matrix products, arithmetic and copies ran while one was open for 0% of the time, Pallas kernels for 10%

profile of v2, /device:TPU:0, one launch (start us, length us, event | category | flops | bytes accessed | tf_op | source)
XLA Modules:
  0.0 120.8 jit_solution(14385271955527454957)
XLA Ops:
  0.6 3.1 %pack_column.3 = (bf16[2304,128]{1,0:T(8,128)(2,1)S(1)}, bf16[1408,128]{1,0:T(8,128)(2,1)S(1)}) custom-call(s32[64,64]{1,0:T(8,128)} %pattern_ref.3, bf16[4096,128]{1,0:T(8,128)(2,1)} %values_ref.1), custom_call_target="tpu_custom_call" | custom-call | tf_op jit(solution)/shard_map/pack_column/pallas_call | solution.py:118
  3.7 1.2 %collective-permute-start.47 = (bf16[1408,128]{1,0:T(8,128)(2,1)S(1)}, bf16[1408,128]{1,0:T(8,128)(2,1)S(1)}, u32[]{:S(2)}, u32[]{:S(2)}) collective-permute-start(bf16[1408,128]{1,0:T(8,128)(2,1)S(1)} %get-tuple-element.64), channel_id=1, source_target_pairs={{0,64},{64,0},{1,65},{65,1},{2,66},{66,2},{3,67},{67,3},{4,68},{68... | collective-permute-start | bytes 1081352 | tf_op jit(solution)/shard_map/ppermute | solution.py:55
  4.9 3.2 %tables.1 = (s32[32,128]{1,0:T(8,128)S(1)}, s32[32,128]{1,0:T(8,128)S(1)}, s32[8,128]{1,0:T(8,128)S(1)}) custom-call(s32[64,64]{1,0:T(8,128)} %pattern_ref.3, s32[64,64]{1,0:T(8,128)} %square_ref.1, s32[64,64]{1,0:T(8,128)} %next_ref.1), custom_call_target="tpu_custom_call" | custom-call | tf_op jit(solution)/shard_map/tables/pallas_call | solution.py:448
  9.3 4.3 %collective-permute-done.47 = bf16[1408,128]{1,0:T(8,128)(2,1)S(1)} collective-permute-done((bf16[1408,128]{1,0:T(8,128)(2,1)S(1)}, bf16[1408,128]{1,0:T(8,128)(2,1)S(1)}, u32[]{:S(2)}, u32[]{:S(2)}) %collective-permute-start.47) | collective-permute-done | bytes 360480 | tf_op jit(solution)/shard_map/ppermute | solution.py:55
  13.6 107.2 %conditional.1 = (bf16[4096,128]{1,0:T(8,128)(2,1)}, bf16[4096,128]{1,0:T(8,128)(2,1)}) conditional(s32[]{:T(128)} %bitcast, (s32[64,64]{1,0:T(8,128)}, bf16[4096,128]{1,0:T(8,128)(2,1)}, bf16[1408,128]{1,0:T(8,128)(2,1)S(1)}, bf16[2304,128]{1,0:T(8,128)(2,1)S(1)}, s32[8,128]{1,0:T(8,128)S(1)}, /*index=5*/s32[32,128]{1,0:T(8,128)S(1)}, ...), branch_computations={%region_0.0_spmd, %region_1.0_spmd} | conditional | bytes 293602368 | solution.py:497
  13.6 2.4 %pack_rows.2.refs_0_ = bf16[1792,128]{1,0:T(8,128)(2,1)S(1)} custom-call(s32[64,64]{1,0:T(8,128)} %get-tuple-element.26.pattern_ref, bf16[4096,128]{1,0:T(8,128)(2,1)} %get-tuple-element.27.values_ref, bf16[1408,128]{1,0:T(8,128)(2,1)S(1)} %get-tuple-element.28.received_ref), custom_call_target="tpu_custom_call" | custom-call | tf_op jit(solution)/shard_map/cond/branch_0_fun/left_chunk/pack_rows/pallas_call | solution.py:153
  16.1 1.8 %collective-permute-start.3 = (bf16[2304,128]{1,0:T(8,128)(2,1)S(1)}, bf16[2304,128]{1,0:T(8,128)(2,1)S(1)}, u32[]{:S(2)}, u32[]{:S(2)}) collective-permute-start(bf16[2304,128]{1,0:T(8,128)(2,1)S(1)} %get-tuple-element.30.refs_10_), channel_id=1, source_target_pairs={{0,64},{1,97},{2,66},{3,99},{4,68},{5,101},{6,70},{7,103},{8,72},{... | collective-permute-start | bytes 1769480 | tf_op jit(solution)/shard_map/cond/branch_0_fun/right_columns/ppermute | solution.py:37
  18.2 2.8 %collective-permute-start = (bf16[1792,128]{1,0:T(8,128)(2,1)S(1)}, bf16[1792,128]{1,0:T(8,128)(2,1)S(1)}, u32[]{:S(2)}, u32[]{:S(2)}) collective-permute-start(bf16[1792,128]{1,0:T(8,128)(2,1)S(1)} %pack_rows.2.refs_0_), channel_id=1, source_target_pairs={{0,6},{1,25},{2,0},{3,27},{4,2},{5,29},{6,4},{7,31},{8,14},{9,1},{... | collective-permute-start | bytes 1376264 | tf_op jit(solution)/shard_map/cond/branch_0_fun/left_chunk/ppermute | solution.py:28
  21.5 1.0 collective-permute-start.2
  22.6 9.4 %collective-permute-done.refs_1_ = bf16[1792,128]{1,0:T(8,128)(2,1)S(1)} collective-permute-done((bf16[1792,128]{1,0:T(8,128)(2,1)S(1)}, bf16[1792,128]{1,0:T(8,128)(2,1)S(1)}, u32[]{:S(2)}, u32[]{:S(2)}) %collective-permute-start) | collective-permute-done | bytes 458784 | tf_op jit(solution)/shard_map/cond/branch_0_fun/left_chunk/ppermute | solution.py:28
  32.0 4.0 %collective-permute-done.2.refs_3_ = bf16[1792,128]{1,0:T(8,128)(2,1)S(1)} collective-permute-done((bf16[1792,128]{1,0:T(8,128)(2,1)S(1)}, bf16[1792,128]{1,0:T(8,128)(2,1)S(1)}, u32[]{:S(2)}, u32[]{:S(2)}) %collective-permute-start.2) | collective-permute-done | bytes 458784 | tf_op jit(solution)/shard_map/cond/branch_0_fun/left_chunk/ppermute | solution.py:28
  36.8 1.8 %collective-permute-start.5 = (bf16[4864,128]{1,0:T(8,128)(2,1)S(1)}, bf16[4864,128]{1,0:T(8,128)(2,1)S(1)}, u32[]{:S(2)}, u32[]{:S(2)}) collective-permute-start(bf16[4864,128]{1,0:T(8,128)(2,1)S(1)} %pack_ring.2.refs_0_), channel_id=1, source_target_pairs={{0,8},{1,3},{2,10},{3,5},{4,12},{5,7},{6,14},{7,1},{8,16},{9,11},{... | collective-permute-start | bytes 3735560 | tf_op jit(solution)/shard_map/cond/branch_0_fun/left_rows/ppermute | solution.py:28
  38.6 2.4 %collective-permute-start.4 = (bf16[4864,128]{1,0:T(8,128)(2,1)S(1)}, bf16[4864,128]{1,0:T(8,128)(2,1)S(1)}, u32[]{:S(2)}, u32[]{:S(2)}) collective-permute-start(bf16[4864,128]{1,0:T(8,128)(2,1)S(1)} %pack_ring.2.refs_0_), channel_id=1, source_target_pairs={{0,24},{1,7},{2,26},{3,1},{4,28},{5,3},{6,30},{7,5},{8,0},{9,15},{... | collective-permute-start | bytes 3735560 | tf_op jit(solution)/shard_map/cond/branch_0_fun/left_rows/ppermute | solution.py:28
  41.0 1.1 collective-permute-start.15
  42.1 1.0 collective-permute-start.13
  43.1 9.0 %collective-permute-done.15 = bf16[2304,128]{1,0:T(8,128)(2,1)S(1)} collective-permute-done((bf16[2304,128]{1,0:T(8,128)(2,1)S(1)}, bf16[2304,128]{1,0:T(8,128)(2,1)S(1)}, u32[]{:S(2)}, u32[]{:S(2)}) %collective-permute-start.15) | collective-permute-done | bytes 589856 | tf_op jit(solution)/shard_map/cond/branch_0_fun/right_columns/ppermute | solution.py:37
  52.6 3.2 %collective-permute-done.5.refs_4_ = bf16[4864,128]{1,0:T(8,128)(2,1)S(1)} collective-permute-done((bf16[4864,128]{1,0:T(8,128)(2,1)S(1)}, bf16[4864,128]{1,0:T(8,128)(2,1)S(1)}, u32[]{:S(2)}, u32[]{:S(2)}) %collective-permute-start.5) | collective-permute-done | bytes 1245216 | tf_op jit(solution)/shard_map/cond/branch_0_fun/left_rows/ppermute | solution.py:28
  56.0 3.3 %collective-permute-start.7 = (bf16[2432,128]{1,0:T(8,128)(2,1)S(1)}, bf16[2432,128]{1,0:T(8,128)(2,1)S(1)}, u32[]{:S(2)}, u32[]{:S(2)}) collective-permute-start(bf16[2432,128]{1,0:T(8,128)(2,1)S(1)} %slice.17), channel_id=1, source_target_pairs={{0,24},{1,7},{2,26},{3,1},{4,28},{5,3},{6,30},{7,5},{8,0},{9,15},{... | collective-permute-start | bytes 1867784 | tf_op jit(solution)/shard_map/cond/branch_0_fun/left_rows/ppermute | solution.py:28
  59.8 7.6 %collective-permute-done.6.refs_2_ = bf16[2432,128]{1,0:T(8,128)(2,1)S(1)} collective-permute-done((bf16[2432,128]{1,0:T(8,128)(2,1)S(1)}, bf16[2432,128]{1,0:T(8,128)(2,1)S(1)}, u32[]{:S(2)}, u32[]{:S(2)}) %collective-permute-start.6) | collective-permute-done | bytes 622624 | tf_op jit(solution)/shard_map/cond/branch_0_fun/left_rows/ppermute | solution.py:28
  67.8 1.5 %collective-permute-done.10.refs_7_ = bf16[2432,128]{1,0:T(8,128)(2,1)S(1)} collective-permute-done((bf16[2432,128]{1,0:T(8,128)(2,1)S(1)}, bf16[2432,128]{1,0:T(8,128)(2,1)S(1)}, u32[]{:S(2)}, u32[]{:S(2)}) %collective-permute-start.10) | collective-permute-done | bytes 622624 | tf_op jit(solution)/shard_map/cond/branch_0_fun/left_rows/ppermute | solution.py:51
  70.3 6.3 %square_blocks.2.refs_10_ = bf16[2304,128]{1,0:T(8,128)(2,1)S(1)} custom-call(s32[32,128]{1,0:T(8,128)S(1)} %get-tuple-element.35.list_ref, bf16[4864,128]{1,0:T(8,128)(2,1)S(1)} %pack_ring.2.refs_0_, bf16[4864,128]{1,0:T(8,128)(2,1)S(1)} %collective-permute-done.4.refs_1_, bf16[2432,128]{1,0:T(8,128)(2,1)S(1)} %collective-permute-done.6.refs_2_, ...), custom_call_target="tpu_custom_call" | custom-call | tf_op jit(solution)/shard_map/cond/branch_0_fun/square/square_blocks/pallas_call | solution.py:228
  76.6 1.2 collective-permute-start.19
  77.8 1.1 collective-permute-start.17
  79.4 1.4 %collective-permute-start.20 = (bf16[2304,128]{1,0:T(8,128)(2,1)S(1)}, bf16[2304,128]{1,0:T(8,128)(2,1)S(1)}, u32[]{:S(2)}, u32[]{:S(2)}) collective-permute-start(bf16[2304,128]{1,0:T(8,128)(2,1)S(1)} %collective-permute-done.19), channel_id=1, source_target_pairs={{0,64},{1,97},{2,66},{3,99},{4,68},{5,101},{6,70},{7,103},{8,72},{... | collective-permute-start | bytes 1769480 | tf_op jit(solution)/shard_map/cond/branch_0_fun/square/ppermute | solution.py:37
  80.7 8.1 %collective-permute-done.17.refs_11_ = bf16[2304,128]{1,0:T(8,128)(2,1)S(1)} collective-permute-done((bf16[2304,128]{1,0:T(8,128)(2,1)S(1)}, bf16[2304,128]{1,0:T(8,128)(2,1)S(1)}, u32[]{:S(2)}, u32[]{:S(2)}) %collective-permute-start.17) | collective-permute-done | bytes 589856 | tf_op jit(solution)/shard_map/cond/branch_0_fun/square/ppermute | solution.py:37
  88.9 6.3 %collective-permute-done.20 = bf16[2304,128]{1,0:T(8,128)(2,1)S(1)} collective-permute-done((bf16[2304,128]{1,0:T(8,128)(2,1)S(1)}, bf16[2304,128]{1,0:T(8,128)(2,1)S(1)}, u32[]{:S(2)}, u32[]{:S(2)}) %collective-permute-start.20) | collective-permute-done | bytes 589856 | tf_op jit(solution)/shard_map/cond/branch_0_fun/square/ppermute | solution.py:37
  95.2 6.3 %collective-permute-done.18.refs_12_ = bf16[2304,128]{1,0:T(8,128)(2,1)S(1)} collective-permute-done((bf16[2304,128]{1,0:T(8,128)(2,1)S(1)}, bf16[2304,128]{1,0:T(8,128)(2,1)S(1)}, u32[]{:S(2)}, u32[]{:S(2)}) %collective-permute-start.18) | collective-permute-done | bytes 589856 | tf_op jit(solution)/shard_map/cond/branch_0_fun/square/ppermute | solution.py:37
  101.5 5.3 %next_sent.2 = bf16[2048,128]{1,0:T(8,128)(2,1)S(1)} custom-call(s32[32,128]{1,0:T(8,128)S(1)} %get-tuple-element.24.list_ref, bf16[4864,128]{1,0:T(8,128)(2,1)S(1)} %pack_ring.2.refs_0_, bf16[4864,128]{1,0:T(8,128)(2,1)S(1)} %collective-permute-done.4.refs_1_, bf16[2432,128]{1,0:T(8,128)(2,1)S(1)} %collective-permute-done.6.refs_2_, ...), custom_call_target="tpu_custom_call" | custom-call | tf_op jit(solution)/shard_map/cond/branch_0_fun/next/next_sent/pallas_call | solution.py:286
  106.8 1.3 %collective-permute-start.22 = (bf16[2048,128]{1,0:T(8,128)(2,1)S(1)}, bf16[2048,128]{1,0:T(8,128)(2,1)S(1)}, u32[]{:S(2)}, u32[]{:S(2)}) collective-permute-start(bf16[2048,128]{1,0:T(8,128)(2,1)S(1)} %next_sent.2), channel_id=1, source_target_pairs={{0,64},{64,0},{1,65},{65,1},{2,66},{66,2},{3,67},{67,3},{4,68},{68... | collective-permute-start | bytes 1572872 | tf_op jit(solution)/shard_map/cond/branch_0_fun/next/ppermute | solution.py:55
  108.1 8.4 %next_own.2 = (bf16[2048,128]{1,0:T(8,128)(2,1)S(1)}, bf16[4096,128]{1,0:T(8,128)(2,1)}) custom-call(s32[32,128]{1,0:T(8,128)S(1)} %get-tuple-element.24.list_ref, bf16[4864,128]{1,0:T(8,128)(2,1)S(1)} %pack_ring.2.refs_0_, bf16[4864,128]{1,0:T(8,128)(2,1)S(1)} %collective-permute-done.4.refs_1_, bf16[2432,128]{1,0:T(8,128)(2,1)S(1)} %collective-permute-done.6.refs_2_, ...), custom_call_target="tpu_custom_call" | custom-call | tf_op jit(solution)/shard_map/cond/branch_0_fun/next/next_own/pallas_call | solution.py:286
  116.5 3.3 %collective-permute-done.22.other_ref = bf16[2048,128]{1,0:T(8,128)(2,1)S(1)} collective-permute-done((bf16[2048,128]{1,0:T(8,128)(2,1)S(1)}, bf16[2048,128]{1,0:T(8,128)(2,1)S(1)}, u32[]{:S(2)}, u32[]{:S(2)}) %collective-permute-start.22) | collective-permute-done | bytes 524320 | tf_op jit(solution)/shard_map/cond/branch_0_fun/next/ppermute | solution.py:55
  119.8 1.0 interleave.2
  (28 shorter events, 5.3 us)
Async XLA Ops:
  3.7 9.9 %collective-permute-start.47 = (bf16[1408,128]{1,0:T(8,128)(2,1)S(1)}, bf16[1408,128]{1,0:T(8,128)(2,1)S(1)}, u32[]{:S(2)}, u32[]{:S(2)}) collective-permute-start(bf16[1408,128]{1,0:T(8,128)(2,1)S(1)} %get-tuple-element.64), channel_id=1, source_target_pairs={{0,64},{64,0},{1,65},{65,1},{2,66},{66,2},{3,67},{67,3},{4,68},{68... | collective-permute-start | bytes 1081352 | tf_op jit(solution)/shard_map/ppermute | solution.py:55
  16.1 19.9 %collective-permute-start.3 = (bf16[2304,128]{1,0:T(8,128)(2,1)S(1)}, bf16[2304,128]{1,0:T(8,128)(2,1)S(1)}, u32[]{:S(2)}, u32[]{:S(2)}) collective-permute-start(bf16[2304,128]{1,0:T(8,128)(2,1)S(1)} %get-tuple-element.30.refs_10_), channel_id=1, source_target_pairs={{0,64},{1,97},{2,66},{3,99},{4,68},{5,101},{6,70},{7,103},{8,72},{... | collective-permute-start | bytes 1769480 | tf_op jit(solution)/shard_map/cond/branch_0_fun/right_columns/ppermute | solution.py:37
  17.9 23.1 %collective-permute-start.14 = (bf16[2304,128]{1,0:T(8,128)(2,1)S(1)}, bf16[2304,128]{1,0:T(8,128)(2,1)S(1)}, u32[]{:S(2)}, u32[]{:S(2)}) collective-permute-start(bf16[2304,128]{1,0:T(8,128)(2,1)S(1)} %get-tuple-element.30.refs_10_), channel_id=1, source_target_pairs={{0,1},{1,0},{2,3},{3,2},{4,5},{5,4},{6,7},{7,6},{8,9},{9,8},{10,11... | collective-permute-start | bytes 1769480 | tf_op jit(solution)/shard_map/cond/branch_0_fun/right_columns/ppermute | solution.py:51
  18.2 13.7 %collective-permute-start = (bf16[1792,128]{1,0:T(8,128)(2,1)S(1)}, bf16[1792,128]{1,0:T(8,128)(2,1)S(1)}, u32[]{:S(2)}, u32[]{:S(2)}) collective-permute-start(bf16[1792,128]{1,0:T(8,128)(2,1)S(1)} %pack_rows.2.refs_0_), channel_id=1, source_target_pairs={{0,6},{1,25},{2,0},{3,27},{4,2},{5,29},{6,4},{7,31},{8,14},{9,1},{... | collective-permute-start | bytes 1376264 | tf_op jit(solution)/shard_map/cond/branch_0_fun/left_chunk/ppermute | solution.py:28
  21.1 10.9 %collective-permute-start.1 = (bf16[1792,128]{1,0:T(8,128)(2,1)S(1)}, bf16[1792,128]{1,0:T(8,128)(2,1)S(1)}, u32[]{:S(2)}, u32[]{:S(2)}) collective-permute-start(bf16[1792,128]{1,0:T(8,128)(2,1)S(1)} %pack_rows.2.refs_0_), channel_id=1, source_target_pairs={{0,4},{1,17},{2,6},{3,19},{4,0},{5,21},{6,2},{7,23},{8,12},{9,25},... | collective-permute-start | bytes 1376264 | tf_op jit(solution)/shard_map/cond/branch_0_fun/left_chunk/ppermute | solution.py:28
  21.5 14.5 %collective-permute-start.2 = (bf16[1792,128]{1,0:T(8,128)(2,1)S(1)}, bf16[1792,128]{1,0:T(8,128)(2,1)S(1)}, u32[]{:S(2)}, u32[]{:S(2)}) collective-permute-start(bf16[1792,128]{1,0:T(8,128)(2,1)S(1)} %pack_rows.2.refs_0_), channel_id=1, source_target_pairs={{0,2},{1,9},{2,4},{3,11},{4,6},{5,13},{6,0},{7,15},{8,10},{9,17},{... | collective-permute-start | bytes 1376264 | tf_op jit(solution)/shard_map/cond/branch_0_fun/left_chunk/ppermute | solution.py:28
  36.8 19.0 %collective-permute-start.5 = (bf16[4864,128]{1,0:T(8,128)(2,1)S(1)}, bf16[4864,128]{1,0:T(8,128)(2,1)S(1)}, u32[]{:S(2)}, u32[]{:S(2)}) collective-permute-start(bf16[4864,128]{1,0:T(8,128)(2,1)S(1)} %pack_ring.2.refs_0_), channel_id=1, source_target_pairs={{0,8},{1,3},{2,10},{3,5},{4,12},{5,7},{6,14},{7,1},{8,16},{9,11},{... | collective-permute-start | bytes 3735560 | tf_op jit(solution)/shard_map/cond/branch_0_fun/left_rows/ppermute | solution.py:28
  38.6 17.3 %collective-permute-start.4 = (bf16[4864,128]{1,0:T(8,128)(2,1)S(1)}, bf16[4864,128]{1,0:T(8,128)(2,1)S(1)}, u32[]{:S(2)}, u32[]{:S(2)}) collective-permute-start(bf16[4864,128]{1,0:T(8,128)(2,1)S(1)} %pack_ring.2.refs_0_), channel_id=1, source_target_pairs={{0,24},{1,7},{2,26},{3,1},{4,28},{5,3},{6,30},{7,5},{8,0},{9,15},{... | collective-permute-start | bytes 3735560 | tf_op jit(solution)/shard_map/cond/branch_0_fun/left_rows/ppermute | solution.py:28
  41.0 11.1 %collective-permute-start.15 = (bf16[2304,128]{1,0:T(8,128)(2,1)S(1)}, bf16[2304,128]{1,0:T(8,128)(2,1)S(1)}, u32[]{:S(2)}, u32[]{:S(2)}) collective-permute-start(bf16[2304,128]{1,0:T(8,128)(2,1)S(1)} %collective-permute-done.14), channel_id=1, source_target_pairs={{0,64},{1,97},{2,66},{3,99},{4,68},{5,101},{6,70},{7,103},{8,72},{... | collective-permute-start | bytes 1769480 | tf_op jit(solution)/shard_map/cond/branch_0_fun/right_columns/ppermute | solution.py:37
  42.1 17.1 %collective-permute-start.13 = (bf16[2304,128]{1,0:T(8,128)(2,1)S(1)}, bf16[2304,128]{1,0:T(8,128)(2,1)S(1)}, u32[]{:S(2)}, u32[]{:S(2)}) collective-permute-start(bf16[2304,128]{1,0:T(8,128)(2,1)S(1)} %collective-permute-done.3.refs_11_), channel_id=1, source_target_pairs={{0,64},{1,97},{2,66},{3,99},{4,68},{5,101},{6,70},{7,103},{8,72},{... | collective-permute-start | bytes 1769480 | tf_op jit(solution)/shard_map/cond/branch_0_fun/right_columns/ppermute | solution.py:37
  52.1 7.2 %collective-permute-start.16 = (bf16[2304,128]{1,0:T(8,128)(2,1)S(1)}, bf16[2304,128]{1,0:T(8,128)(2,1)S(1)}, u32[]{:S(2)}, u32[]{:S(2)}) collective-permute-start(bf16[2304,128]{1,0:T(8,128)(2,1)S(1)} %collective-permute-done.15), channel_id=1, source_target_pairs={{0,1},{1,0},{2,3},{3,2},{4,5},{5,4},{6,7},{7,6},{8,9},{9,8},{10,11... | collective-permute-start | bytes 1769480 | tf_op jit(solution)/shard_map/cond/branch_0_fun/right_columns/ppermute | solution.py:51
  52.1 15.8 %collective-permute-start.8 = (bf16[4864,128]{1,0:T(8,128)(2,1)S(1)}, bf16[4864,128]{1,0:T(8,128)(2,1)S(1)}, u32[]{:S(2)}, u32[]{:S(2)}) collective-permute-start(bf16[4864,128]{1,0:T(8,128)(2,1)S(1)} %pack_ring.2.refs_0_), channel_id=1, source_target_pairs={{0,1},{1,0},{2,3},{3,2},{4,5},{5,4},{6,7},{7,6},{8,9},{9,8},{10,11... | collective-permute-start | bytes 3735560 | tf_op jit(solution)/shard_map/cond/branch_0_fun/left_rows/ppermute | solution.py:51
  55.8 11.5 %collective-permute-start.6 = (bf16[2432,128]{1,0:T(8,128)(2,1)S(1)}, bf16[2432,128]{1,0:T(8,128)(2,1)S(1)}, u32[]{:S(2)}, u32[]{:S(2)}) collective-permute-start(bf16[2432,128]{1,0:T(8,128)(2,1)S(1)} %slice.16), channel_id=1, source_target_pairs={{0,8},{1,3},{2,10},{3,5},{4,12},{5,7},{6,14},{7,1},{8,16},{9,11},{... | collective-permute-start | bytes 1867784 | tf_op jit(solution)/shard_map/cond/branch_0_fun/left_rows/ppermute | solution.py:28
  56.0 11.4 %collective-permute-start.7 = (bf16[2432,128]{1,0:T(8,128)(2,1)S(1)}, bf16[2432,128]{1,0:T(8,128)(2,1)S(1)}, u32[]{:S(2)}, u32[]{:S(2)}) collective-permute-start(bf16[2432,128]{1,0:T(8,128)(2,1)S(1)} %slice.17), channel_id=1, source_target_pairs={{0,24},{1,7},{2,26},{3,1},{4,28},{5,3},{6,30},{7,5},{8,0},{9,15},{... | collective-permute-start | bytes 1867784 | tf_op jit(solution)/shard_map/cond/branch_0_fun/left_rows/ppermute | solution.py:28
  59.2 11.0 %collective-permute-start.9 = (bf16[4864,128]{1,0:T(8,128)(2,1)S(1)}, bf16[4864,128]{1,0:T(8,128)(2,1)S(1)}, u32[]{:S(2)}, u32[]{:S(2)}) collective-permute-start(bf16[4864,128]{1,0:T(8,128)(2,1)S(1)} %collective-permute-done.4.refs_1_), channel_id=1, source_target_pairs={{0,1},{1,0},{2,3},{3,2},{4,5},{5,4},{6,7},{7,6},{8,9},{9,8},{10,11... | collective-permute-start | bytes 3735560 | tf_op jit(solution)/shard_map/cond/branch_0_fun/left_rows/ppermute | solution.py:51
  59.2 11.0 %collective-permute-start.12 = (bf16[4864,128]{1,0:T(8,128)(2,1)S(1)}, bf16[4864,128]{1,0:T(8,128)(2,1)S(1)}, u32[]{:S(2)}, u32[]{:S(2)}) collective-permute-start(bf16[4864,128]{1,0:T(8,128)(2,1)S(1)} %collective-permute-done.5.refs_4_), channel_id=1, source_target_pairs={{0,1},{1,0},{2,3},{3,2},{4,5},{5,4},{6,7},{7,6},{8,9},{9,8},{10,11... | collective-permute-start | bytes 3735560 | tf_op jit(solution)/shard_map/cond/branch_0_fun/left_rows/ppermute | solution.py:51
  67.3 2.1 %collective-permute-start.10 = (bf16[2432,128]{1,0:T(8,128)(2,1)S(1)}, bf16[2432,128]{1,0:T(8,128)(2,1)S(1)}, u32[]{:S(2)}, u32[]{:S(2)}) collective-permute-start(bf16[2432,128]{1,0:T(8,128)(2,1)S(1)} %collective-permute-done.6.refs_2_), channel_id=1, source_target_pairs={{0,1},{1,0},{2,3},{3,2},{4,5},{5,4},{6,7},{7,6},{8,9},{9,8},{10,11... | collective-permute-start | bytes 1867784 | tf_op jit(solution)/shard_map/cond/branch_0_fun/left_rows/ppermute | solution.py:51
  67.3 2.9 %collective-permute-start.11 = (bf16[2432,128]{1,0:T(8,128)(2,1)S(1)}, bf16[2432,128]{1,0:T(8,128)(2,1)S(1)}, u32[]{:S(2)}, u32[]{:S(2)}) collective-permute-start(bf16[2432,128]{1,0:T(8,128)(2,1)S(1)} %collective-permute-done.7.refs_3_), channel_id=1, source_target_pairs={{0,1},{1,0},{2,3},{3,2},{4,5},{5,4},{6,7},{7,6},{8,9},{9,8},{10,11... | collective-permute-start | bytes 1867784 | tf_op jit(solution)/shard_map/cond/branch_0_fun/left_rows/ppermute | solution.py:51
  76.6 2.8 %collective-permute-start.19 = (bf16[2304,128]{1,0:T(8,128)(2,1)S(1)}, bf16[2304,128]{1,0:T(8,128)(2,1)S(1)}, u32[]{:S(2)}, u32[]{:S(2)}) collective-permute-start(bf16[2304,128]{1,0:T(8,128)(2,1)S(1)} %square_blocks.2.refs_10_), channel_id=1, source_target_pairs={{0,1},{1,0},{2,3},{3,2},{4,5},{5,4},{6,7},{7,6},{8,9},{9,8},{10,11... | collective-permute-start | bytes 1769480 | tf_op jit(solution)/shard_map/cond/branch_0_fun/square/ppermute | solution.py:51
  77.8 11.1 %collective-permute-start.17 = (bf16[2304,128]{1,0:T(8,128)(2,1)S(1)}, bf16[2304,128]{1,0:T(8,128)(2,1)S(1)}, u32[]{:S(2)}, u32[]{:S(2)}) collective-permute-start(bf16[2304,128]{1,0:T(8,128)(2,1)S(1)} %square_blocks.2.refs_10_), channel_id=1, source_target_pairs={{0,64},{1,97},{2,66},{3,99},{4,68},{5,101},{6,70},{7,103},{8,72},{... | collective-permute-start | bytes 1769480 | tf_op jit(solution)/shard_map/cond/branch_0_fun/square/ppermute | solution.py:37
  79.4 15.8 %collective-permute-start.20 = (bf16[2304,128]{1,0:T(8,128)(2,1)S(1)}, bf16[2304,128]{1,0:T(8,128)(2,1)S(1)}, u32[]{:S(2)}, u32[]{:S(2)}) collective-permute-start(bf16[2304,128]{1,0:T(8,128)(2,1)S(1)} %collective-permute-done.19), channel_id=1, source_target_pairs={{0,64},{1,97},{2,66},{3,99},{4,68},{5,101},{6,70},{7,103},{8,72},{... | collective-permute-start | bytes 1769480 | tf_op jit(solution)/shard_map/cond/branch_0_fun/square/ppermute | solution.py:37
  88.9 12.6 %collective-permute-start.18 = (bf16[2304,128]{1,0:T(8,128)(2,1)S(1)}, bf16[2304,128]{1,0:T(8,128)(2,1)S(1)}, u32[]{:S(2)}, u32[]{:S(2)}) collective-permute-start(bf16[2304,128]{1,0:T(8,128)(2,1)S(1)} %collective-permute-done.17.refs_11_), channel_id=1, source_target_pairs={{0,64},{1,97},{2,66},{3,99},{4,68},{5,101},{6,70},{7,103},{8,72},{... | collective-permute-start | bytes 1769480 | tf_op jit(solution)/shard_map/cond/branch_0_fun/square/ppermute | solution.py:37
  95.2 6.3 %collective-permute-start.21 = (bf16[2304,128]{1,0:T(8,128)(2,1)S(1)}, bf16[2304,128]{1,0:T(8,128)(2,1)S(1)}, u32[]{:S(2)}, u32[]{:S(2)}) collective-permute-start(bf16[2304,128]{1,0:T(8,128)(2,1)S(1)} %collective-permute-done.20), channel_id=1, source_target_pairs={{0,1},{1,0},{2,3},{3,2},{4,5},{5,4},{6,7},{7,6},{8,9},{9,8},{10,11... | collective-permute-start | bytes 1769480 | tf_op jit(solution)/shard_map/cond/branch_0_fun/square/ppermute | solution.py:51
  106.8 13.0 %collective-permute-start.22 = (bf16[2048,128]{1,0:T(8,128)(2,1)S(1)}, bf16[2048,128]{1,0:T(8,128)(2,1)S(1)}, u32[]{:S(2)}, u32[]{:S(2)}) collective-permute-start(bf16[2048,128]{1,0:T(8,128)(2,1)S(1)} %next_sent.2), channel_id=1, source_target_pairs={{0,64},{64,0},{1,65},{65,1},{2,66},{66,2},{3,67},{67,3},{4,68},{68... | collective-permute-start | bytes 1572872 | tf_op jit(solution)/shard_map/cond/branch_0_fun/next/ppermute | solution.py:55

commit v3 on v2

--- a/solution.py
+++ b/solution.py
@@ -12,7 +12,7 @@
 MASK = (1 << SHIFT) - 1
 BF16 = jnp.bfloat16
 F32 = jnp.float32
-TIERS = ((18, 11, 14, 38, 18), (32, 16, 32, 128, 32))
+TIERS = ((18, 11, 12, 34, 16), (18, 11, 14, 38, 18), (32, 16, 32, 128, 32))
 VMEM_LIMIT = 20 * 1024 * 1024
 
 
@@ -161,20 +161,24 @@
 
 
 def pack_ring(info, chunks, cap):
+    cut = chunks[2].shape[0] // TILE
+    parts = ((0, 0), (1, 0), (2, 0), (2, cut), (3, 0))
+
     def kernel(info_ref, *refs):
-        out = refs[4]
-        for e in range(4):
-            def copy(n, carry, e=e):
-                place = jnp.minimum(info_ref[e, 2] + n, cap - 1)
-                out[at_block(place), :] = refs[e][at_block(n), :]
+        out = refs[5]
+        for (e, skip), ref in zip(parts, refs[:5], strict=True):
+            first, number = info_ref[e, 2] + skip, info_ref[e, 1] - skip
+
+            def copy(n, carry, ref=ref, first=first):
+                out[at_block(jnp.minimum(first + n, cap - 1)), :] = ref[at_block(n), :]
                 return carry
 
-            lax.fori_loop(0, info_ref[e, 1], copy, 0)
+            lax.fori_loop(0, jnp.minimum(number, ref.shape[0] // TILE), copy, 0)
 
     return pl.pallas_call(
         kernel,
         grid_spec=pltpu.PrefetchScalarGridSpec(
-            num_scalar_prefetch=1, grid=(), in_specs=[VMEM] * 4, out_specs=VMEM),
+            num_scalar_prefetch=1, grid=(), in_specs=[VMEM] * 5, out_specs=VMEM),
         out_shape=blocks_of(cap),
         compiler_params=pltpu.CompilerParams(vmem_limit_bytes=VMEM_LIMIT),
         name="pack_ring",
@@ -200,10 +204,16 @@
     copies = fetch(left_srcs, left_offs, left, sems)
     copies += fetch(right_srcs, right_offs, right, sems.at[pl.ds(n, len(right_srcs))])
     zero = jnp.zeros((TILE, TILE), BF16)
-    left[pl.ds(left.shape[0] - TILE, TILE), :] = zero
+    if left is not None:
+        left[pl.ds(left.shape[0] - TILE, TILE), :] = zero
     right[pl.ds(right.shape[0] - TILE, TILE), :] = zero
     for copy in copies:
         copy.wait()
+
+
+def store_of(blocks):
+    shape = (blocks * TILE, TILE)
+    return pltpu.VMEM(shape, BF16) if blocks <= 400 else jax.ShapeDtypeStruct(shape, BF16)
 
 
 def square_blocks(lists, lefts, rights, cap):
@@ -228,28 +238,26 @@
     return pl.pallas_call(
         kernel,
         grid_spec=pltpu.PrefetchScalarGridSpec(
-            num_scalar_prefetch=1, grid=(), in_specs=[ANY] * (nl + nr), out_specs=VMEM,
+            num_scalar_prefetch=1, grid=(), in_specs=[ANY] * (nl + nr), out_specs=[VMEM, VMEM],
             scratch_shapes=[
-                pltpu.VMEM(((left_total + 1) * TILE, TILE), BF16),
                 pltpu.VMEM(((right_total + 1) * TILE, TILE), BF16),
                 pltpu.SemaphoreType.DMA((nl + nr,)),
             ]),
-        out_shape=blocks_of(cap),
+        out_shape=[blocks_of(cap), store_of(left_total + 1)],
         compiler_params=pltpu.CompilerParams(vmem_limit_bytes=vmem_for(left_total + right_total)),
         name="square_blocks",
     )(lists, *lefts, *rights)
 
 
-def next_blocks(lists, lefts, rights, own):
-    left_offs, left_total = offsets_of(lefts)
+def next_blocks(lists, left, rights, own):
     right_offs, right_total = offsets_of(rights)
-    nl, nr = len(lefts), len(rights)
+    nr = len(rights)
     n_out = 2 if own else 1
 
     def kernel(list_ref, *refs):
-        outs = refs[nl + nr : nl + nr + n_out]
-        left, right, sems = refs[nl + nr + n_out :]
-        load_operands(refs[:nl], refs[nl : nl + nr], left_offs, right_offs, left, right, sems)
+        left, outs = refs[0], refs[1 + nr : 1 + nr + n_out]
+        right, sems = refs[1 + nr + n_out :]
+        load_operands((), refs[1 : 1 + nr], (), right_offs, None, right, sems)
         layer = lax.axis_index("layer")
         column = layer if own else 1 - layer
 
@@ -286,16 +294,15 @@
     return pl.pallas_call(
         kernel,
         grid_spec=pltpu.PrefetchScalarGridSpec(
-            num_scalar_prefetch=1, grid=(), in_specs=[ANY] * (nl + nr), out_specs=[VMEM] * n_out,
+            num_scalar_prefetch=1, grid=(), in_specs=[VMEM] + [ANY] * nr, out_specs=[VMEM] * n_out,
             scratch_shapes=[
-                pltpu.VMEM(((left_total + 1) * TILE, TILE), BF16),
                 pltpu.VMEM(((right_total + 1) * TILE, TILE), BF16),
-                pltpu.SemaphoreType.DMA((nl + nr,)),
+                pltpu.SemaphoreType.DMA((nr,)),
             ]),
         out_shape=[blocks_of(16)] + ([blocks_of(32)] if own else []),
-        compiler_params=pltpu.CompilerParams(vmem_limit_bytes=vmem_for(left_total + right_total)),
+        compiler_params=pltpu.CompilerParams(vmem_limit_bytes=vmem_for(right_total + left.shape[0] // TILE)),
         name="next_own" if own else "next_sent",
-    )(lists, *lefts, *rights)
+    )(lists, left, *rights)
 
 
 def interleave(mine, other):
@@ -365,10 +372,13 @@
             jnp.max(dot01(counts, ring)),
             jnp.max(dot01(dot01(owner, keep), group)),
         )
-        fits = need[0] <= TIERS[0][0]
-        for a, b in zip(need[1:], TIERS[0][1:], strict=True):
-            fits = fits & (a <= b)
-        half, _, _, c2, c3 = [jnp.where(fits, a, b).astype(jnp.int32) for a, b in zip(*TIERS, strict=True)]
+        fits = [functools.reduce(jnp.logical_and, [a <= b for a, b in zip(need, t, strict=True)]) for t in TIERS[:2]]
+
+        def by_tier(a, b, c):
+            return jnp.where(fits[0], a, jnp.where(fits[1], b, c)).astype(jnp.int32)
+
+        half, _, _, c2, c3 = [by_tier(*caps) for caps in zip(*TIERS, strict=True)]
+        tier = by_tier(0, 1, 2)
 
         o, kk = iota((32, 64), 0), iota((32, 64), 1)
         j = o >> 4
@@ -442,7 +452,7 @@
         ring_number = along(ring_sel * number[:8])
         ring_offset = along(ring_sel * offset[:8])
         lane8 = iota((8, 128), 1)
-        info = jnp.where(lane8 == 1, ring_number, jnp.where(lane8 == 2, ring_offset, jnp.where(fits, 0.0, 1.0)))
+        info = jnp.where(lane8 == 1, ring_number, jnp.where(lane8 == 2, ring_offset, tier.astype(F32)))
         info_out[...] = info.astype(jnp.int32)
 
     return pl.pallas_call(
@@ -466,11 +476,13 @@
 
     with jax.named_scope("left_chunk"):
         chunk = pack_rows(pattern, values, received, c1)
-        chunks = [chunk] + [shift_ring(chunk, -e, 0) for e in (1, 2, 3)]
+        far, near = shift_ring(chunk, 1, 0), shift_ring(chunk, -1, 0)
+        cut = c1 // 2 * TILE
+        chunks = [chunk, near, shift_ring(far[:cut], 1, 0), shift_ring(near[cut:], -1, 0), far]
     with jax.named_scope("right_columns"):
         carried = carry_x(after(own, chunk))
         *chunks, carried = lax.optimization_barrier((*chunks, carried))
-        crossed, carried2 = carry_x(after(swap_core(own), chunks[1])), carry_x(carried)
+        crossed, carried2 = carry_x(after(swap_core(own), near)), carry_x(carried)
     with jax.named_scope("left_rows"):
         ring = pack_ring(info, chunks, c2)
         ring3, ring1 = shift_ring(ring, 1, 1), shift_ring(ring, -1, 1)
@@ -481,11 +493,12 @@
     with jax.named_scope("right_columns"):
         rights = [own, carried, carried2, swap_core(crossed)]
     with jax.named_scope("square"):
-        squares = gather_x(square_blocks(square_list, lefts, rights, c3))
+        kept, left = square_blocks(square_list, lefts, rights, c3)
+        squares = gather_x(kept)
     with jax.named_scope("next"):
-        (sent,) = next_blocks(next_list, lefts, squares, False)
+        (sent,) = next_blocks(next_list, left, squares, False)
         other = swap_layer(sent)
-        mine, square = next_blocks(next_list, lefts, squares, True)
+        mine, square = next_blocks(next_list, left, squares, True)
         next_sign = interleave(mine, other)
     return (square, next_sign)
 
@@ -493,8 +506,13 @@
 def local(values, pattern, keep_square, keep_next):
     own, received = first_half(TIERS[0], values, pattern)
     square_list, next_list, info = tables(pattern, keep_square, keep_next)
-    branches = [functools.partial(packed, caps) for caps in TIERS]
-    return lax.switch(info[0, 0], branches, values, pattern, own, received, square_list, next_list, info)
+    tier = info[0, 0]
+    first, second, last = [functools.partial(packed, caps) for caps in TIERS]
+
+    def others(*args):
+        return lax.cond(tier == 1, second, last, *args)
+
+    return lax.cond(tier == 0, first, others, values, pattern, own, received, square_list, next_list, info)
 
 
 def solution(mesh):

time: 121 us -> 111 us (0.917); the launches traced: 121 us -> 108 us
  Pallas kernels: 30.5 us -> 23.5 us
  waiting for transfers between devices: 64.5 us -> 58.3 us
    ppermute x6, waiting for transfers between devices: 29.7 us -> 19.3 us  [carry_x(): lax.ppermute(value, ('layer', 'row', 'col'), [(i, target(i)) for i in ran...]
    pallas_call x2, Pallas kernels: 13.7 us -> 7.75 us  [next_blocks(): pl.pallas_call(kernel, grid_spec=pltpu.PrefetchScalarGridSpec(num_scalar_...]
    ppermute x2, waiting for transfers between devices: 7.56 us -> 11.1 us  [swap_layer(): return lax.ppermute(value, 'layer', [(0, 1), (1, 0)])]
    ppermute x7 -> x8, starting transfers between devices: 11.8 us -> 14.8 us  [shift_ring(): return lax.ppermute(value, 'col', [(c, target(c)) for c in range(32)])]
    ppermute x9, starting transfers between devices: 3.08 us -> 1.12 us  [swap_core(): return lax.ppermute(value, 'col', [(c, c ^ 1) for c in range(32)])]
    ppermute x7 -> x8, waiting for transfers between devices: 24.2 us -> 24.8 us  [shift_ring(): return lax.ppermute(value, 'col', [(c, target(c)) for c in range(32)])]
  transfers between devices with their start and end apart: 24 -> 25, of which waited for: 13 -> 13; matrix products, arithmetic and copies ran while one was open for 0% -> 1% of each run, Pallas kernels for 10% -> 8%
where the time goes in v3:
time: 111 us; the launch traced here: 108 us
  waiting for transfers between devices  58.3 us (53%)
  starting transfers between devices  23.7 us (21%)
  Pallas kernels  23.5 us (21%)
  local copies, waits for them, and re-layouts  1.59 us (1%)
  between operations  1.3 us (1%)
    ppermute x8, waiting for transfers between devices, shift_ring(): return lax.ppermute(value, 'col', [(c, target(c)) for c in range(32)])  24.8 us
    ppermute x6, waiting for transfers between devices, carry_x(): lax.ppermute(value, ('layer', 'row', 'col'), [(i, target(i)) for i in ran...  19.3 us
    ppermute x8, starting transfers between devices, shift_ring(): return lax.ppermute(value, 'col', [(c, target(c)) for c in range(32)])  14.8 us
    ppermute x2, waiting for transfers between devices, swap_layer(): return lax.ppermute(value, 'layer', [(0, 1), (1, 0)])  11.1 us
    pallas_call x2, Pallas kernels, next_blocks(): pl.pallas_call(kernel, grid_spec=pltpu.PrefetchScalarGridSpec(num_scalar_...  7.75 us
    ppermute x6, starting transfers between devices, carry_x(): lax.ppermute(value, ('layer', 'row', 'col'), [(i, target(i)) for i in ran...  6.32 us
    pallas_call x1, Pallas kernels, square_blocks(): pl.pallas_call(kernel, grid_spec=pltpu.PrefetchScalarGridSpec(num_scalar_...  6.1 us
    pallas_call x1, Pallas kernels, tables(): pl.pallas_call(kernel, in_specs=[VMEM] * 3, out_specs=[VMEM] * 3, out_sha...  3.3 us
  transfers between devices with their start and end apart: 25, of which 13 were waited for; matrix products, arithmetic and copies ran while one was open for 1% of the time, Pallas kernels for 8%

profile of v3, /device:TPU:0, one launch (start us, length us, event | category | flops | bytes accessed | tf_op | source)
XLA Modules:
  0.0 108.4 jit_solution(15852240327255724236)
XLA Ops:
  0.6 3.1 %pack_column.3 = (bf16[2304,128]{1,0:T(8,128)(2,1)S(1)}, bf16[1408,128]{1,0:T(8,128)(2,1)S(1)}) custom-call(s32[64,64]{1,0:T(8,128)} %pattern_ref.3, bf16[4096,128]{1,0:T(8,128)(2,1)} %values_ref.1), custom_call_target="tpu_custom_call" | custom-call | tf_op jit(solution)/shard_map/pack_column/pallas_call | solution.py:118
  3.7 1.3 %collective-permute-start.73 = (bf16[1408,128]{1,0:T(8,128)(2,1)S(1)}, bf16[1408,128]{1,0:T(8,128)(2,1)S(1)}, u32[]{:S(2)}, u32[]{:S(2)}) collective-permute-start(bf16[1408,128]{1,0:T(8,128)(2,1)S(1)} %get-tuple-element.129), channel_id=1, source_target_pairs={{0,64},{64,0},{1,65},{65,1},{2,66},{66,2},{3,67},{67,3},{4,68},{68... | collective-permute-start | bytes 1081352 | tf_op jit(solution)/shard_map/ppermute | solution.py:55
  5.0 3.3 %tables.1 = (s32[32,128]{1,0:T(8,128)S(1)}, s32[32,128]{1,0:T(8,128)S(1)}, s32[8,128]{1,0:T(8,128)S(1)}) custom-call(s32[64,64]{1,0:T(8,128)} %pattern_ref.3, s32[64,64]{1,0:T(8,128)} %square_ref.1, s32[64,64]{1,0:T(8,128)} %next_ref.1), custom_call_target="tpu_custom_call" | custom-call | tf_op jit(solution)/shard_map/tables/pallas_call | solution.py:458
  9.5 3.7 %collective-permute-done.73 = bf16[1408,128]{1,0:T(8,128)(2,1)S(1)} collective-permute-done((bf16[1408,128]{1,0:T(8,128)(2,1)S(1)}, bf16[1408,128]{1,0:T(8,128)(2,1)S(1)}, u32[]{:S(2)}, u32[]{:S(2)}) %collective-permute-start.73) | collective-permute-done | bytes 360480 | tf_op jit(solution)/shard_map/ppermute | solution.py:55
  13.2 94.3 %conditional.2 = ((bf16[4096,128]{1,0:T(8,128)(2,1)}, bf16[4096,128]{1,0:T(8,128)(2,1)S(1)})) conditional(s32[]{:T(128)} %convert_element_type.6, (s32[]{:T(128)}, s32[64,64]{1,0:T(8,128)}, bf16[4096,128]{1,0:T(8,128)(2,1)}, s32[8,128]{1,0:T(8,128)S(1)}, s32[32,128]{1,0:T(8,128)S(1)}, /*index=5*/s32[32,128]{1,0:T(8,128)S(1)}, ...), branch_computations={%region_0.0_spmd, %region_3.0_spmd} | conditional | flops 2 | bytes 295699616 | solution.py:515
  13.2 2.4 %pack_rows.5.refs_0_ = bf16[1536,128]{1,0:T(8,128)(2,1)S(1)} custom-call(s32[64,64]{1,0:T(8,128)} %get-tuple-element.103.pattern_ref, bf16[4096,128]{1,0:T(8,128)(2,1)} %get-tuple-element.104.values_ref, bf16[1408,128]{1,0:T(8,128)(2,1)S(1)} %get-tuple-element.105.received_ref), custom_call_target="tpu_custom_call" | custom-call | tf_op jit(solution)/shard_map/cond/branch_1_fun/left_chunk/pack_rows/pallas_call | solution.py:153
  15.6 2.5 %collective-permute-start.50 = (bf16[1536,128]{1,0:T(8,128)(2,1)S(1)}, bf16[1536,128]{1,0:T(8,128)(2,1)S(1)}, u32[]{:S(2)}, u32[]{:S(2)}) collective-permute-start(bf16[1536,128]{1,0:T(8,128)(2,1)S(1)} %pack_rows.5.refs_0_), channel_id=1, source_target_pairs={{0,2},{1,9},{2,4},{3,11},{4,6},{5,13},{6,0},{7,15},{8,10},{9,17},{... | collective-permute-start | bytes 1179656 | tf_op jit(solution)/shard_map/cond/branch_1_fun/left_chunk/ppermute | solution.py:28
  18.1 1.4 %collective-permute-start.49 = (bf16[1536,128]{1,0:T(8,128)(2,1)S(1)}, bf16[1536,128]{1,0:T(8,128)(2,1)S(1)}, u32[]{:S(2)}, u32[]{:S(2)}) collective-permute-start(bf16[1536,128]{1,0:T(8,128)(2,1)S(1)} %pack_rows.5.refs_0_), channel_id=1, source_target_pairs={{0,6},{1,25},{2,0},{3,27},{4,2},{5,29},{6,4},{7,31},{8,14},{9,1},{... | collective-permute-start | bytes 1179656 | tf_op jit(solution)/shard_map/cond/branch_1_fun/left_chunk/ppermute | solution.py:28
  19.5 1.2 %collective-permute-start.53 = (bf16[2304,128]{1,0:T(8,128)(2,1)S(1)}, bf16[2304,128]{1,0:T(8,128)(2,1)S(1)}, u32[]{:S(2)}, u32[]{:S(2)}) collective-permute-start(bf16[2304,128]{1,0:T(8,128)(2,1)S(1)} %get-tuple-element.107.refs_10_), channel_id=1, source_target_pairs={{0,64},{1,97},{2,66},{3,99},{4,68},{5,101},{6,70},{7,103},{8,72},{... | collective-permute-start | bytes 1769480 | tf_op jit(solution)/shard_map/cond/branch_1_fun/right_columns/ppermute | solution.py:37
  20.7 4.5 %collective-permute-done.50.refs_4_ = bf16[1536,128]{1,0:T(8,128)(2,1)S(1)} collective-permute-done((bf16[1536,128]{1,0:T(8,128)(2,1)S(1)}, bf16[1536,128]{1,0:T(8,128)(2,1)S(1)}, u32[]{:S(2)}, u32[]{:S(2)}) %collective-permute-start.50) | collective-permute-done | bytes 393248 | tf_op jit(solution)/shard_map/cond/branch_1_fun/left_chunk/ppermute | solution.py:28
  26.0 2.6 %collective-permute-start.52 = (bf16[768,128]{1,0:T(8,128)(2,1)S(1)}, bf16[768,128]{1,0:T(8,128)(2,1)S(1)}, u32[]{:S(2)}, u32[]{:S(2)}) collective-permute-start(bf16[768,128]{1,0:T(8,128)(2,1)S(1)} %slice.49), channel_id=1, source_target_pairs={{0,6},{1,25},{2,0},{3,27},{4,2},{5,29},{6,4},{7,31},{8,14},{9,1},{... | collective-permute-start | bytes 589832 | tf_op jit(solution)/shard_map/cond/branch_1_fun/left_chunk/ppermute | solution.py:28
  28.6 3.5 %collective-permute-done.51.refs_2_ = bf16[768,128]{1,0:T(8,128)(2,1)S(1)} collective-permute-done((bf16[768,128]{1,0:T(8,128)(2,1)S(1)}, bf16[768,128]{1,0:T(8,128)(2,1)S(1)}, u32[]{:S(2)}, u32[]{:S(2)}) %collective-permute-start.51) | collective-permute-done | bytes 196640 | tf_op jit(solution)/shard_map/cond/branch_1_fun/left_chunk/ppermute | solution.py:28
  33.0 2.3 %collective-permute-start.55 = (bf16[4352,128]{1,0:T(8,128)(2,1)S(1)}, bf16[4352,128]{1,0:T(8,128)(2,1)S(1)}, u32[]{:S(2)}, u32[]{:S(2)}) collective-permute-start(bf16[4352,128]{1,0:T(8,128)(2,1)S(1)} %pack_ring.5.refs_0_), channel_id=1, source_target_pairs={{0,8},{1,3},{2,10},{3,5},{4,12},{5,7},{6,14},{7,1},{8,16},{9,11},{... | collective-permute-start | bytes 3342344 | tf_op jit(solution)/shard_map/cond/branch_1_fun/left_rows/ppermute | solution.py:28
  35.3 1.9 %collective-permute-start.54 = (bf16[4352,128]{1,0:T(8,128)(2,1)S(1)}, bf16[4352,128]{1,0:T(8,128)(2,1)S(1)}, u32[]{:S(2)}, u32[]{:S(2)}) collective-permute-start(bf16[4352,128]{1,0:T(8,128)(2,1)S(1)} %pack_ring.5.refs_0_), channel_id=1, source_target_pairs={{0,24},{1,7},{2,26},{3,1},{4,28},{5,3},{6,30},{7,5},{8,0},{9,15},{... | collective-permute-start | bytes 3342344 | tf_op jit(solution)/shard_map/cond/branch_1_fun/left_rows/ppermute | solution.py:28
  37.2 1.6 %collective-permute-start.63 = (bf16[2304,128]{1,0:T(8,128)(2,1)S(1)}, bf16[2304,128]{1,0:T(8,128)(2,1)S(1)}, u32[]{:S(2)}, u32[]{:S(2)}) collective-permute-start(bf16[2304,128]{1,0:T(8,128)(2,1)S(1)} %collective-permute-done.53.refs_11_), channel_id=1, source_target_pairs={{0,64},{1,97},{2,66},{3,99},{4,68},{5,101},{6,70},{7,103},{8,72},{... | collective-permute-start | bytes 1769480 | tf_op jit(solution)/shard_map/cond/branch_1_fun/right_columns/ppermute | solution.py:37
  38.8 1.4 %collective-permute-start.65 = (bf16[2304,128]{1,0:T(8,128)(2,1)S(1)}, bf16[2304,128]{1,0:T(8,128)(2,1)S(1)}, u32[]{:S(2)}, u32[]{:S(2)}) collective-permute-start(bf16[2304,128]{1,0:T(8,128)(2,1)S(1)} %collective-permute-done.64), channel_id=1, source_target_pairs={{0,64},{1,97},{2,66},{3,99},{4,68},{5,101},{6,70},{7,103},{8,72},{... | collective-permute-start | bytes 1769480 | tf_op jit(solution)/shard_map/cond/branch_1_fun/right_columns/ppermute | solution.py:37
  40.2 10.4 %collective-permute-done.55.refs_4_ = bf16[4352,128]{1,0:T(8,128)(2,1)S(1)} collective-permute-done((bf16[4352,128]{1,0:T(8,128)(2,1)S(1)}, bf16[4352,128]{1,0:T(8,128)(2,1)S(1)}, u32[]{:S(2)}, u32[]{:S(2)}) %collective-permute-start.55) | collective-permute-done | bytes 1114144 | tf_op jit(solution)/shard_map/cond/branch_1_fun/left_rows/ppermute | solution.py:28
  50.9 3.1 %collective-permute-start.57 = (bf16[2176,128]{1,0:T(8,128)(2,1)S(1)}, bf16[2176,128]{1,0:T(8,128)(2,1)S(1)}, u32[]{:S(2)}, u32[]{:S(2)}) collective-permute-start(bf16[2176,128]{1,0:T(8,128)(2,1)S(1)} %slice.51), channel_id=1, source_target_pairs={{0,24},{1,7},{2,26},{3,1},{4,28},{5,3},{6,30},{7,5},{8,0},{9,15},{... | collective-permute-start | bytes 1671176 | tf_op jit(solution)/shard_map/cond/branch_1_fun/left_rows/ppermute | solution.py:28
  55.1 6.3 %collective-permute-done.56.refs_2_ = bf16[2176,128]{1,0:T(8,128)(2,1)S(1)} collective-permute-done((bf16[2176,128]{1,0:T(8,128)(2,1)S(1)}, bf16[2176,128]{1,0:T(8,128)(2,1)S(1)}, u32[]{:S(2)}, u32[]{:S(2)}) %collective-permute-start.56) | collective-permute-done | bytes 557088 | tf_op jit(solution)/shard_map/cond/branch_1_fun/left_rows/ppermute | solution.py:28
  61.9 1.4 %collective-permute-done.60.refs_7_ = bf16[2176,128]{1,0:T(8,128)(2,1)S(1)} collective-permute-done((bf16[2176,128]{1,0:T(8,128)(2,1)S(1)}, bf16[2176,128]{1,0:T(8,128)(2,1)S(1)}, u32[]{:S(2)}, u32[]{:S(2)}) %collective-permute-start.60) | collective-permute-done | bytes 557088 | tf_op jit(solution)/shard_map/cond/branch_1_fun/left_rows/ppermute | solution.py:51
  63.4 0.8 collective-permute-done.61.refs_8_
  64.2 6.1 %square_blocks.5 = (bf16[2048,128]{1,0:T(8,128)(2,1)S(1)}, bf16[34944,128]{1,0:T(8,128)(2,1)S(1)}) custom-call(s32[32,128]{1,0:T(8,128)S(1)} %get-tuple-element.101.list_ref, bf16[4352,128]{1,0:T(8,128)(2,1)S(1)} %pack_ring.5.refs_0_, bf16[4352,128]{1,0:T(8,128)(2,1)S(1)} %collective-permute-done.54.refs_1_, ...), custom_call_target="tpu_custom_call" | custom-call | tf_op jit(solution)/shard_map/cond/branch_1_fun/square/square_blocks/pallas_call | solution.py:238
  70.4 1.1 %collective-permute-start.67 = (bf16[2048,128]{1,0:T(8,128)(2,1)S(1)}, bf16[2048,128]{1,0:T(8,128)(2,1)S(1)}, u32[]{:S(2)}, u32[]{:S(2)}) collective-permute-start(bf16[2048,128]{1,0:T(8,128)(2,1)S(1)} %get-tuple-element.116.refs_1_), channel_id=1, source_target_pairs={{0,64},{1,97},{2,66},{3,99},{4,68},{5,101},{6,70},{7,103},{8,72},{... | collective-permute-start | bytes 1572872 | tf_op jit(solution)/shard_map/cond/branch_1_fun/square/ppermute | solution.py:37
  71.5 0.8 collective-permute-done.69
  72.3 1.0 collective-permute-start.70
  73.3 7.5 %collective-permute-done.67.refs_2_ = bf16[2048,128]{1,0:T(8,128)(2,1)S(1)} collective-permute-done((bf16[2048,128]{1,0:T(8,128)(2,1)S(1)}, bf16[2048,128]{1,0:T(8,128)(2,1)S(1)}, u32[]{:S(2)}, u32[]{:S(2)}) %collective-permute-start.67) | collective-permute-done | bytes 524320 | tf_op jit(solution)/shard_map/cond/branch_1_fun/square/ppermute | solution.py:37
  80.8 5.6 %collective-permute-done.70 = bf16[2048,128]{1,0:T(8,128)(2,1)S(1)} collective-permute-done((bf16[2048,128]{1,0:T(8,128)(2,1)S(1)}, bf16[2048,128]{1,0:T(8,128)(2,1)S(1)}, u32[]{:S(2)}, u32[]{:S(2)}) %collective-permute-start.70) | collective-permute-done | bytes 524320 | tf_op jit(solution)/shard_map/cond/branch_1_fun/square/ppermute | solution.py:37
  86.5 5.6 %collective-permute-done.68.refs_3_ = bf16[2048,128]{1,0:T(8,128)(2,1)S(1)} collective-permute-done((bf16[2048,128]{1,0:T(8,128)(2,1)S(1)}, bf16[2048,128]{1,0:T(8,128)(2,1)S(1)}, u32[]{:S(2)}, u32[]{:S(2)}) %collective-permute-start.68) | collective-permute-done | bytes 524320 | tf_op jit(solution)/shard_map/cond/branch_1_fun/square/ppermute | solution.py:37
  92.1 3.2 %next_sent.5 = bf16[2048,128]{1,0:T(8,128)(2,1)S(1)} custom-call(s32[32,128]{1,0:T(8,128)S(1)} %get-tuple-element.100.list_ref, bf16[34944,128]{1,0:T(8,128)(2,1)S(1)} %get-tuple-element.115.refs_0_, bf16[2048,128]{1,0:T(8,128)(2,1)S(1)} %get-tuple-element.116.refs_1_, bf16[2048,128]{1,0:T(8,128)(2,1)S(1)} %collective-permute-done.67.refs_2_, ...), custom_call_target="tpu_custom_call" | custom-call | tf_op jit(solution)/shard_map/cond/branch_1_fun/next/next_sent/pallas_call | solution.py:294
  95.4 4.5 %next_own.5 = (bf16[2048,128]{1,0:T(8,128)(2,1)S(1)}, bf16[4096,128]{1,0:T(8,128)(2,1)}) custom-call(s32[32,128]{1,0:T(8,128)S(1)} %get-tuple-element.100.list_ref, bf16[34944,128]{1,0:T(8,128)(2,1)S(1)} %get-tuple-element.115.refs_0_, bf16[2048,128]{1,0:T(8,128)(2,1)S(1)} %get-tuple-element.116.refs_1_, ...), custom_call_target="tpu_custom_call" | custom-call | tf_op jit(solution)/shard_map/cond/branch_1_fun/next/next_own/pallas_call | solution.py:294
  99.9 7.5 %collective-permute-done.72.other_ref = bf16[2048,128]{1,0:T(8,128)(2,1)S(1)} collective-permute-done((bf16[2048,128]{1,0:T(8,128)(2,1)S(1)}, bf16[2048,128]{1,0:T(8,128)(2,1)S(1)}, u32[]{:S(2)}, u32[]{:S(2)}) %collective-permute-start.72) | collective-permute-done | bytes 524320 | tf_op jit(solution)/shard_map/cond/branch_1_fun/next/ppermute | solution.py:55
  107.5 1.0 copy-done.7
  (34 shorter events, 4.3 us)
Async XLA Ops:
  3.7 9.5 %collective-permute-start.73 = (bf16[1408,128]{1,0:T(8,128)(2,1)S(1)}, bf16[1408,128]{1,0:T(8,128)(2,1)S(1)}, u32[]{:S(2)}, u32[]{:S(2)}) collective-permute-start(bf16[1408,128]{1,0:T(8,128)(2,1)S(1)} %get-tuple-element.129), channel_id=1, source_target_pairs={{0,64},{64,0},{1,65},{65,1},{2,66},{66,2},{3,67},{67,3},{4,68},{68... | collective-permute-start | bytes 1081352 | tf_op jit(solution)/shard_map/ppermute | solution.py:55
  15.6 9.6 %collective-permute-start.50 = (bf16[1536,128]{1,0:T(8,128)(2,1)S(1)}, bf16[1536,128]{1,0:T(8,128)(2,1)S(1)}, u32[]{:S(2)}, u32[]{:S(2)}) collective-permute-start(bf16[1536,128]{1,0:T(8,128)(2,1)S(1)} %pack_rows.5.refs_0_), channel_id=1, source_target_pairs={{0,2},{1,9},{2,4},{3,11},{4,6},{5,13},{6,0},{7,15},{8,10},{9,17},{... | collective-permute-start | bytes 1179656 | tf_op jit(solution)/shard_map/cond/branch_1_fun/left_chunk/ppermute | solution.py:28
  18.1 7.9 %collective-permute-start.49 = (bf16[1536,128]{1,0:T(8,128)(2,1)S(1)}, bf16[1536,128]{1,0:T(8,128)(2,1)S(1)}, u32[]{:S(2)}, u32[]{:S(2)}) collective-permute-start(bf16[1536,128]{1,0:T(8,128)(2,1)S(1)} %pack_rows.5.refs_0_), channel_id=1, source_target_pairs={{0,6},{1,25},{2,0},{3,27},{4,2},{5,29},{6,4},{7,31},{8,14},{9,1},{... | collective-permute-start | bytes 1179656 | tf_op jit(solution)/shard_map/cond/branch_1_fun/left_chunk/ppermute | solution.py:28
  19.5 12.6 %collective-permute-start.53 = (bf16[2304,128]{1,0:T(8,128)(2,1)S(1)}, bf16[2304,128]{1,0:T(8,128)(2,1)S(1)}, u32[]{:S(2)}, u32[]{:S(2)}) collective-permute-start(bf16[2304,128]{1,0:T(8,128)(2,1)S(1)} %get-tuple-element.107.refs_10_), channel_id=1, source_target_pairs={{0,64},{1,97},{2,66},{3,99},{4,68},{5,101},{6,70},{7,103},{8,72},{... | collective-permute-start | bytes 1769480 | tf_op jit(solution)/shard_map/cond/branch_1_fun/right_columns/ppermute | solution.py:37
  25.2 6.9 %collective-permute-start.51 = (bf16[768,128]{1,0:T(8,128)(2,1)S(1)}, bf16[768,128]{1,0:T(8,128)(2,1)S(1)}, u32[]{:S(2)}, u32[]{:S(2)}) collective-permute-start(bf16[768,128]{1,0:T(8,128)(2,1)S(1)} %slice.48), channel_id=1, source_target_pairs={{0,2},{1,9},{2,4},{3,11},{4,6},{5,13},{6,0},{7,15},{8,10},{9,17},{... | collective-permute-start | bytes 589832 | tf_op jit(solution)/shard_map/cond/branch_1_fun/left_chunk/ppermute | solution.py:28
  26.0 6.2 %collective-permute-start.52 = (bf16[768,128]{1,0:T(8,128)(2,1)S(1)}, bf16[768,128]{1,0:T(8,128)(2,1)S(1)}, u32[]{:S(2)}, u32[]{:S(2)}) collective-permute-start(bf16[768,128]{1,0:T(8,128)(2,1)S(1)} %slice.49), channel_id=1, source_target_pairs={{0,6},{1,25},{2,0},{3,27},{4,2},{5,29},{6,4},{7,31},{8,14},{9,1},{... | collective-permute-start | bytes 589832 | tf_op jit(solution)/shard_map/cond/branch_1_fun/left_chunk/ppermute | solution.py:28
  28.6 10.2 %collective-permute-start.64 = (bf16[2304,128]{1,0:T(8,128)(2,1)S(1)}, bf16[2304,128]{1,0:T(8,128)(2,1)S(1)}, u32[]{:S(2)}, u32[]{:S(2)}) collective-permute-start(bf16[2304,128]{1,0:T(8,128)(2,1)S(1)} %get-tuple-element.107.refs_10_), channel_id=1, source_target_pairs={{0,1},{1,0},{2,3},{3,2},{4,5},{5,4},{6,7},{7,6},{8,9},{9,8},{10,11... | collective-permute-start | bytes 1769480 | tf_op jit(solution)/shard_map/cond/branch_1_fun/right_columns/ppermute | solution.py:51
  33.0 17.6 %collective-permute-start.55 = (bf16[4352,128]{1,0:T(8,128)(2,1)S(1)}, bf16[4352,128]{1,0:T(8,128)(2,1)S(1)}, u32[]{:S(2)}, u32[]{:S(2)}) collective-permute-start(bf16[4352,128]{1,0:T(8,128)(2,1)S(1)} %pack_ring.5.refs_0_), channel_id=1, source_target_pairs={{0,8},{1,3},{2,10},{3,5},{4,12},{5,7},{6,14},{7,1},{8,16},{9,11},{... | collective-permute-start | bytes 3342344 | tf_op jit(solution)/shard_map/cond/branch_1_fun/left_rows/ppermute | solution.py:28
  35.3 15.6 %collective-permute-start.54 = (bf16[4352,128]{1,0:T(8,128)(2,1)S(1)}, bf16[4352,128]{1,0:T(8,128)(2,1)S(1)}, u32[]{:S(2)}, u32[]{:S(2)}) collective-permute-start(bf16[4352,128]{1,0:T(8,128)(2,1)S(1)} %pack_ring.5.refs_0_), channel_id=1, source_target_pairs={{0,24},{1,7},{2,26},{3,1},{4,28},{5,3},{6,30},{7,5},{8,0},{9,15},{... | collective-permute-start | bytes 3342344 | tf_op jit(solution)/shard_map/cond/branch_1_fun/left_rows/ppermute | solution.py:28
  37.2 17.4 %collective-permute-start.58 = (bf16[4352,128]{1,0:T(8,128)(2,1)S(1)}, bf16[4352,128]{1,0:T(8,128)(2,1)S(1)}, u32[]{:S(2)}, u32[]{:S(2)}) collective-permute-start(bf16[4352,128]{1,0:T(8,128)(2,1)S(1)} %pack_ring.5.refs_0_), channel_id=1, source_target_pairs={{0,1},{1,0},{2,3},{3,2},{4,5},{5,4},{6,7},{7,6},{8,9},{9,8},{10,11... | collective-permute-start | bytes 3342344 | tf_op jit(solution)/shard_map/cond/branch_1_fun/left_rows/ppermute | solution.py:51
  37.2 16.9 %collective-permute-start.63 = (bf16[2304,128]{1,0:T(8,128)(2,1)S(1)}, bf16[2304,128]{1,0:T(8,128)(2,1)S(1)}, u32[]{:S(2)}, u32[]{:S(2)}) collective-permute-start(bf16[2304,128]{1,0:T(8,128)(2,1)S(1)} %collective-permute-done.53.refs_11_), channel_id=1, source_target_pairs={{0,64},{1,97},{2,66},{3,99},{4,68},{5,101},{6,70},{7,103},{8,72},{... | collective-permute-start | bytes 1769480 | tf_op jit(solution)/shard_map/cond/branch_1_fun/right_columns/ppermute | solution.py:37
  38.8 15.8 %collective-permute-start.65 = (bf16[2304,128]{1,0:T(8,128)(2,1)S(1)}, bf16[2304,128]{1,0:T(8,128)(2,1)S(1)}, u32[]{:S(2)}, u32[]{:S(2)}) collective-permute-start(bf16[2304,128]{1,0:T(8,128)(2,1)S(1)} %collective-permute-done.64), channel_id=1, source_target_pairs={{0,64},{1,97},{2,66},{3,99},{4,68},{5,101},{6,70},{7,103},{8,72},{... | collective-permute-start | bytes 1769480 | tf_op jit(solution)/shard_map/cond/branch_1_fun/right_columns/ppermute | solution.py:37
  50.6 10.8 %collective-permute-start.56 = (bf16[2176,128]{1,0:T(8,128)(2,1)S(1)}, bf16[2176,128]{1,0:T(8,128)(2,1)S(1)}, u32[]{:S(2)}, u32[]{:S(2)}) collective-permute-start(bf16[2176,128]{1,0:T(8,128)(2,1)S(1)} %slice.50), channel_id=1, source_target_pairs={{0,8},{1,3},{2,10},{3,5},{4,12},{5,7},{6,14},{7,1},{8,16},{9,11},{... | collective-permute-start | bytes 1671176 | tf_op jit(solution)/shard_map/cond/branch_1_fun/left_rows/ppermute | solution.py:28
  50.9 10.5 %collective-permute-start.57 = (bf16[2176,128]{1,0:T(8,128)(2,1)S(1)}, bf16[2176,128]{1,0:T(8,128)(2,1)S(1)}, u32[]{:S(2)}, u32[]{:S(2)}) collective-permute-start(bf16[2176,128]{1,0:T(8,128)(2,1)S(1)} %slice.51), channel_id=1, source_target_pairs={{0,24},{1,7},{2,26},{3,1},{4,28},{5,3},{6,30},{7,5},{8,0},{9,15},{... | collective-permute-start | bytes 1671176 | tf_op jit(solution)/shard_map/cond/branch_1_fun/left_rows/ppermute | solution.py:28
  54.0 9.4 %collective-permute-start.62 = (bf16[4352,128]{1,0:T(8,128)(2,1)S(1)}, bf16[4352,128]{1,0:T(8,128)(2,1)S(1)}, u32[]{:S(2)}, u32[]{:S(2)}) collective-permute-start(bf16[4352,128]{1,0:T(8,128)(2,1)S(1)} %collective-permute-done.55.refs_4_), channel_id=1, source_target_pairs={{0,1},{1,0},{2,3},{3,2},{4,5},{5,4},{6,7},{7,6},{8,9},{9,8},{10,11... | collective-permute-start | bytes 3342344 | tf_op jit(solution)/shard_map/cond/branch_1_fun/left_rows/ppermute | solution.py:51
  54.6 9.6 %collective-permute-start.59 = (bf16[4352,128]{1,0:T(8,128)(2,1)S(1)}, bf16[4352,128]{1,0:T(8,128)(2,1)S(1)}, u32[]{:S(2)}, u32[]{:S(2)}) collective-permute-start(bf16[4352,128]{1,0:T(8,128)(2,1)S(1)} %collective-permute-done.54.refs_1_), channel_id=1, source_target_pairs={{0,1},{1,0},{2,3},{3,2},{4,5},{5,4},{6,7},{7,6},{8,9},{9,8},{10,11... | collective-permute-start | bytes 3342344 | tf_op jit(solution)/shard_map/cond/branch_1_fun/left_rows/ppermute | solution.py:51
  54.6 7.3 %collective-permute-start.66 = (bf16[2304,128]{1,0:T(8,128)(2,1)S(1)}, bf16[2304,128]{1,0:T(8,128)(2,1)S(1)}, u32[]{:S(2)}, u32[]{:S(2)}) collective-permute-start(bf16[2304,128]{1,0:T(8,128)(2,1)S(1)} %collective-permute-done.65), channel_id=1, source_target_pairs={{0,1},{1,0},{2,3},{3,2},{4,5},{5,4},{6,7},{7,6},{8,9},{9,8},{10,11... | collective-permute-start | bytes 1769480 | tf_op jit(solution)/shard_map/cond/branch_1_fun/right_columns/ppermute | solution.py:51
  61.4 2.0 %collective-permute-start.60 = (bf16[2176,128]{1,0:T(8,128)(2,1)S(1)}, bf16[2176,128]{1,0:T(8,128)(2,1)S(1)}, u32[]{:S(2)}, u32[]{:S(2)}) collective-permute-start(bf16[2176,128]{1,0:T(8,128)(2,1)S(1)} %collective-permute-done.56.refs_2_), channel_id=1, source_target_pairs={{0,1},{1,0},{2,3},{3,2},{4,5},{5,4},{6,7},{7,6},{8,9},{9,8},{10,11... | collective-permute-start | bytes 1671176 | tf_op jit(solution)/shard_map/cond/branch_1_fun/left_rows/ppermute | solution.py:51
  61.4 2.7 %collective-permute-start.61 = (bf16[2176,128]{1,0:T(8,128)(2,1)S(1)}, bf16[2176,128]{1,0:T(8,128)(2,1)S(1)}, u32[]{:S(2)}, u32[]{:S(2)}) collective-permute-start(bf16[2176,128]{1,0:T(8,128)(2,1)S(1)} %collective-permute-done.57.refs_3_), channel_id=1, source_target_pairs={{0,1},{1,0},{2,3},{3,2},{4,5},{5,4},{6,7},{7,6},{8,9},{9,8},{10,11... | collective-permute-start | bytes 1671176 | tf_op jit(solution)/shard_map/cond/branch_1_fun/left_rows/ppermute | solution.py:51
  70.3 2.0 %collective-permute-start.69 = (bf16[2048,128]{1,0:T(8,128)(2,1)S(1)}, bf16[2048,128]{1,0:T(8,128)(2,1)S(1)}, u32[]{:S(2)}, u32[]{:S(2)}) collective-permute-start(bf16[2048,128]{1,0:T(8,128)(2,1)S(1)} %get-tuple-element.116.refs_1_), channel_id=1, source_target_pairs={{0,1},{1,0},{2,3},{3,2},{4,5},{5,4},{6,7},{7,6},{8,9},{9,8},{10,11... | collective-permute-start | bytes 1572872 | tf_op jit(solution)/shard_map/cond/branch_1_fun/square/ppermute | solution.py:51
  70.4 10.5 %collective-permute-start.67 = (bf16[2048,128]{1,0:T(8,128)(2,1)S(1)}, bf16[2048,128]{1,0:T(8,128)(2,1)S(1)}, u32[]{:S(2)}, u32[]{:S(2)}) collective-permute-start(bf16[2048,128]{1,0:T(8,128)(2,1)S(1)} %get-tuple-element.116.refs_1_), channel_id=1, source_target_pairs={{0,64},{1,97},{2,66},{3,99},{4,68},{5,101},{6,70},{7,103},{8,72},{... | collective-permute-start | bytes 1572872 | tf_op jit(solution)/shard_map/cond/branch_1_fun/square/ppermute | solution.py:37
  72.3 14.2 %collective-permute-start.70 = (bf16[2048,128]{1,0:T(8,128)(2,1)S(1)}, bf16[2048,128]{1,0:T(8,128)(2,1)S(1)}, u32[]{:S(2)}, u32[]{:S(2)}) collective-permute-start(bf16[2048,128]{1,0:T(8,128)(2,1)S(1)} %collective-permute-done.69), channel_id=1, source_target_pairs={{0,64},{1,97},{2,66},{3,99},{4,68},{5,101},{6,70},{7,103},{8,72},{... | collective-permute-start | bytes 1572872 | tf_op jit(solution)/shard_map/cond/branch_1_fun/square/ppermute | solution.py:37
  80.8 11.2 %collective-permute-start.68 = (bf16[2048,128]{1,0:T(8,128)(2,1)S(1)}, bf16[2048,128]{1,0:T(8,128)(2,1)S(1)}, u32[]{:S(2)}, u32[]{:S(2)}) collective-permute-start(bf16[2048,128]{1,0:T(8,128)(2,1)S(1)} %collective-permute-done.67.refs_2_), channel_id=1, source_target_pairs={{0,64},{1,97},{2,66},{3,99},{4,68},{5,101},{6,70},{7,103},{8,72},{... | collective-permute-start | bytes 1572872 | tf_op jit(solution)/shard_map/cond/branch_1_fun/square/ppermute | solution.py:37
  86.4 5.6 %collective-permute-start.71 = (bf16[2048,128]{1,0:T(8,128)(2,1)S(1)}, bf16[2048,128]{1,0:T(8,128)(2,1)S(1)}, u32[]{:S(2)}, u32[]{:S(2)}) collective-permute-start(bf16[2048,128]{1,0:T(8,128)(2,1)S(1)} %collective-permute-done.70), channel_id=1, source_target_pairs={{0,1},{1,0},{2,3},{3,2},{4,5},{5,4},{6,7},{7,6},{8,9},{9,8},{10,11... | collective-permute-start | bytes 1572872 | tf_op jit(solution)/shard_map/cond/branch_1_fun/square/ppermute | solution.py:51
  95.3 12.1 %collective-permute-start.72 = (bf16[2048,128]{1,0:T(8,128)(2,1)S(1)}, bf16[2048,128]{1,0:T(8,128)(2,1)S(1)}, u32[]{:S(2)}, u32[]{:S(2)}) collective-permute-start(bf16[2048,128]{1,0:T(8,128)(2,1)S(1)} %next_sent.5), channel_id=1, source_target_pairs={{0,64},{64,0},{1,65},{65,1},{2,66},{66,2},{3,67},{67,3},{4,68},{68... | collective-permute-start | bytes 1572872 | tf_op jit(solution)/shard_map/cond/branch_1_fun/next/ppermute | solution.py:55
  107.5 1.0 copy-start.7

commit v4 on v3

--- a/solution.py
+++ b/solution.py
@@ -89,39 +89,31 @@
     return offsets, total
 
 
-def pack_column(pattern, values, half, part):
-    def kernel(pattern_ref, values_ref, own_ref, sent_ref):
+def pack_column(pattern, values, cap, sent):
+    def kernel(pattern_ref, values_ref, out_ref):
         layer = lax.axis_index("layer")
         first = lax.axis_index("row") * 32
         column = layer * 32 + lax.axis_index("col")
 
-        def step(a, counts):
-            n, m = counts
-            for s in range(2):
-                t = 2 * a + s
-                keep = pattern_ref[first + t, column]
-
-                @pl.when((keep != 0) & (n < half))
-                def _(n=n, t=t):
-                    own_ref[at_block(n), :] = values_ref[at_block(t), :]
-
-                @pl.when((keep != 0) & (m < part) & (layer != s))
-                def _(m=m, t=t):
-                    sent_ref[at_block(m), :] = values_ref[at_block(t), :]
-
-                n = n + keep
-                m = m + jnp.where(layer != s, keep, 0)
-            return n, m
-
-        lax.fori_loop(0, 16, step, (0, 0))
+        def step(a, n):
+            t = 2 * a + 1 - layer if sent else a
+            keep = pattern_ref[first + t, column]
+
+            @pl.when((keep != 0) & (n < cap))
+            def _():
+                out_ref[at_block(n), :] = values_ref[at_block(t), :]
+
+            return n + keep
+
+        lax.fori_loop(0, 16 if sent else 32, step, 0, unroll=4)
 
     return pl.pallas_call(
         kernel,
         grid_spec=pltpu.PrefetchScalarGridSpec(
-            num_scalar_prefetch=1, grid=(), in_specs=[VMEM], out_specs=[VMEM, VMEM]),
-        out_shape=[blocks_of(half), blocks_of(part)],
+            num_scalar_prefetch=1, grid=(), in_specs=[VMEM], out_specs=VMEM),
+        out_shape=blocks_of(cap),
         compiler_params=pltpu.CompilerParams(vmem_limit_bytes=VMEM_LIMIT),
-        name="pack_column",
+        name="pack_sent" if sent else "pack_own",
     )(pattern, values)
 
 
@@ -465,8 +457,8 @@
 
 
 def first_half(caps, values, pattern):
-    own, sent = pack_column(pattern, values, caps[0], caps[1])
-    return own, swap_layer(sent)
+    sent = pack_column(pattern, values, caps[1], True)
+    return pack_column(after(pattern, sent), values, caps[0], False), swap_layer(sent)
 
 
 def packed(caps, values, pattern, own, received, square_list, next_list, info):

time: 111 us -> 109 us (0.982)
  waiting for transfers between devices: 58.3 us -> 55.8 us
    ppermute x2, waiting for transfers between devices: 11.1 us -> 8.7 us  [swap_layer(): return lax.ppermute(value, 'layer', [(0, 1), (1, 0)])]
    pallas_call x1 -> x2, Pallas kernels: 3.06 us -> 4.18 us  [pack_column(): pl.pallas_call(kernel, grid_spec=pltpu.PrefetchScalarGridSpec(num_scalar_...]
  transfers between devices with their start and end apart: 25 -> 25, of which waited for: 13 -> 13; matrix products, arithmetic and copies ran while one was open for 1% -> 1% of each run, Pallas kernels for 8% -> 11%
where the time goes in v4:
time: 109 us; the launch traced here: 107 us
  waiting for transfers between devices  55.8 us (51%)
  starting transfers between devices  24.6 us (23%)
  Pallas kernels  23.2 us (21%)
  local copies, waits for them, and re-layouts  1.6 us (1%)
  between operations  1.33 us (1%)
    ppermute x8, waiting for transfers between devices, shift_ring(): return lax.ppermute(value, 'col', [(c, target(c)) for c in range(32)])  24.7 us
    ppermute x6, waiting for transfers between devices, carry_x(): lax.ppermute(value, ('layer', 'row', 'col'), [(i, target(i)) for i in ran...  19.3 us
    ppermute x8, starting transfers between devices, shift_ring(): return lax.ppermute(value, 'col', [(c, target(c)) for c in range(32)])  14.7 us
    ppermute x2, waiting for transfers between devices, swap_layer(): return lax.ppermute(value, 'layer', [(0, 1), (1, 0)])  8.7 us
    pallas_call x2, Pallas kernels, next_blocks(): pl.pallas_call(kernel, grid_spec=pltpu.PrefetchScalarGridSpec(num_scalar_...  7.97 us
    ppermute x6, starting transfers between devices, carry_x(): lax.ppermute(value, ('layer', 'row', 'col'), [(i, target(i)) for i in ran...  6.27 us
    pallas_call x1, Pallas kernels, square_blocks(): pl.pallas_call(kernel, grid_spec=pltpu.PrefetchScalarGridSpec(num_scalar_...  5.33 us
    pallas_call x2, Pallas kernels, pack_column(): pl.pallas_call(kernel, grid_spec=pltpu.PrefetchScalarGridSpec(num_scalar_...  4.18 us
  transfers between devices with their start and end apart: 25, of which 13 were waited for; matrix products, arithmetic and copies ran while one was open for 1% of the time, Pallas kernels for 11%

profile of v4, /device:TPU:0, one launch (start us, length us, event | category | flops | bytes accessed | tf_op | source)
XLA Modules:
  0.0 106.6 jit_solution(17748651172302003650)
XLA Ops:
  0.7 2.6 %pack_sent.3 = bf16[1408,128]{1,0:T(8,128)(2,1)S(1)} custom-call(s32[64,64]{1,0:T(8,128)} %pattern_ref.4, bf16[4096,128]{1,0:T(8,128)(2,1)} %values_ref.3), custom_call_target="tpu_custom_call" | custom-call | tf_op jit(solution)/shard_map/pack_sent/pallas_call | solution.py:110
  3.2 1.6 %collective-permute-start.73 = (bf16[1408,128]{1,0:T(8,128)(2,1)S(1)}, bf16[1408,128]{1,0:T(8,128)(2,1)S(1)}, u32[]{:S(2)}, u32[]{:S(2)}) collective-permute-start(bf16[1408,128]{1,0:T(8,128)(2,1)S(1)} %pack_sent.3), channel_id=1, source_target_pairs={{0,64},{64,0},{1,65},{65,1},{2,66},{66,2},{3,67},{67,3},{4,68},{68... | collective-permute-start | bytes 1081352 | tf_op jit(solution)/shard_map/ppermute | solution.py:55
  4.8 3.4 %tables.1 = (s32[32,128]{1,0:T(8,128)S(1)}, s32[32,128]{1,0:T(8,128)S(1)}, s32[8,128]{1,0:T(8,128)S(1)}) custom-call(s32[64,64]{1,0:T(8,128)} %pattern_ref.4, s32[64,64]{1,0:T(8,128)} %square_ref.1, s32[64,64]{1,0:T(8,128)} %next_ref.1), custom_call_target="tpu_custom_call" | custom-call | tf_op jit(solution)/shard_map/tables/pallas_call | solution.py:450
  9.3 1.6 %pack_own.3 = bf16[2304,128]{1,0:T(8,128)(2,1)S(1)} custom-call(s32[64,64]{1,0:T(8,128)} %pattern_ref.4, bf16[4096,128]{1,0:T(8,128)(2,1)S(1)} %copy-done.1), custom_call_target="tpu_custom_call" | custom-call | tf_op jit(solution)/shard_map/pack_own/pallas_call | solution.py:110
  11.0 2.2 %collective-permute-done.73 = bf16[1408,128]{1,0:T(8,128)(2,1)S(1)} collective-permute-done((bf16[1408,128]{1,0:T(8,128)(2,1)S(1)}, bf16[1408,128]{1,0:T(8,128)(2,1)S(1)}, u32[]{:S(2)}, u32[]{:S(2)}) %collective-permute-start.73) | collective-permute-done | bytes 360480 | tf_op jit(solution)/shard_map/ppermute | solution.py:55
  13.2 92.5 %conditional.2 = ((bf16[4096,128]{1,0:T(8,128)(2,1)}, bf16[4096,128]{1,0:T(8,128)(2,1)S(1)})) conditional(s32[]{:T(128)} %convert_element_type.6, (s32[]{:T(128)}, s32[64,64]{1,0:T(8,128)S(1)}, bf16[4096,128]{1,0:T(8,128)(2,1)S(1)}, s32[8,128]{1,0:T(8,128)S(1)}, s32[32,128]{1,0:T(8,128)S(1)}, /*index=5*/s32[32,128]{1,0:T(8,128)S(1)}, ...), branch_computations={%region_0.0_spmd, %region_3.0_spmd} | conditional | flops 2 | bytes 295699616 | solution.py:507
  13.2 1.4 %pack_rows.5.refs_0_ = bf16[1536,128]{1,0:T(8,128)(2,1)S(1)} custom-call(s32[64,64]{1,0:T(8,128)S(1)} %get-tuple-element.102.pattern_ref, bf16[4096,128]{1,0:T(8,128)(2,1)S(1)} %get-tuple-element.103.values_ref, bf16[1408,128]{1,0:T(8,128)(2,1)S(1)} %get-tuple-element.104.received_ref), custom_call_target="tpu_custom_call" | custom-call | tf_op jit(solution)/shard_map/cond/branch_1_fun/left_chunk/pack_rows/pallas_call | solution.py:145
  14.6 2.1 %collective-permute-start.50 = (bf16[1536,128]{1,0:T(8,128)(2,1)S(1)}, bf16[1536,128]{1,0:T(8,128)(2,1)S(1)}, u32[]{:S(2)}, u32[]{:S(2)}) collective-permute-start(bf16[1536,128]{1,0:T(8,128)(2,1)S(1)} %pack_rows.5.refs_0_), channel_id=1, source_target_pairs={{0,2},{1,9},{2,4},{3,11},{4,6},{5,13},{6,0},{7,15},{8,10},{9,17},{... | collective-permute-start | bytes 1179656 | tf_op jit(solution)/shard_map/cond/branch_1_fun/left_chunk/ppermute | solution.py:28
  16.8 1.5 %collective-permute-start.49 = (bf16[1536,128]{1,0:T(8,128)(2,1)S(1)}, bf16[1536,128]{1,0:T(8,128)(2,1)S(1)}, u32[]{:S(2)}, u32[]{:S(2)}) collective-permute-start(bf16[1536,128]{1,0:T(8,128)(2,1)S(1)} %pack_rows.5.refs_0_), channel_id=1, source_target_pairs={{0,6},{1,25},{2,0},{3,27},{4,2},{5,29},{6,4},{7,31},{8,14},{9,1},{... | collective-permute-start | bytes 1179656 | tf_op jit(solution)/shard_map/cond/branch_1_fun/left_chunk/ppermute | solution.py:28
  18.3 1.4 %collective-permute-start.53 = (bf16[2304,128]{1,0:T(8,128)(2,1)S(1)}, bf16[2304,128]{1,0:T(8,128)(2,1)S(1)}, u32[]{:S(2)}, u32[]{:S(2)}) collective-permute-start(bf16[2304,128]{1,0:T(8,128)(2,1)S(1)} %get-tuple-element.106.refs_10_), channel_id=1, source_target_pairs={{0,64},{1,97},{2,66},{3,99},{4,68},{5,101},{6,70},{7,103},{8,72},{... | collective-permute-start | bytes 1769480 | tf_op jit(solution)/shard_map/cond/branch_1_fun/right_columns/ppermute | solution.py:37
  19.7 4.3 %collective-permute-done.50.refs_4_ = bf16[1536,128]{1,0:T(8,128)(2,1)S(1)} collective-permute-done((bf16[1536,128]{1,0:T(8,128)(2,1)S(1)}, bf16[1536,128]{1,0:T(8,128)(2,1)S(1)}, u32[]{:S(2)}, u32[]{:S(2)}) %collective-permute-start.50) | collective-permute-done | bytes 393248 | tf_op jit(solution)/shard_map/cond/branch_1_fun/left_chunk/ppermute | solution.py:28
  24.7 2.7 %collective-permute-start.52 = (bf16[768,128]{1,0:T(8,128)(2,1)S(1)}, bf16[768,128]{1,0:T(8,128)(2,1)S(1)}, u32[]{:S(2)}, u32[]{:S(2)}) collective-permute-start(bf16[768,128]{1,0:T(8,128)(2,1)S(1)} %slice.49), channel_id=1, source_target_pairs={{0,6},{1,25},{2,0},{3,27},{4,2},{5,29},{6,4},{7,31},{8,14},{9,1},{... | collective-permute-start | bytes 589832 | tf_op jit(solution)/shard_map/cond/branch_1_fun/left_chunk/ppermute | solution.py:28
  27.4 3.5 %collective-permute-done.51.refs_2_ = bf16[768,128]{1,0:T(8,128)(2,1)S(1)} collective-permute-done((bf16[768,128]{1,0:T(8,128)(2,1)S(1)}, bf16[768,128]{1,0:T(8,128)(2,1)S(1)}, u32[]{:S(2)}, u32[]{:S(2)}) %collective-permute-start.51) | collective-permute-done | bytes 196640 | tf_op jit(solution)/shard_map/cond/branch_1_fun/left_chunk/ppermute | solution.py:28
  31.8 2.1 %collective-permute-start.55 = (bf16[4352,128]{1,0:T(8,128)(2,1)S(1)}, bf16[4352,128]{1,0:T(8,128)(2,1)S(1)}, u32[]{:S(2)}, u32[]{:S(2)}) collective-permute-start(bf16[4352,128]{1,0:T(8,128)(2,1)S(1)} %pack_ring.5.refs_0_), channel_id=1, source_target_pairs={{0,8},{1,3},{2,10},{3,5},{4,12},{5,7},{6,14},{7,1},{8,16},{9,11},{... | collective-permute-start | bytes 3342344 | tf_op jit(solution)/shard_map/cond/branch_1_fun/left_rows/ppermute | solution.py:28
  33.9 2.1 %collective-permute-start.54 = (bf16[4352,128]{1,0:T(8,128)(2,1)S(1)}, bf16[4352,128]{1,0:T(8,128)(2,1)S(1)}, u32[]{:S(2)}, u32[]{:S(2)}) collective-permute-start(bf16[4352,128]{1,0:T(8,128)(2,1)S(1)} %pack_ring.5.refs_0_), channel_id=1, source_target_pairs={{0,24},{1,7},{2,26},{3,1},{4,28},{5,3},{6,30},{7,5},{8,0},{9,15},{... | collective-permute-start | bytes 3342344 | tf_op jit(solution)/shard_map/cond/branch_1_fun/left_rows/ppermute | solution.py:28
  36.0 1.5 %collective-permute-start.63 = (bf16[2304,128]{1,0:T(8,128)(2,1)S(1)}, bf16[2304,128]{1,0:T(8,128)(2,1)S(1)}, u32[]{:S(2)}, u32[]{:S(2)}) collective-permute-start(bf16[2304,128]{1,0:T(8,128)(2,1)S(1)} %collective-permute-done.53.refs_11_), channel_id=1, source_target_pairs={{0,64},{1,97},{2,66},{3,99},{4,68},{5,101},{6,70},{7,103},{8,72},{... | collective-permute-start | bytes 1769480 | tf_op jit(solution)/shard_map/cond/branch_1_fun/right_columns/ppermute | solution.py:37
  37.5 1.4 %collective-permute-start.65 = (bf16[2304,128]{1,0:T(8,128)(2,1)S(1)}, bf16[2304,128]{1,0:T(8,128)(2,1)S(1)}, u32[]{:S(2)}, u32[]{:S(2)}) collective-permute-start(bf16[2304,128]{1,0:T(8,128)(2,1)S(1)} %collective-permute-done.64), channel_id=1, source_target_pairs={{0,64},{1,97},{2,66},{3,99},{4,68},{5,101},{6,70},{7,103},{8,72},{... | collective-permute-start | bytes 1769480 | tf_op jit(solution)/shard_map/cond/branch_1_fun/right_columns/ppermute | solution.py:37
  38.9 10.5 %collective-permute-done.55.refs_4_ = bf16[4352,128]{1,0:T(8,128)(2,1)S(1)} collective-permute-done((bf16[4352,128]{1,0:T(8,128)(2,1)S(1)}, bf16[4352,128]{1,0:T(8,128)(2,1)S(1)}, u32[]{:S(2)}, u32[]{:S(2)}) %collective-permute-start.55) | collective-permute-done | bytes 1114144 | tf_op jit(solution)/shard_map/cond/branch_1_fun/left_rows/ppermute | solution.py:28
  49.6 3.3 %collective-permute-start.57 = (bf16[2176,128]{1,0:T(8,128)(2,1)S(1)}, bf16[2176,128]{1,0:T(8,128)(2,1)S(1)}, u32[]{:S(2)}, u32[]{:S(2)}) collective-permute-start(bf16[2176,128]{1,0:T(8,128)(2,1)S(1)} %slice.51), channel_id=1, source_target_pairs={{0,24},{1,7},{2,26},{3,1},{4,28},{5,3},{6,30},{7,5},{8,0},{9,15},{... | collective-permute-start | bytes 1671176 | tf_op jit(solution)/shard_map/cond/branch_1_fun/left_rows/ppermute | solution.py:28
  53.9 6.3 %collective-permute-done.56.refs_2_ = bf16[2176,128]{1,0:T(8,128)(2,1)S(1)} collective-permute-done((bf16[2176,128]{1,0:T(8,128)(2,1)S(1)}, bf16[2176,128]{1,0:T(8,128)(2,1)S(1)}, u32[]{:S(2)}, u32[]{:S(2)}) %collective-permute-start.56) | collective-permute-done | bytes 557088 | tf_op jit(solution)/shard_map/cond/branch_1_fun/left_rows/ppermute | solution.py:28
  60.8 1.4 %collective-permute-done.60.refs_7_ = bf16[2176,128]{1,0:T(8,128)(2,1)S(1)} collective-permute-done((bf16[2176,128]{1,0:T(8,128)(2,1)S(1)}, bf16[2176,128]{1,0:T(8,128)(2,1)S(1)}, u32[]{:S(2)}, u32[]{:S(2)}) %collective-permute-start.60) | collective-permute-done | bytes 557088 | tf_op jit(solution)/shard_map/cond/branch_1_fun/left_rows/ppermute | solution.py:51
  63.0 5.3 %square_blocks.5 = (bf16[2048,128]{1,0:T(8,128)(2,1)S(1)}, bf16[34944,128]{1,0:T(8,128)(2,1)S(1)}) custom-call(s32[32,128]{1,0:T(8,128)S(1)} %get-tuple-element.100.list_ref, bf16[4352,128]{1,0:T(8,128)(2,1)S(1)} %pack_ring.5.refs_0_, bf16[4352,128]{1,0:T(8,128)(2,1)S(1)} %collective-permute-done.54.refs_1_, ...), custom_call_target="tpu_custom_call" | custom-call | tf_op jit(solution)/shard_map/cond/branch_1_fun/square/square_blocks/pallas_call | solution.py:230
  68.4 1.0 collective-permute-start.69
  70.0 0.9 collective-permute-done.69
  70.9 1.3 %collective-permute-start.70 = (bf16[2048,128]{1,0:T(8,128)(2,1)S(1)}, bf16[2048,128]{1,0:T(8,128)(2,1)S(1)}, u32[]{:S(2)}, u32[]{:S(2)}) collective-permute-start(bf16[2048,128]{1,0:T(8,128)(2,1)S(1)} %collective-permute-done.69), channel_id=1, source_target_pairs={{0,64},{1,97},{2,66},{3,99},{4,68},{5,101},{6,70},{7,103},{8,72},{... | collective-permute-start | bytes 1572872 | tf_op jit(solution)/shard_map/cond/branch_1_fun/square/ppermute | solution.py:37
  72.2 7.5 %collective-permute-done.67.refs_2_ = bf16[2048,128]{1,0:T(8,128)(2,1)S(1)} collective-permute-done((bf16[2048,128]{1,0:T(8,128)(2,1)S(1)}, bf16[2048,128]{1,0:T(8,128)(2,1)S(1)}, u32[]{:S(2)}, u32[]{:S(2)}) %collective-permute-start.67) | collective-permute-done | bytes 524320 | tf_op jit(solution)/shard_map/cond/branch_1_fun/square/ppermute | solution.py:37
  79.8 5.6 %collective-permute-done.70 = bf16[2048,128]{1,0:T(8,128)(2,1)S(1)} collective-permute-done((bf16[2048,128]{1,0:T(8,128)(2,1)S(1)}, bf16[2048,128]{1,0:T(8,128)(2,1)S(1)}, u32[]{:S(2)}, u32[]{:S(2)}) %collective-permute-start.70) | collective-permute-done | bytes 524320 | tf_op jit(solution)/shard_map/cond/branch_1_fun/square/ppermute | solution.py:37
  85.4 5.6 %collective-permute-done.68.refs_3_ = bf16[2048,128]{1,0:T(8,128)(2,1)S(1)} collective-permute-done((bf16[2048,128]{1,0:T(8,128)(2,1)S(1)}, bf16[2048,128]{1,0:T(8,128)(2,1)S(1)}, u32[]{:S(2)}, u32[]{:S(2)}) %collective-permute-start.68) | collective-permute-done | bytes 524320 | tf_op jit(solution)/shard_map/cond/branch_1_fun/square/ppermute | solution.py:37
  91.0 2.5 %next_sent.5 = bf16[2048,128]{1,0:T(8,128)(2,1)S(1)} custom-call(s32[32,128]{1,0:T(8,128)S(1)} %get-tuple-element.99.list_ref, bf16[34944,128]{1,0:T(8,128)(2,1)S(1)} %get-tuple-element.114.refs_0_, bf16[2048,128]{1,0:T(8,128)(2,1)S(1)} %get-tuple-element.115.refs_1_, bf16[2048,128]{1,0:T(8,128)(2,1)S(1)} %collective-permute-done.67.refs_2_, ...), custom_call_target="tpu_custom_call" | custom-call | tf_op jit(solution)/shard_map/cond/branch_1_fun/next/next_sent/pallas_call | solution.py:286
  93.6 5.5 %next_own.5 = (bf16[2048,128]{1,0:T(8,128)(2,1)S(1)}, bf16[4096,128]{1,0:T(8,128)(2,1)}) custom-call(s32[32,128]{1,0:T(8,128)S(1)} %get-tuple-element.99.list_ref, bf16[34944,128]{1,0:T(8,128)(2,1)S(1)} %get-tuple-element.114.refs_0_, bf16[2048,128]{1,0:T(8,128)(2,1)S(1)} %get-tuple-element.115.refs_1_, ...), custom_call_target="tpu_custom_call" | custom-call | tf_op jit(solution)/shard_map/cond/branch_1_fun/next/next_own/pallas_call | solution.py:286
  99.1 6.5 %collective-permute-done.72.other_ref = bf16[2048,128]{1,0:T(8,128)(2,1)S(1)} collective-permute-done((bf16[2048,128]{1,0:T(8,128)(2,1)S(1)}, bf16[2048,128]{1,0:T(8,128)(2,1)S(1)}, u32[]{:S(2)}, u32[]{:S(2)}) %collective-permute-start.72) | collective-permute-done | bytes 524320 | tf_op jit(solution)/shard_map/cond/branch_1_fun/next/ppermute | solution.py:55
  105.7 1.0 copy-done.9
  (39 shorter events, 5.4 us)
Async XLA Ops:
  0.6 12.6 %copy-start.8 = (s32[64,64]{1,0:T(8,128)S(1)}, s32[64,64]{1,0:T(8,128)}, u32[]{:S(2)}) copy-start(s32[64,64]{1,0:T(8,128)} %pattern_ref.4) | copy-start | bytes 49156
  0.6 8.7 %copy-start.1 = (bf16[4096,128]{1,0:T(8,128)(2,1)S(1)}, bf16[4096,128]{1,0:T(8,128)(2,1)}, u32[]{:S(2)}) copy-start(bf16[4096,128]{1,0:T(8,128)(2,1)} %values_ref.3) | copy-start | bytes 3145732
  3.2 10.0 %collective-permute-start.73 = (bf16[1408,128]{1,0:T(8,128)(2,1)S(1)}, bf16[1408,128]{1,0:T(8,128)(2,1)S(1)}, u32[]{:S(2)}, u32[]{:S(2)}) collective-permute-start(bf16[1408,128]{1,0:T(8,128)(2,1)S(1)} %pack_sent.3), channel_id=1, source_target_pairs={{0,64},{64,0},{1,65},{65,1},{2,66},{66,2},{3,67},{67,3},{4,68},{68... | collective-permute-start | bytes 1081352 | tf_op jit(solution)/shard_map/ppermute | solution.py:55
  14.6 9.4 %collective-permute-start.50 = (bf16[1536,128]{1,0:T(8,128)(2,1)S(1)}, bf16[1536,128]{1,0:T(8,128)(2,1)S(1)}, u32[]{:S(2)}, u32[]{:S(2)}) collective-permute-start(bf16[1536,128]{1,0:T(8,128)(2,1)S(1)} %pack_rows.5.refs_0_), channel_id=1, source_target_pairs={{0,2},{1,9},{2,4},{3,11},{4,6},{5,13},{6,0},{7,15},{8,10},{9,17},{... | collective-permute-start | bytes 1179656 | tf_op jit(solution)/shard_map/cond/branch_1_fun/left_chunk/ppermute | solution.py:28
  16.8 7.9 %collective-permute-start.49 = (bf16[1536,128]{1,0:T(8,128)(2,1)S(1)}, bf16[1536,128]{1,0:T(8,128)(2,1)S(1)}, u32[]{:S(2)}, u32[]{:S(2)}) collective-permute-start(bf16[1536,128]{1,0:T(8,128)(2,1)S(1)} %pack_rows.5.refs_0_), channel_id=1, source_target_pairs={{0,6},{1,25},{2,0},{3,27},{4,2},{5,29},{6,4},{7,31},{8,14},{9,1},{... | collective-permute-start | bytes 1179656 | tf_op jit(solution)/shard_map/cond/branch_1_fun/left_chunk/ppermute | solution.py:28
  18.3 12.6 %collective-permute-start.53 = (bf16[2304,128]{1,0:T(8,128)(2,1)S(1)}, bf16[2304,128]{1,0:T(8,128)(2,1)S(1)}, u32[]{:S(2)}, u32[]{:S(2)}) collective-permute-start(bf16[2304,128]{1,0:T(8,128)(2,1)S(1)} %get-tuple-element.106.refs_10_), channel_id=1, source_target_pairs={{0,64},{1,97},{2,66},{3,99},{4,68},{5,101},{6,70},{7,103},{8,72},{... | collective-permute-start | bytes 1769480 | tf_op jit(solution)/shard_map/cond/branch_1_fun/right_columns/ppermute | solution.py:37
  24.0 6.9 %collective-permute-start.51 = (bf16[768,128]{1,0:T(8,128)(2,1)S(1)}, bf16[768,128]{1,0:T(8,128)(2,1)S(1)}, u32[]{:S(2)}, u32[]{:S(2)}) collective-permute-start(bf16[768,128]{1,0:T(8,128)(2,1)S(1)} %slice.48), channel_id=1, source_target_pairs={{0,2},{1,9},{2,4},{3,11},{4,6},{5,13},{6,0},{7,15},{8,10},{9,17},{... | collective-permute-start | bytes 589832 | tf_op jit(solution)/shard_map/cond/branch_1_fun/left_chunk/ppermute | solution.py:28
  24.7 6.3 %collective-permute-start.52 = (bf16[768,128]{1,0:T(8,128)(2,1)S(1)}, bf16[768,128]{1,0:T(8,128)(2,1)S(1)}, u32[]{:S(2)}, u32[]{:S(2)}) collective-permute-start(bf16[768,128]{1,0:T(8,128)(2,1)S(1)} %slice.49), channel_id=1, source_target_pairs={{0,6},{1,25},{2,0},{3,27},{4,2},{5,29},{6,4},{7,31},{8,14},{9,1},{... | collective-permute-start | bytes 589832 | tf_op jit(solution)/shard_map/cond/branch_1_fun/left_chunk/ppermute | solution.py:28
  27.4 10.1 %collective-permute-start.64 = (bf16[2304,128]{1,0:T(8,128)(2,1)S(1)}, bf16[2304,128]{1,0:T(8,128)(2,1)S(1)}, u32[]{:S(2)}, u32[]{:S(2)}) collective-permute-start(bf16[2304,128]{1,0:T(8,128)(2,1)S(1)} %get-tuple-element.106.refs_10_), channel_id=1, source_target_pairs={{0,1},{1,0},{2,3},{3,2},{4,5},{5,4},{6,7},{7,6},{8,9},{9,8},{10,11... | collective-permute-start | bytes 1769480 | tf_op jit(solution)/shard_map/cond/branch_1_fun/right_columns/ppermute | solution.py:51
  31.8 17.6 %collective-permute-start.55 = (bf16[4352,128]{1,0:T(8,128)(2,1)S(1)}, bf16[4352,128]{1,0:T(8,128)(2,1)S(1)}, u32[]{:S(2)}, u32[]{:S(2)}) collective-permute-start(bf16[4352,128]{1,0:T(8,128)(2,1)S(1)} %pack_ring.5.refs_0_), channel_id=1, source_target_pairs={{0,8},{1,3},{2,10},{3,5},{4,12},{5,7},{6,14},{7,1},{8,16},{9,11},{... | collective-permute-start | bytes 3342344 | tf_op jit(solution)/shard_map/cond/branch_1_fun/left_rows/ppermute | solution.py:28
  33.9 15.6 %collective-permute-start.54 = (bf16[4352,128]{1,0:T(8,128)(2,1)S(1)}, bf16[4352,128]{1,0:T(8,128)(2,1)S(1)}, u32[]{:S(2)}, u32[]{:S(2)}) collective-permute-start(bf16[4352,128]{1,0:T(8,128)(2,1)S(1)} %pack_ring.5.refs_0_), channel_id=1, source_target_pairs={{0,24},{1,7},{2,26},{3,1},{4,28},{5,3},{6,30},{7,5},{8,0},{9,15},{... | collective-permute-start | bytes 3342344 | tf_op jit(solution)/shard_map/cond/branch_1_fun/left_rows/ppermute | solution.py:28
  36.0 17.4 %collective-permute-start.58 = (bf16[4352,128]{1,0:T(8,128)(2,1)S(1)}, bf16[4352,128]{1,0:T(8,128)(2,1)S(1)}, u32[]{:S(2)}, u32[]{:S(2)}) collective-permute-start(bf16[4352,128]{1,0:T(8,128)(2,1)S(1)} %pack_ring.5.refs_0_), channel_id=1, source_target_pairs={{0,1},{1,0},{2,3},{3,2},{4,5},{5,4},{6,7},{7,6},{8,9},{9,8},{10,11... | collective-permute-start | bytes 3342344 | tf_op jit(solution)/shard_map/cond/branch_1_fun/left_rows/ppermute | solution.py:51
  36.0 16.9 %collective-permute-start.63 = (bf16[2304,128]{1,0:T(8,128)(2,1)S(1)}, bf16[2304,128]{1,0:T(8,128)(2,1)S(1)}, u32[]{:S(2)}, u32[]{:S(2)}) collective-permute-start(bf16[2304,128]{1,0:T(8,128)(2,1)S(1)} %collective-permute-done.53.refs_11_), channel_id=1, source_target_pairs={{0,64},{1,97},{2,66},{3,99},{4,68},{5,101},{6,70},{7,103},{8,72},{... | collective-permute-start | bytes 1769480 | tf_op jit(solution)/shard_map/cond/branch_1_fun/right_columns/ppermute | solution.py:37
  37.5 15.9 %collective-permute-start.65 = (bf16[2304,128]{1,0:T(8,128)(2,1)S(1)}, bf16[2304,128]{1,0:T(8,128)(2,1)S(1)}, u32[]{:S(2)}, u32[]{:S(2)}) collective-permute-start(bf16[2304,128]{1,0:T(8,128)(2,1)S(1)} %collective-permute-done.64), channel_id=1, source_target_pairs={{0,64},{1,97},{2,66},{3,99},{4,68},{5,101},{6,70},{7,103},{8,72},{... | collective-permute-start | bytes 1769480 | tf_op jit(solution)/shard_map/cond/branch_1_fun/right_columns/ppermute | solution.py:37
  49.5 10.8 %collective-permute-start.56 = (bf16[2176,128]{1,0:T(8,128)(2,1)S(1)}, bf16[2176,128]{1,0:T(8,128)(2,1)S(1)}, u32[]{:S(2)}, u32[]{:S(2)}) collective-permute-start(bf16[2176,128]{1,0:T(8,128)(2,1)S(1)} %slice.50), channel_id=1, source_target_pairs={{0,8},{1,3},{2,10},{3,5},{4,12},{5,7},{6,14},{7,1},{8,16},{9,11},{... | collective-permute-start | bytes 1671176 | tf_op jit(solution)/shard_map/cond/branch_1_fun/left_rows/ppermute | solution.py:28
  49.6 10.7 %collective-permute-start.57 = (bf16[2176,128]{1,0:T(8,128)(2,1)S(1)}, bf16[2176,128]{1,0:T(8,128)(2,1)S(1)}, u32[]{:S(2)}, u32[]{:S(2)}) collective-permute-start(bf16[2176,128]{1,0:T(8,128)(2,1)S(1)} %slice.51), channel_id=1, source_target_pairs={{0,24},{1,7},{2,26},{3,1},{4,28},{5,3},{6,30},{7,5},{8,0},{9,15},{... | collective-permute-start | bytes 1671176 | tf_op jit(solution)/shard_map/cond/branch_1_fun/left_rows/ppermute | solution.py:28
  52.9 9.4 %collective-permute-start.62 = (bf16[4352,128]{1,0:T(8,128)(2,1)S(1)}, bf16[4352,128]{1,0:T(8,128)(2,1)S(1)}, u32[]{:S(2)}, u32[]{:S(2)}) collective-permute-start(bf16[4352,128]{1,0:T(8,128)(2,1)S(1)} %collective-permute-done.55.refs_4_), channel_id=1, source_target_pairs={{0,1},{1,0},{2,3},{3,2},{4,5},{5,4},{6,7},{7,6},{8,9},{9,8},{10,11... | collective-permute-start | bytes 3342344 | tf_op jit(solution)/shard_map/cond/branch_1_fun/left_rows/ppermute | solution.py:51
  53.4 9.6 %collective-permute-start.59 = (bf16[4352,128]{1,0:T(8,128)(2,1)S(1)}, bf16[4352,128]{1,0:T(8,128)(2,1)S(1)}, u32[]{:S(2)}, u32[]{:S(2)}) collective-permute-start(bf16[4352,128]{1,0:T(8,128)(2,1)S(1)} %collective-permute-done.54.refs_1_), channel_id=1, source_target_pairs={{0,1},{1,0},{2,3},{3,2},{4,5},{5,4},{6,7},{7,6},{8,9},{9,8},{10,11... | collective-permute-start | bytes 3342344 | tf_op jit(solution)/shard_map/cond/branch_1_fun/left_rows/ppermute | solution.py:51
  53.4 7.3 %collective-permute-start.66 = (bf16[2304,128]{1,0:T(8,128)(2,1)S(1)}, bf16[2304,128]{1,0:T(8,128)(2,1)S(1)}, u32[]{:S(2)}, u32[]{:S(2)}) collective-permute-start(bf16[2304,128]{1,0:T(8,128)(2,1)S(1)} %collective-permute-done.65), channel_id=1, source_target_pairs={{0,1},{1,0},{2,3},{3,2},{4,5},{5,4},{6,7},{7,6},{8,9},{9,8},{10,11... | collective-permute-start | bytes 1769480 | tf_op jit(solution)/shard_map/cond/branch_1_fun/right_columns/ppermute | solution.py:51
  60.3 2.0 %collective-permute-start.60 = (bf16[2176,128]{1,0:T(8,128)(2,1)S(1)}, bf16[2176,128]{1,0:T(8,128)(2,1)S(1)}, u32[]{:S(2)}, u32[]{:S(2)}) collective-permute-start(bf16[2176,128]{1,0:T(8,128)(2,1)S(1)} %collective-permute-done.56.refs_2_), channel_id=1, source_target_pairs={{0,1},{1,0},{2,3},{3,2},{4,5},{5,4},{6,7},{7,6},{8,9},{9,8},{10,11... | collective-permute-start | bytes 1671176 | tf_op jit(solution)/shard_map/cond/branch_1_fun/left_rows/ppermute | solution.py:51
  60.3 2.7 %collective-permute-start.61 = (bf16[2176,128]{1,0:T(8,128)(2,1)S(1)}, bf16[2176,128]{1,0:T(8,128)(2,1)S(1)}, u32[]{:S(2)}, u32[]{:S(2)}) collective-permute-start(bf16[2176,128]{1,0:T(8,128)(2,1)S(1)} %collective-permute-done.57.refs_3_), channel_id=1, source_target_pairs={{0,1},{1,0},{2,3},{3,2},{4,5},{5,4},{6,7},{7,6},{8,9},{9,8},{10,11... | collective-permute-start | bytes 1671176 | tf_op jit(solution)/shard_map/cond/branch_1_fun/left_rows/ppermute | solution.py:51
  68.4 2.5 %collective-permute-start.69 = (bf16[2048,128]{1,0:T(8,128)(2,1)S(1)}, bf16[2048,128]{1,0:T(8,128)(2,1)S(1)}, u32[]{:S(2)}, u32[]{:S(2)}) collective-permute-start(bf16[2048,128]{1,0:T(8,128)(2,1)S(1)} %get-tuple-element.115.refs_1_), channel_id=1, source_target_pairs={{0,1},{1,0},{2,3},{3,2},{4,5},{5,4},{6,7},{7,6},{8,9},{9,8},{10,11... | collective-permute-start | bytes 1572872 | tf_op jit(solution)/shard_map/cond/branch_1_fun/square/ppermute | solution.py:51
  69.4 10.4 %collective-permute-start.67 = (bf16[2048,128]{1,0:T(8,128)(2,1)S(1)}, bf16[2048,128]{1,0:T(8,128)(2,1)S(1)}, u32[]{:S(2)}, u32[]{:S(2)}) collective-permute-start(bf16[2048,128]{1,0:T(8,128)(2,1)S(1)} %get-tuple-element.115.refs_1_), channel_id=1, source_target_pairs={{0,64},{1,97},{2,66},{3,99},{4,68},{5,101},{6,70},{7,103},{8,72},{... | collective-permute-start | bytes 1572872 | tf_op jit(solution)/shard_map/cond/branch_1_fun/square/ppermute | solution.py:37
  70.9 14.5 %collective-permute-start.70 = (bf16[2048,128]{1,0:T(8,128)(2,1)S(1)}, bf16[2048,128]{1,0:T(8,128)(2,1)S(1)}, u32[]{:S(2)}, u32[]{:S(2)}) collective-permute-start(bf16[2048,128]{1,0:T(8,128)(2,1)S(1)} %collective-permute-done.69), channel_id=1, source_target_pairs={{0,64},{1,97},{2,66},{3,99},{4,68},{5,101},{6,70},{7,103},{8,72},{... | collective-permute-start | bytes 1572872 | tf_op jit(solution)/shard_map/cond/branch_1_fun/square/ppermute | solution.py:37
  79.8 11.2 %collective-permute-start.68 = (bf16[2048,128]{1,0:T(8,128)(2,1)S(1)}, bf16[2048,128]{1,0:T(8,128)(2,1)S(1)}, u32[]{:S(2)}, u32[]{:S(2)}) collective-permute-start(bf16[2048,128]{1,0:T(8,128)(2,1)S(1)} %collective-permute-done.67.refs_2_), channel_id=1, source_target_pairs={{0,64},{1,97},{2,66},{3,99},{4,68},{5,101},{6,70},{7,103},{8,72},{... | collective-permute-start | bytes 1572872 | tf_op jit(solution)/shard_map/cond/branch_1_fun/square/ppermute | solution.py:37
  85.4 5.6 %collective-permute-start.71 = (bf16[2048,128]{1,0:T(8,128)(2,1)S(1)}, bf16[2048,128]{1,0:T(8,128)(2,1)S(1)}, u32[]{:S(2)}, u32[]{:S(2)}) collective-permute-start(bf16[2048,128]{1,0:T(8,128)(2,1)S(1)} %collective-permute-done.70), channel_id=1, source_target_pairs={{0,1},{1,0},{2,3},{3,2},{4,5},{5,4},{6,7},{7,6},{8,9},{9,8},{10,11... | collective-permute-start | bytes 1572872 | tf_op jit(solution)/shard_map/cond/branch_1_fun/square/ppermute | solution.py:51
  93.5 12.1 %collective-permute-start.72 = (bf16[2048,128]{1,0:T(8,128)(2,1)S(1)}, bf16[2048,128]{1,0:T(8,128)(2,1)S(1)}, u32[]{:S(2)}, u32[]{:S(2)}) collective-permute-start(bf16[2048,128]{1,0:T(8,128)(2,1)S(1)} %next_sent.5), channel_id=1, source_target_pairs={{0,64},{64,0},{1,65},{65,1},{2,66},{66,2},{3,67},{67,3},{4,68},{68... | collective-permute-start | bytes 1572872 | tf_op jit(solution)/shard_map/cond/branch_1_fun/next/ppermute | solution.py:55
  105.7 1.0 copy-start.9
